TPU v7x, 128 devices: a whole 4x4x4 slice. The times are simulated.
128 devices in a mesh: leaf: 128 (over z, y, x, core).
Axes of the slice: x: 4, y: 4, z: 4, core: 2. Of those that a mesh axis runs over, the one named last changes fastest.
Arguments:
- rhs: bfloat16 [8192, 64, 256], P('leaf'), may hold values from -6 to 6
- points: bfloat16 [8192, 3, 256], P('leaf'), may hold values from 0 to 0.099609375
- upward_leaf_bases: bfloat16 [8192, 64, 256], P('leaf'), may hold values from -0.375 to 0.375
- downward_leaf_bases: bfloat16 [8192, 64, 256], P('leaf'), may hold values from -0.5 to 0.5
- up_leaf: bfloat16 [8192, 64, 64], P('leaf'), may hold values from -0.25 to 0.25
- leaf_down_transfer: bfloat16 [8192, 64, 64], P('leaf'), may hold values from -0.5 to 0.5
- couple_leaf: bfloat16 [8192, 8, 64, 64], P('leaf'), may hold values from -0.25 to 0.25
- list_leaf: int32 [8192, 8], P('leaf'), may hold values from 0 to 8191, as said below
- count_leaf: int32 [8192], P('leaf'), may hold values from 1 to 8
- up_node: bfloat16 [1024, 64, 64], P('leaf'), may hold values from -0.25 to 0.25
- down_node: bfloat16 [1024, 64, 64], P('leaf'), may hold values from -0.5 to 0.5
- couple_node: bfloat16 [1024, 4, 64, 64], P('leaf'), may hold values from -0.375 to 0.375
- list_node: int32 [1024, 4], P('leaf'), may hold values from 0 to 1023, as said below
- count_node: int32 [1024], P('leaf'), may hold values from 1 to 4
- up_top: float32 [128, 5, 64, 64], P('leaf'), as said below
- down_top: float32 [128, 5, 64, 64], P('leaf'), as said below
- couple_top: float32 [128, 6, 4, 64, 64], P('leaf'), as said below
Outputs:
- applied: bfloat16 [8192, 64, 256], P('leaf')
Inputs may be any that keep to these rules, and one draw needn't show every extreme that they name: For k < count_leaf[s], list_leaf[s, k] is a leaf 2 to 8 leaves away from s; for k >= count_leaf[s] it is s. For k < count_node[a], list_node[a, k] is a level-1 node 2 to 4 nodes away from a; for k >= count_node[a] it is a. up_top[d, h] is equal for all d with the same d // 2^h. down_top[d, h] is equal for all d with the same d // 2^h. couple_top[d, h] is equal for all d with the same d // 2^h.
All inputs are finite; a program needn't handle non-finite values.
Results may differ from a plain program's by a relative error of at most 0.0065.
Values may be sent and summed in bfloat16 or wider, within the bound.
No kernel may reach another device: no remote copies, remote signals or barrier semaphores. Data moves between devices by JAX's collectives and lax.ppermute only.
A program may use at most 192 MiB of HBM per device.

v0:
```python
import jax
import jax.numpy as jnp
from jax import lax
from jax.sharding import PartitionSpec as P

W0 = 8
W1 = 4


core_square = 0.0004
highest_precision = lax.Precision.HIGHEST
partner_offsets = (-3, -2, 2, 3)


def padded_2(cells, sides, width):
    for axis, dim in sides:
        count = lax.axis_size(axis)
        ends = count - 1
        head = lax.slice_in_dim(cells, 0, width, axis=dim)
        tail = lax.slice_in_dim(cells, cells.shape[dim] - width, cells.shape[dim], axis=dim)
        cells = jnp.concatenate(
            [
                lax.ppermute(tail, axis, [(i, (i + 1) % count) for i in range(ends)]),
                cells,
                lax.ppermute(head, axis, [((i + 1) % count, i) for i in range(ends)]),
            ],
            axis=dim,
        )
    return cells


def shifted(block, axis, distance):
    devices = range(lax.axis_size(axis))
    route = [(i - distance, i) for i in devices if i - distance in devices]
    return lax.ppermute(block, axis, route)


def kernel_block(source, target):
    summed = jnp.zeros((source.shape[0], source.shape[2], target.shape[2]), jnp.float32)
    for coordinate in range(3):
        spacing = source[:, coordinate, :, None] - target[:, coordinate, None, :]
        summed = summed + spacing * spacing
    return (1.0 / source.shape[2] * lax.rsqrt(summed + core_square)).astype(jnp.bfloat16)


def couple_rows(padded, lists, counts, blocks, first_row):
    local_index = lists - first_row
    picked = jnp.take(padded, local_index, axis=0)
    live_mask = (jnp.arange(lists.shape[1])[None, :] < counts[:, None]).astype(jnp.bfloat16)
    picked = picked * live_mask[:, :, None, None]
    return jnp.einsum("nksr,nkrq->nsq", picked, blocks, preferred_element_type=jnp.float32)


def partner_valid(node_index, offset, node_count):
    valid = (node_index + offset >= 0) & (node_index + offset < node_count)
    if offset == -3:
        valid = valid & (node_index % 2 == 1)
    if offset == 3:
        valid = valid & (node_index % 2 == 0)
    return valid


def shards(
    rhs,
    points,
    upward_leaf_bases,
    downward_leaf_bases,
    up_leaf,
    leaf_down_transfer,
    couple_leaf,
    list_leaf,
    count_leaf,
    up_node,
    down_node,
    couple_node,
    list_node,
    count_node,
    up_top,
    down_top,
    couple_top,
):
    leaves, columns, point_count = rhs.shape
    rank_size = upward_leaf_bases.shape[1]
    groups = up_node.shape[0]
    per_group = leaves // groups
    device = lax.axis_index("leaf")
    devices = lax.axis_size("leaf")
    top_bits = devices.bit_length() - 1
    joined = jnp.concatenate([rhs, points], axis=1)
    padded = padded_2(joined, (("leaf", 0),), 1)
    target = points.astype(jnp.float32)
    nearby_sum_total = jnp.zeros((leaves, columns, point_count), jnp.float32)
    for offset in range(3):
        window = padded[offset : offset + leaves]
        kernel = kernel_block(window[:, columns:].astype(jnp.float32), target)
        nearby_sum_total = nearby_sum_total + jnp.einsum(
            "lsp,lpq->lsq", window[:, :columns], kernel, preferred_element_type=jnp.float32
        )
    leaf_coefficient = jnp.einsum(
        "qjg,qfg->qjf", rhs, upward_leaf_bases, preferred_element_type=jnp.float32
    ).astype(jnp.bfloat16)
    grouped = leaf_coefficient.reshape(groups, per_group, columns, rank_size)
    node_coeff = jnp.einsum(
        "absr,abrq->asq",
        grouped,
        up_leaf.reshape(groups, per_group, rank_size, rank_size),
        preferred_element_type=jnp.float32,
    ).astype(jnp.bfloat16)
    leaf_rim = padded_2(leaf_coefficient, (("leaf", 0),), W0)
    node_rim = padded_2(node_coeff, (("leaf", 0),), W1)
    leaf_gain_factor = couple_rows(
        leaf_rim, list_leaf, count_leaf, couple_leaf, device * leaves - W0
    )
    node_gain = couple_rows(node_rim, list_node, count_node, couple_node, device * groups - W1)
    level_value = jnp.einsum("asr,arq->sq", node_coeff, up_node, preferred_element_type=jnp.float32)
    couple_sums = []
    for height in range(top_bits - 1):
        if height > 0:
            carry_up = jnp.dot(level_value, up_top[0, height - 1], precision=highest_precision)
            level_value = carry_up + shifted(carry_up, "leaf", -(1 << height - 1))
        node_index = device >> height
        node_count = devices >> height
        summed = jnp.zeros_like(level_value)
        for slot_index, offset in enumerate(partner_offsets):
            partner = shifted(level_value, "leaf", -(offset << height))
            valid = partner_valid(node_index, offset, node_count)
            product = jnp.dot(
                partner, couple_top[0, height, slot_index], precision=highest_precision
            )
            summed = summed + jnp.where(valid, product, 0.0)
        couple_sums.append(summed)
    down_value = couple_sums[top_bits - 2]
    for height in range(top_bits - 2, 0, -1):
        arrived = shifted(down_value, "leaf", 1 << height - 1)
        down_value = jnp.where((device >> height - 1) % 2 == 1, arrived, down_value)
        down_value = couple_sums[height - 1] + jnp.dot(
            down_value, down_top[0, height - 1], precision=highest_precision
        )
    down_round = down_value.astype(jnp.bfloat16)
    node_output_value = (
        node_gain
        + jnp.einsum("sr,arq->asq", down_round, down_node, preferred_element_type=jnp.float32)
    ).astype(jnp.bfloat16)
    leaf_term = jnp.einsum(
        "asr,abrq->absq",
        node_output_value,
        leaf_down_transfer.reshape(groups, per_group, rank_size, rank_size),
        preferred_element_type=jnp.float32,
    )
    leaf_output_value = (leaf_gain_factor + leaf_term.reshape(leaves, columns, rank_size)).astype(
        jnp.bfloat16
    )
    product_output = nearby_sum_total + jnp.einsum(
        "gjo,gob->gjb", leaf_output_value, downward_leaf_bases, preferred_element_type=jnp.float32
    )
    return product_output.astype(jnp.bfloat16)


def solution(mesh):
    placed = (
        P("leaf", None, None),
        P("leaf", None, None),
        P("leaf", None, None),
        P("leaf", None, None),
        P("leaf", None, None),
        P("leaf", None, None),
        P("leaf", None, None, None),
        P("leaf", None),
        P("leaf"),
        P("leaf", None, None),
        P("leaf", None, None),
        P("leaf", None, None, None),
        P("leaf", None),
        P("leaf"),
        P("leaf", None, None, None),
        P("leaf", None, None, None),
        P("leaf", None, None, None, None),
    )
    return jax.shard_map(
        shards, mesh=mesh, in_specs=placed, out_specs=P("leaf", None, None), check_vma=False
    )
```

profile of v0, /device:TPU:95, one launch (start us, length us, event | category | flops | bytes accessed | tf_op | source)
XLA Modules:
  0.0 320.8 jit_solution(6485923564915263696)
XLA Ops:
  12.0 7.3 %collective-permute-start.7 = (f32[64,64]{1,0:T(8,128)}, f32[64,64]{1,0:T(8,128)S(1)}, u32[]{:S(2)}, u32[]{:S(2)}) collective-permute-start(f32[64,64]{1,0:T(8,128)} %convolution_bitcast_fusion.3), channel_id=1, source_target_pairs={{0,2},{1,3},{2,4},{3,5},{4,6},{5,7},{6,8},{7,9},{8,10},{9,11},{10,... | collective-permute-start | bytes 49160 | tf_op jit(solution)/shard_map/ppermute | solution.py:35
  19.4 3.4 %collective-permute-start.6 = (f32[64,64]{1,0:T(8,128)}, f32[64,64]{1,0:T(8,128)}, u32[]{:S(2)}, u32[]{:S(2)}) collective-permute-start(f32[64,64]{1,0:T(8,128)} %convolution_bitcast_fusion.3), channel_id=1, source_target_pairs={{0,3},{1,4},{2,5},{3,6},{4,7},{5,8},{6,9},{7,10},{8,11},{9,12},{10... | collective-permute-start | bytes 49160 | tf_op jit(solution)/shard_map/ppermute | solution.py:35
  31.9 10.5 %fusion.1 = f32[64,256,64]{1,2,0:T(8,128)} fusion(bf16[64,64,256]{2,1,0:T(8,128)(2,1)} %param.17, f32[64,256]{1,0:T(8,128)S(1)} %get-tuple-element.23, f32[64,256]{1,0:T(8,128)S(1)} %get-tuple-element.24, f32[64,256]{1,0:T(8,128)S(1)} %get-tuple-element.22), kind=kOutput, calls=%fused_computation.6 | convolution fusion | flops 583008256 | bytes 6488064 | tf_op jit(solution)/shard_map/lsp,lpq->lsq/dot_general | solution.py:96
  43.6 7.9 %collective-permute-start.4 = (bf16[4,64,64]{2,1,0:T(8,128)(2,1)S(1)}, bf16[4,64,64]{2,1,0:T(8,128)(2,1)S(1)}, u32[]{:S(2)}, u32[]{:S(2)}) collective-permute-start(bf16[4,64,64]{2,1,0:T(8,128)(2,1)S(1)} %get-tuple-element.25), channel_id=1, source_target_pairs={{0,1},{1,2},{2,3},{3,4},{4,5},{5,6},{6,7},{7,8},{8,9},{9,10},{10,1... | collective-permute-start | bytes 98312 | tf_op jit(solution)/shard_map/ppermute | solution.py:23
  55.1 7.8 %collective-permute-start.2 = (bf16[8,64,64]{2,1,0:T(8,128)(2,1)}, bf16[8,64,64]{2,1,0:T(8,128)(2,1)S(1)}, u32[]{:S(2)}, u32[]{:S(2)}) collective-permute-start(bf16[8,64,64]{2,1,0:T(8,128)(2,1)} %get-tuple-element.20), channel_id=1, source_target_pairs={{0,1},{1,2},{2,3},{3,4},{4,5},{5,6},{6,7},{7,8},{8,9},{9,10},{10,1... | collective-permute-start | bytes 196616 | tf_op jit(solution)/shard_map/ppermute | solution.py:23
  66.5 6.2 %collective-permute-done.15 = f32[64,64]{1,0:T(8,128)S(1)} collective-permute-done((f32[64,64]{1,0:T(8,128)S(1)}, f32[64,64]{1,0:T(8,128)S(1)}, u32[]{:S(2)}, u32[]{:S(2)}) %collective-permute-start.15) | collective-permute-done | bytes 16416 | tf_op jit(solution)/shard_map/ppermute | solution.py:35
  76.7 3.6 %collective-permute-done.14 = f32[64,64]{1,0:T(8,128)S(1)} collective-permute-done((f32[64,64]{1,0:T(8,128)S(1)}, f32[64,64]{1,0:T(8,128)S(1)}, u32[]{:S(2)}, u32[]{:S(2)}) %collective-permute-start.14) | collective-permute-done | bytes 16416 | tf_op jit(solution)/shard_map/ppermute | solution.py:35
  83.0 6.5 %collective-permute-done.13 = f32[64,64]{1,0:T(8,128)S(1)} collective-permute-done((f32[64,64]{1,0:T(8,128)S(1)}, f32[64,64]{1,0:T(8,128)S(1)}, u32[]{:S(2)}, u32[]{:S(2)}) %collective-permute-start.13) | collective-permute-done | bytes 16416 | tf_op jit(solution)/shard_map/ppermute | solution.py:35
  92.1 7.9 %collective-permute-start = (bf16[1,67,256]{2,1,0:T(8,128)(2,1)}, bf16[1,67,256]{2,1,0:T(8,128)(2,1)}, u32[]{:S(2)}, u32[]{:S(2)}) collective-permute-start(bf16[1,67,256]{2,1,0:T(8,128)(2,1)} %get-tuple-element.19), channel_id=1, source_target_pairs={{0,1},{1,2},{2,3},{3,4},{4,5},{5,6},{6,7},{7,8},{8,9},{9,10},{10,1... | collective-permute-start | bytes 102920 | tf_op jit(solution)/shard_map/ppermute | solution.py:23
  112.4 3.7 %collective-permute-done.1 = bf16[1,67,256]{2,1,0:T(8,128)(2,1)S(1)} collective-permute-done((bf16[1,67,256]{2,1,0:T(8,128)(2,1)}, bf16[1,67,256]{2,1,0:T(8,128)(2,1)S(1)}, u32[]{:S(2)}, u32[]{:S(2)}) %collective-permute-start.1) | collective-permute-done | bytes 34336 | tf_op jit(solution)/shard_map/ppermute | solution.py:25
  120.9 10.7 %fusion = f32[64,64,256]{2,1,0:T(8,128)} fusion(f32[64,256]{1,0:T(8,128)} %copy-done.15, f32[64,256]{1,0:T(8,128)S(1)} %get-tuple-element.30, f32[64,256]{1,0:T(8,128)} %copy-done.17, f32[64,256]{1,0:T(8,128)S(1)} %get-tuple-element.31, f32[64,256]{1,0:T(8,128)} %copy-done.13, f32[64,256]{1,0:T(8,128)S(1)} %get-tuple-element.32, ...), kind=kOutput, calls=%fused_computation.5 | convolution fusion | flops 584056832 | bytes 6817280 | tf_op jit(solution)/shard_map/lsp,lpq->lsq/dot_general | solution.py:96
  135.2 4.1 %collective-permute-start.24 = (f32[64,64]{1,0:T(8,128)S(1)}, f32[64,64]{1,0:T(8,128)S(1)}, u32[]{:S(2)}, u32[]{:S(2)}) collective-permute-start(f32[64,64]{1,0:T(8,128)S(1)} %add.313), channel_id=1, source_target_pairs={{24,0},{25,1},{26,2},{27,3},{28,4},{29,5},{30,6},{31,7},{32,8},{33... | collective-permute-start | bytes 49160 | tf_op jit(solution)/shard_map/ppermute | solution.py:35
  141.6 4.7 %collective-permute-done.25 = f32[64,64]{1,0:T(8,128)S(1)} collective-permute-done((f32[64,64]{1,0:T(8,128)S(1)}, f32[64,64]{1,0:T(8,128)S(1)}, u32[]{:S(2)}, u32[]{:S(2)}) %collective-permute-start.25) | collective-permute-done | bytes 16416 | tf_op jit(solution)/shard_map/ppermute | solution.py:35
  149.1 4.4 %collective-permute-start.29 = (f32[64,64]{1,0:T(8,128)S(1)}, f32[64,64]{1,0:T(8,128)S(1)}, u32[]{:S(2)}, u32[]{:S(2)}) collective-permute-start(f32[64,64]{1,0:T(8,128)S(1)} %add.322), channel_id=1, source_target_pairs={{48,0},{49,1},{50,2},{51,3},{52,4},{53,5},{54,6},{55,7},{56,8},{57... | collective-permute-start | bytes 49160 | tf_op jit(solution)/shard_map/ppermute | solution.py:35
  155.8 5.3 %collective-permute-start.30 = (f32[64,64]{1,0:T(8,128)S(1)}, f32[64,64]{1,0:T(8,128)S(1)}, u32[]{:S(2)}, u32[]{:S(2)}) collective-permute-start(f32[64,64]{1,0:T(8,128)S(1)} %fusion.96), channel_id=1, source_target_pairs={{16,0},{17,1},{18,2},{19,3},{20,4},{21,5},{22,6},{23,7},{24,8},{25... | collective-permute-start | bytes 49160 | tf_op jit(solution)/shard_map/ppermute | solution.py:35
  165.7 9.0 %collective-permute-start.33 = (f32[64,64]{1,0:T(8,128)S(1)}, f32[64,64]{1,0:T(8,128)S(1)}, u32[]{:S(2)}, u32[]{:S(2)}) collective-permute-start(f32[64,64]{1,0:T(8,128)S(1)} %add.331), channel_id=1, source_target_pairs={{64,0},{65,1},{66,2},{67,3},{68,4},{69,5},{70,6},{71,7},{72,8},{73... | collective-permute-start | bytes 49160 | tf_op jit(solution)/shard_map/ppermute | solution.py:35
  177.2 4.7 %collective-permute-done.32 = f32[64,64]{1,0:T(8,128)S(1)} collective-permute-done((f32[64,64]{1,0:T(8,128)S(1)}, f32[64,64]{1,0:T(8,128)S(1)}, u32[]{:S(2)}, u32[]{:S(2)}) %collective-permute-start.32) | collective-permute-done | bytes 16416 | tf_op jit(solution)/shard_map/ppermute | solution.py:35
  182.7 4.5 %collective-permute-start.27 = (f32[64,64]{1,0:T(8,128)S(1)}, f32[64,64]{1,0:T(8,128)S(1)}, u32[]{:S(2)}, u32[]{:S(2)}) collective-permute-start(f32[64,64]{1,0:T(8,128)S(1)} %add.322), channel_id=1, source_target_pairs={{0,32},{1,33},{2,34},{3,35},{4,36},{5,37},{6,38},{7,39},{8,40},{9,... | collective-permute-start | bytes 49160 | tf_op jit(solution)/shard_map/ppermute | solution.py:35
  195.8 5.8 %collective-permute-done.26 = f32[64,64]{1,0:T(8,128)S(1)} collective-permute-done((f32[64,64]{1,0:T(8,128)S(1)}, f32[64,64]{1,0:T(8,128)S(1)}, u32[]{:S(2)}, u32[]{:S(2)}) %collective-permute-start.26) | collective-permute-done | bytes 16416 | tf_op jit(solution)/shard_map/ppermute | solution.py:35
  201.6 3.5 %collective-permute-start.23 = (f32[64,64]{1,0:T(8,128)S(1)}, f32[64,64]{1,0:T(8,128)S(1)}, u32[]{:S(2)}, u32[]{:S(2)}) collective-permute-start(f32[64,64]{1,0:T(8,128)S(1)} %add.313), channel_id=1, source_target_pairs={{16,0},{17,1},{18,2},{19,3},{20,4},{21,5},{22,6},{23,7},{24,8},{25... | collective-permute-start | bytes 49160 | tf_op jit(solution)/shard_map/ppermute | solution.py:35
  205.3 3.4 %collective-permute-done.23 = f32[64,64]{1,0:T(8,128)S(1)} collective-permute-done((f32[64,64]{1,0:T(8,128)S(1)}, f32[64,64]{1,0:T(8,128)S(1)}, u32[]{:S(2)}, u32[]{:S(2)}) %collective-permute-start.23) | collective-permute-done | bytes 16416 | tf_op jit(solution)/shard_map/ppermute | solution.py:35
  215.8 3.8 %collective-permute-done.21 = f32[64,64]{1,0:T(8,128)S(1)} collective-permute-done((f32[64,64]{1,0:T(8,128)S(1)}, f32[64,64]{1,0:T(8,128)S(1)}, u32[]{:S(2)}, u32[]{:S(2)}) %collective-permute-start.21) | collective-permute-done | bytes 16416 | tf_op jit(solution)/shard_map/ppermute | solution.py:35
  219.6 3.7 %collective-permute-start.17 = (f32[64,64]{1,0:T(8,128)}, f32[64,64]{1,0:T(8,128)S(1)}, u32[]{:S(2)}, u32[]{:S(2)}) collective-permute-start(f32[64,64]{1,0:T(8,128)} %add.304), channel_id=1, source_target_pairs={{0,8},{1,9},{2,10},{3,11},{4,12},{5,13},{6,14},{7,15},{8,16},{9,17... | collective-permute-start | bytes 49160 | tf_op jit(solution)/shard_map/ppermute | solution.py:35
  224.5 9.0 %collective-permute-start.37 = (f32[64,64]{1,0:T(8,128)S(1)}, f32[64,64]{1,0:T(8,128)S(1)}, u32[]{:S(2)}, u32[]{:S(2)}) collective-permute-start(f32[64,64]{1,0:T(8,128)S(1)} %fusion.59), channel_id=1, source_target_pairs={{0,4},{1,5},{2,6},{3,7},{4,8},{5,9},{6,10},{7,11},{8,12},{9,13},{1... | collective-permute-start | bytes 49160 | tf_op jit(solution)/shard_map/ppermute | solution.py:35
  234.6 3.7 %collective-permute-start.16 = (f32[64,64]{1,0:T(8,128)}, f32[64,64]{1,0:T(8,128)S(1)}, u32[]{:S(2)}, u32[]{:S(2)}) collective-permute-start(f32[64,64]{1,0:T(8,128)} %add.304), channel_id=1, source_target_pairs={{0,12},{1,13},{2,14},{3,15},{4,16},{5,17},{6,18},{7,19},{8,20},{9,... | collective-permute-start | bytes 49160 | tf_op jit(solution)/shard_map/ppermute | solution.py:35
  238.4 3.4 %collective-permute-done.16 = f32[64,64]{1,0:T(8,128)S(1)} collective-permute-done((f32[64,64]{1,0:T(8,128)}, f32[64,64]{1,0:T(8,128)S(1)}, u32[]{:S(2)}, u32[]{:S(2)}) %collective-permute-start.16) | collective-permute-done | bytes 16416 | tf_op jit(solution)/shard_map/ppermute | solution.py:35
  242.0 9.8 %collective-permute-start.38 = (f32[64,64]{1,0:T(8,128)S(1)}, f32[64,64]{1,0:T(8,128)S(1)}, u32[]{:S(2)}, u32[]{:S(2)}) collective-permute-start(f32[64,64]{1,0:T(8,128)S(1)} %fusion.63), channel_id=1, source_target_pairs={{0,2},{1,3},{2,4},{3,5},{4,6},{5,7},{6,8},{7,9},{8,10},{9,11},{10,... | collective-permute-start | bytes 49160 | tf_op jit(solution)/shard_map/ppermute | solution.py:35
  253.8 26.3 %collective-permute-start.39 = (f32[64,64]{1,0:T(8,128)}, f32[64,64]{1,0:T(8,128)}, u32[]{:S(2)}, u32[]{:S(2)}) collective-permute-start(f32[64,64]{1,0:T(8,128)} %fusion.67), channel_id=1, source_target_pairs={{0,1},{1,2},{2,3},{3,4},{4,5},{5,6},{6,7},{7,8},{8,9},{9,10},{10,1... | collective-permute-start | bytes 49160 | tf_op jit(solution)/shard_map/ppermute | solution.py:35
  281.4 13.5 %gather_fusion = bf16[512,64,64]{2,1,0:T(8,128)(2,1)} fusion(bf16[80,64,64]{2,1,0:T(8,128)(2,1)S(1)} %pad_maximum_fusion, s32[1024]{0:T(1024)S(1)} %pad_clamp_fusion.1), kind=kCustom, calls=%fused_computation | custom fusion | bytes 8390656 | tf_op jit(solution)/shard_map/jit(_take)/gather | solution.py:48
  296.9 3.2 fusion.74
  300.1 8.7 %fusion.40 = bf16[64,64,64]{2,1,0:T(8,128)(2,1)S(1)} fusion(f32[8,64,8,64]{3,1,2,0:T(8,128)} %fusion.74, bf16[64,8,64,64]{3,2,1,0:T(8,128)(2,1)} %param.23, bf16[64,8,64,64]{3,2,1,0:T(8,128)(2,1)} %bitcast.214, pred[64,8]{1,0:T(8,128)(4,1)S(1)} %copy.23, bf16[64,8]{1,0:T(8,128)(2,1)} %fusion.165), kind=kOutput, calls=%fused_computation.49 | convolution fusion | flops 273154048 | bytes 9963008 | tf_op jit(solution)/shard_map/nksr,nkrq->nsq/dot_general | solution.py:51
  309.8 11.1 %fusion.33 = bf16[64,64,256]{2,1,0:T(8,128)(2,1)} fusion(f32[64,64,256]{2,1,0:T(8,128)S(1)} %fusion.185, f32[64,64,256]{2,1,0:T(8,128)S(1)} %copy-done.29, f32[64,256,64]{1,2,0:T(8,128)S(1)} %copy-done.28, f32[64,256]{1,0:T(8,128)S(1)} %copy-done.20, f32[64,256]{1,0:T(8,128)S(1)} %copy-done.21, f32[64,256]{1,0:T(8,128)S(1)} %copy-done.19, ...), kind=kOutput, calls=%fused_computation.39 | convolution fusion | flops 588251136 | bytes 17303040 | tf_op jit(solution)/shard_map/lsp,lpq->lsq/dot_general | solution.py:96
  (184 shorter events, 98.5 us)
Async XLA Ops:
  6.8 45.5 %collective-permute-start.9 = (f32[64,64]{1,0:T(8,128)}, f32[64,64]{1,0:T(8,128)S(1)}, u32[]{:S(2)}, u32[]{:S(2)}) collective-permute-start(f32[64,64]{1,0:T(8,128)} %convolution_bitcast_fusion.3), channel_id=1, source_target_pairs={{3,0},{4,1},{5,2},{6,3},{7,4},{8,5},{9,6},{10,7},{11,8},{12,9},{13... | collective-permute-start | bytes 49160 | tf_op jit(solution)/shard_map/ppermute | solution.py:35
  9.8 45.3 %collective-permute-start.8 = (f32[64,64]{1,0:T(8,128)}, f32[64,64]{1,0:T(8,128)S(1)}, u32[]{:S(2)}, u32[]{:S(2)}) collective-permute-start(f32[64,64]{1,0:T(8,128)} %convolution_bitcast_fusion.3), channel_id=1, source_target_pairs={{2,0},{3,1},{4,2},{5,3},{6,4},{7,5},{8,6},{9,7},{10,8},{11,9},{12,... | collective-permute-start | bytes 49160 | tf_op jit(solution)/shard_map/ppermute | solution.py:35
  12.0 51.7 %collective-permute-start.7 = (f32[64,64]{1,0:T(8,128)}, f32[64,64]{1,0:T(8,128)S(1)}, u32[]{:S(2)}, u32[]{:S(2)}) collective-permute-start(f32[64,64]{1,0:T(8,128)} %convolution_bitcast_fusion.3), channel_id=1, source_target_pairs={{0,2},{1,3},{2,4},{3,5},{4,6},{5,7},{6,8},{7,9},{8,10},{9,11},{10,... | collective-permute-start | bytes 49160 | tf_op jit(solution)/shard_map/ppermute | solution.py:35
  19.4 276.5 %collective-permute-start.6 = (f32[64,64]{1,0:T(8,128)}, f32[64,64]{1,0:T(8,128)}, u32[]{:S(2)}, u32[]{:S(2)}) collective-permute-start(f32[64,64]{1,0:T(8,128)} %convolution_bitcast_fusion.3), channel_id=1, source_target_pairs={{0,3},{1,4},{2,5},{3,6},{4,7},{5,8},{6,9},{7,10},{8,11},{9,12},{10... | collective-permute-start | bytes 49160 | tf_op jit(solution)/shard_map/ppermute | solution.py:35
  23.7 19.8 %collective-permute-start.10 = (f32[64,64]{1,0:T(8,128)S(1)}, f32[64,64]{1,0:T(8,128)S(1)}, u32[]{:S(2)}, u32[]{:S(2)}) collective-permute-start(f32[64,64]{1,0:T(8,128)S(1)} %fusion.120), channel_id=1, source_target_pairs={{1,0},{2,1},{3,2},{4,3},{5,4},{6,5},{7,6},{8,7},{9,8},{10,9},{11,1... | collective-permute-start | bytes 49160 | tf_op jit(solution)/shard_map/ppermute | solution.py:35
  43.6 48.6 %collective-permute-start.4 = (bf16[4,64,64]{2,1,0:T(8,128)(2,1)S(1)}, bf16[4,64,64]{2,1,0:T(8,128)(2,1)S(1)}, u32[]{:S(2)}, u32[]{:S(2)}) collective-permute-start(bf16[4,64,64]{2,1,0:T(8,128)(2,1)S(1)} %get-tuple-element.25), channel_id=1, source_target_pairs={{0,1},{1,2},{2,3},{3,4},{4,5},{5,6},{6,7},{7,8},{8,9},{9,10},{10,1... | collective-permute-start | bytes 98312 | tf_op jit(solution)/shard_map/ppermute | solution.py:23
  52.4 47.6 %collective-permute-start.5 = (bf16[4,64,64]{2,1,0:T(8,128)(2,1)S(1)}, bf16[4,64,64]{2,1,0:T(8,128)(2,1)S(1)}, u32[]{:S(2)}, u32[]{:S(2)}) collective-permute-start(bf16[4,64,64]{2,1,0:T(8,128)(2,1)S(1)} %get-tuple-element.26), channel_id=1, source_target_pairs={{1,0},{2,1},{3,2},{4,3},{5,4},{6,5},{7,6},{8,7},{9,8},{10,9},{11,1... | collective-permute-start | bytes 98312 | tf_op jit(solution)/shard_map/ppermute | solution.py:25
  55.1 225.0 %collective-permute-start.2 = (bf16[8,64,64]{2,1,0:T(8,128)(2,1)}, bf16[8,64,64]{2,1,0:T(8,128)(2,1)S(1)}, u32[]{:S(2)}, u32[]{:S(2)}) collective-permute-start(bf16[8,64,64]{2,1,0:T(8,128)(2,1)} %get-tuple-element.20), channel_id=1, source_target_pairs={{0,1},{1,2},{2,3},{3,4},{4,5},{5,6},{6,7},{7,8},{8,9},{9,10},{10,1... | collective-permute-start | bytes 196616 | tf_op jit(solution)/shard_map/ppermute | solution.py:23
  63.7 8.9 %collective-permute-start.15 = (f32[64,64]{1,0:T(8,128)S(1)}, f32[64,64]{1,0:T(8,128)S(1)}, u32[]{:S(2)}, u32[]{:S(2)}) collective-permute-start(f32[64,64]{1,0:T(8,128)S(1)} %fusion.114), channel_id=1, source_target_pairs={{2,0},{3,1},{4,2},{5,3},{6,4},{7,5},{8,6},{9,7},{10,8},{11,9},{12,... | collective-permute-start | bytes 49160 | tf_op jit(solution)/shard_map/ppermute | solution.py:35
  72.6 7.7 %collective-permute-start.14 = (f32[64,64]{1,0:T(8,128)S(1)}, f32[64,64]{1,0:T(8,128)S(1)}, u32[]{:S(2)}, u32[]{:S(2)}) collective-permute-start(f32[64,64]{1,0:T(8,128)S(1)} %add.295), channel_id=1, source_target_pairs={{6,0},{7,1},{8,2},{9,3},{10,4},{11,5},{12,6},{13,7},{14,8},{15,9},... | collective-permute-start | bytes 49160 | tf_op jit(solution)/shard_map/ppermute | solution.py:35
  80.3 9.2 %collective-permute-start.13 = (f32[64,64]{1,0:T(8,128)S(1)}, f32[64,64]{1,0:T(8,128)S(1)}, u32[]{:S(2)}, u32[]{:S(2)}) collective-permute-start(f32[64,64]{1,0:T(8,128)S(1)} %add.295), channel_id=1, source_target_pairs={{4,0},{5,1},{6,2},{7,3},{8,4},{9,5},{10,6},{11,7},{12,8},{13,9},{1... | collective-permute-start | bytes 49160 | tf_op jit(solution)/shard_map/ppermute | solution.py:35
  89.4 190.7 %collective-permute-start.3 = (bf16[8,64,64]{2,1,0:T(8,128)(2,1)}, bf16[8,64,64]{2,1,0:T(8,128)(2,1)}, u32[]{:S(2)}, u32[]{:S(2)}) collective-permute-start(bf16[8,64,64]{2,1,0:T(8,128)(2,1)} %get-tuple-element.21), channel_id=1, source_target_pairs={{1,0},{2,1},{3,2},{4,3},{5,4},{6,5},{7,6},{8,7},{9,8},{10,9},{11,1... | collective-permute-start | bytes 196616 | tf_op jit(solution)/shard_map/ppermute | solution.py:25
  92.1 18.4 %collective-permute-start = (bf16[1,67,256]{2,1,0:T(8,128)(2,1)}, bf16[1,67,256]{2,1,0:T(8,128)(2,1)}, u32[]{:S(2)}, u32[]{:S(2)}) collective-permute-start(bf16[1,67,256]{2,1,0:T(8,128)(2,1)} %get-tuple-element.19), channel_id=1, source_target_pairs={{0,1},{1,2},{2,3},{3,4},{4,5},{5,6},{6,7},{7,8},{8,9},{9,10},{10,1... | collective-permute-start | bytes 102920 | tf_op jit(solution)/shard_map/ppermute | solution.py:23
  106.2 10.0 %collective-permute-start.1 = (bf16[1,67,256]{2,1,0:T(8,128)(2,1)}, bf16[1,67,256]{2,1,0:T(8,128)(2,1)S(1)}, u32[]{:S(2)}, u32[]{:S(2)}) collective-permute-start(bf16[1,67,256]{2,1,0:T(8,128)(2,1)} %get-tuple-element.18), channel_id=1, source_target_pairs={{1,0},{2,1},{3,2},{4,3},{5,4},{6,5},{7,6},{8,7},{9,8},{10,9},{11,1... | collective-permute-start | bytes 102920 | tf_op jit(solution)/shard_map/ppermute | solution.py:25
  110.5 24.6 %collective-permute-start.19 = (f32[64,64]{1,0:T(8,128)}, f32[64,64]{1,0:T(8,128)S(1)}, u32[]{:S(2)}, u32[]{:S(2)}) collective-permute-start(f32[64,64]{1,0:T(8,128)} %add.304), channel_id=1, source_target_pairs={{12,0},{13,1},{14,2},{15,3},{16,4},{17,5},{18,6},{19,7},{20,8},{21... | collective-permute-start | bytes 49160 | tf_op jit(solution)/shard_map/ppermute | solution.py:35
  116.2 15.4 %collective-permute-start.20 = (f32[64,64]{1,0:T(8,128)}, f32[64,64]{1,0:T(8,128)S(1)}, u32[]{:S(2)}, u32[]{:S(2)}) collective-permute-start(f32[64,64]{1,0:T(8,128)} %fusion.108), channel_id=1, source_target_pairs={{4,0},{5,1},{6,2},{7,3},{8,4},{9,5},{10,6},{11,7},{12,8},{13,9},{1... | collective-permute-start | bytes 49160 | tf_op jit(solution)/shard_map/ppermute | solution.py:35
  131.5 7.9 %collective-permute-start.18 = (f32[64,64]{1,0:T(8,128)}, f32[64,64]{1,0:T(8,128)S(1)}, u32[]{:S(2)}, u32[]{:S(2)}) collective-permute-start(f32[64,64]{1,0:T(8,128)} %add.304), channel_id=1, source_target_pairs={{8,0},{9,1},{10,2},{11,3},{12,4},{13,5},{14,6},{15,7},{16,8},{17,9... | collective-permute-start | bytes 49160 | tf_op jit(solution)/shard_map/ppermute | solution.py:35
  135.2 13.9 %collective-permute-start.24 = (f32[64,64]{1,0:T(8,128)S(1)}, f32[64,64]{1,0:T(8,128)S(1)}, u32[]{:S(2)}, u32[]{:S(2)}) collective-permute-start(f32[64,64]{1,0:T(8,128)S(1)} %add.313), channel_id=1, source_target_pairs={{24,0},{25,1},{26,2},{27,3},{28,4},{29,5},{30,6},{31,7},{32,8},{33... | collective-permute-start | bytes 49160 | tf_op jit(solution)/shard_map/ppermute | solution.py:35
  139.5 6.8 %collective-permute-start.25 = (f32[64,64]{1,0:T(8,128)S(1)}, f32[64,64]{1,0:T(8,128)S(1)}, u32[]{:S(2)}, u32[]{:S(2)}) collective-permute-start(f32[64,64]{1,0:T(8,128)S(1)} %fusion.102), channel_id=1, source_target_pairs={{8,0},{9,1},{10,2},{11,3},{12,4},{13,5},{14,6},{15,7},{16,8},{17,9... | collective-permute-start | bytes 49160 | tf_op jit(solution)/shard_map/ppermute | solution.py:35
  146.2 7.5 %collective-permute-start.22 = (f32[64,64]{1,0:T(8,128)S(1)}, f32[64,64]{1,0:T(8,128)S(1)}, u32[]{:S(2)}, u32[]{:S(2)}) collective-permute-start(f32[64,64]{1,0:T(8,128)S(1)} %add.313), channel_id=1, source_target_pairs={{0,16},{1,17},{2,18},{3,19},{4,20},{5,21},{6,22},{7,23},{8,24},{9,... | collective-permute-start | bytes 49160 | tf_op jit(solution)/shard_map/ppermute | solution.py:35
  149.1 6.7 %collective-permute-start.29 = (f32[64,64]{1,0:T(8,128)S(1)}, f32[64,64]{1,0:T(8,128)S(1)}, u32[]{:S(2)}, u32[]{:S(2)}) collective-permute-start(f32[64,64]{1,0:T(8,128)S(1)} %add.322), channel_id=1, source_target_pairs={{48,0},{49,1},{50,2},{51,3},{52,4},{53,5},{54,6},{55,7},{56,8},{57... | collective-permute-start | bytes 49160 | tf_op jit(solution)/shard_map/ppermute | solution.py:35
  153.7 11.1 %collective-permute-start.28 = (f32[64,64]{1,0:T(8,128)S(1)}, f32[64,64]{1,0:T(8,128)S(1)}, u32[]{:S(2)}, u32[]{:S(2)}) collective-permute-start(f32[64,64]{1,0:T(8,128)S(1)} %add.322), channel_id=1, source_target_pairs={{32,0},{33,1},{34,2},{35,3},{36,4},{37,5},{38,6},{39,7},{40,8},{41... | collective-permute-start | bytes 49160 | tf_op jit(solution)/shard_map/ppermute | solution.py:35
  155.8 7.1 %collective-permute-start.30 = (f32[64,64]{1,0:T(8,128)S(1)}, f32[64,64]{1,0:T(8,128)S(1)}, u32[]{:S(2)}, u32[]{:S(2)}) collective-permute-start(f32[64,64]{1,0:T(8,128)S(1)} %fusion.96), channel_id=1, source_target_pairs={{16,0},{17,1},{18,2},{19,3},{20,4},{21,5},{22,6},{23,7},{24,8},{25... | collective-permute-start | bytes 49160 | tf_op jit(solution)/shard_map/ppermute | solution.py:35
  162.9 90.2 %collective-permute-start.11 = (f32[64,64]{1,0:T(8,128)S(1)}, f32[64,64]{1,0:T(8,128)S(1)}, u32[]{:S(2)}, u32[]{:S(2)}) collective-permute-start(f32[64,64]{1,0:T(8,128)S(1)} %copy-done.10), channel_id=1, source_target_pairs={{0,6},{1,7},{2,8},{3,9},{4,10},{5,11},{6,12},{7,13},{8,14},{9,15},... | collective-permute-start | bytes 49160 | tf_op jit(solution)/shard_map/ppermute | solution.py:35
  165.7 10.1 %collective-permute-start.33 = (f32[64,64]{1,0:T(8,128)S(1)}, f32[64,64]{1,0:T(8,128)S(1)}, u32[]{:S(2)}, u32[]{:S(2)}) collective-permute-start(f32[64,64]{1,0:T(8,128)S(1)} %add.331), channel_id=1, source_target_pairs={{64,0},{65,1},{66,2},{67,3},{68,4},{69,5},{70,6},{71,7},{72,8},{73... | collective-permute-start | bytes 49160 | tf_op jit(solution)/shard_map/ppermute | solution.py:35
  194.3 7.3 %collective-permute-start.26 = (f32[64,64]{1,0:T(8,128)S(1)}, f32[64,64]{1,0:T(8,128)S(1)}, u32[]{:S(2)}, u32[]{:S(2)}) collective-permute-start(f32[64,64]{1,0:T(8,128)S(1)} %add.322), channel_id=1, source_target_pairs={{0,48},{1,49},{2,50},{3,51},{4,52},{5,53},{6,54},{7,55},{8,56},{9,... | collective-permute-start | bytes 49160 | tf_op jit(solution)/shard_map/ppermute | solution.py:35
  201.6 7.1 %collective-permute-start.23 = (f32[64,64]{1,0:T(8,128)S(1)}, f32[64,64]{1,0:T(8,128)S(1)}, u32[]{:S(2)}, u32[]{:S(2)}) collective-permute-start(f32[64,64]{1,0:T(8,128)S(1)} %add.313), channel_id=1, source_target_pairs={{16,0},{17,1},{18,2},{19,3},{20,4},{21,5},{22,6},{23,7},{24,8},{25... | collective-permute-start | bytes 49160 | tf_op jit(solution)/shard_map/ppermute | solution.py:35
  213.3 6.2 %collective-permute-start.21 = (f32[64,64]{1,0:T(8,128)S(1)}, f32[64,64]{1,0:T(8,128)S(1)}, u32[]{:S(2)}, u32[]{:S(2)}) collective-permute-start(f32[64,64]{1,0:T(8,128)S(1)} %add.313), channel_id=1, source_target_pairs={{0,24},{1,25},{2,26},{3,27},{4,28},{5,29},{6,30},{7,31},{8,32},{9,... | collective-permute-start | bytes 49160 | tf_op jit(solution)/shard_map/ppermute | solution.py:35
  224.5 10.0 %collective-permute-start.37 = (f32[64,64]{1,0:T(8,128)S(1)}, f32[64,64]{1,0:T(8,128)S(1)}, u32[]{:S(2)}, u32[]{:S(2)}) collective-permute-start(f32[64,64]{1,0:T(8,128)S(1)} %fusion.59), channel_id=1, source_target_pairs={{0,4},{1,5},{2,6},{3,7},{4,8},{5,9},{6,10},{7,11},{8,12},{9,13},{1... | collective-permute-start | bytes 49160 | tf_op jit(solution)/shard_map/ppermute | solution.py:35
  234.6 7.3 %collective-permute-start.16 = (f32[64,64]{1,0:T(8,128)}, f32[64,64]{1,0:T(8,128)S(1)}, u32[]{:S(2)}, u32[]{:S(2)}) collective-permute-start(f32[64,64]{1,0:T(8,128)} %add.304), channel_id=1, source_target_pairs={{0,12},{1,13},{2,14},{3,15},{4,16},{5,17},{6,18},{7,19},{8,20},{9,... | collective-permute-start | bytes 49160 | tf_op jit(solution)/shard_map/ppermute | solution.py:35
  242.0 10.8 %collective-permute-start.38 = (f32[64,64]{1,0:T(8,128)S(1)}, f32[64,64]{1,0:T(8,128)S(1)}, u32[]{:S(2)}, u32[]{:S(2)}) collective-permute-start(f32[64,64]{1,0:T(8,128)S(1)} %fusion.63), channel_id=1, source_target_pairs={{0,2},{1,3},{2,4},{3,5},{4,6},{5,7},{6,8},{7,9},{8,10},{9,11},{10,... | collective-permute-start | bytes 49160 | tf_op jit(solution)/shard_map/ppermute | solution.py:35
  253.8 41.1 %collective-permute-start.39 = (f32[64,64]{1,0:T(8,128)}, f32[64,64]{1,0:T(8,128)}, u32[]{:S(2)}, u32[]{:S(2)}) collective-permute-start(f32[64,64]{1,0:T(8,128)} %fusion.67), channel_id=1, source_target_pairs={{0,1},{1,2},{2,3},{3,4},{4,5},{5,6},{6,7},{7,8},{8,9},{9,10},{10,1... | collective-permute-start | bytes 49160 | tf_op jit(solution)/shard_map/ppermute | solution.py:35
  (38 other events, 1311.2 us)
where the time goes:
time: 323 us; the launch traced here: 321 us
  starting transfers between devices  163 us (50%)
  matrix products  69.2 us (21%)
  waiting for transfers between devices  59.5 us (18%)
  local copies, waits for them, and re-layouts  22 us (7%)
  other arithmetic  6.15 us (2%)
    ppermute x34, starting transfers between devices, shifted(): return lax.ppermute(block, axis, route)  133 us
    ppermute x34, waiting for transfers between devices, shifted(): return lax.ppermute(block, axis, route)  55.8 us
    dot_general x3, matrix products, shards(): jnp.einsum('lsp,lpq->lsq', window[:, :columns], kernel, preferred_element...  32.3 us
    ppermute x3, starting transfers between devices, padded_2(): lax.ppermute(tail, axis, [(i, (i + 1) % count) for i in range(ends)])  23.6 us
    gather x2, local copies, waits for them, and re-layouts, couple_rows(): picked = jnp.take(padded, local_index, axis=0)  15 us
    dot_general x2, matrix products, couple_rows(): jnp.einsum('nksr,nkrq->nsq', picked, blocks, preferred_element_type=jnp.f...  11 us
    dot_general x24, matrix products, shards(): jnp.dot(partner, couple_top[0, height, slot_index], precision=highest_pre...  8.48 us
  transfers between devices with their start and end apart: 40, of which 19 were waited for; matrix products, arithmetic and copies ran while one was open for 20% of the time, Pallas kernels for 0%

commit v1 on v0

v1 whole, which is shorter than its diff:
```python
import functools

import jax
import jax.numpy as jnp
from jax import lax
from jax.experimental import pallas as pl
from jax.experimental.pallas import tpu as pltpu
from jax.sharding import PartitionSpec as P

bf16 = jnp.bfloat16
f32 = jnp.float32
core_square = 0.0004
W0 = 8
W1 = 4
LEAF_AT, NODE_AT, RHS_AT, COORD_AT, HALO_TILES = 0, 4, 6, 8, 9
CARRY_AT, COEFF_AT = 9, 10


def dot(a, b):
    return jnp.dot(a, b, preferred_element_type=f32)


def dot_rows(a, b):
    return lax.dot_general(a, b, (((1,), (1,)), ((), ())), preferred_element_type=f32)


def dot_columns(a, b):
    return lax.dot_general(a, b, (((0,), (0,)), ((), ())), preferred_element_type=f32)


def low_lanes(shape):
    return lax.broadcasted_iota(jnp.int32, shape, len(shape) - 1) < shape[-1] // 2


def join(low, high):
    return jnp.where(low_lanes(low.shape), low.astype(f32), high.astype(f32)).astype(bf16)


def twice(block):
    return jnp.concatenate([block, block], axis=1)


def split(wide):
    hi = wide.astype(bf16).astype(f32)
    return jnp.concatenate([hi, wide - hi], axis=1).astype(bf16)


def fused_halves(block):
    half = block.shape[1] // 2
    return block[:, :half] + block[:, half:]


def wide_dot(left, matrix_parts):
    weights = jnp.concatenate([matrix_parts, matrix_parts], axis=0)
    return fused_halves(dot(split(left), weights))


def call(body, out_shape, grid, in_specs, out_specs, scratch=(), name=None, aliases=None, mib=16):
    return pl.pallas_call(
        body,
        out_shape=out_shape,
        grid=grid,
        in_specs=in_specs,
        out_specs=out_specs,
        scratch_shapes=list(scratch),
        input_output_aliases=aliases or {},
        compiler_params=pltpu.CompilerParams(vmem_limit_bytes=mib * 2**20),
        name=name,
    )


def whole(array):
    rank = array.ndim
    return pl.BlockSpec(array.shape, lambda i, rank=rank: (0,) * rank)


def rows(array, count):
    rank = array.ndim
    return pl.BlockSpec((count,) + array.shape[1:], lambda i, rank=rank: (i,) + (0,) * (rank - 1))


def scalars():
    return pl.BlockSpec(memory_space=pltpu.SMEM)


def shape(dims, dtype):
    return jax.ShapeDtypeStruct(dims, dtype)


def coordinate_rows(points):
    count = points.shape[1]
    scaled = points.astype(f32) * 256.0
    square = jnp.sum(scaled * scaled, axis=0, keepdims=True)
    row = lax.broadcasted_iota(jnp.int32, (16, count), 0)
    padded = jnp.concatenate([scaled, jnp.zeros((13, count), f32)], axis=0)

    def fill(base, at, ones_at, value):
        hi = value.astype(bf16).astype(f32)
        mid = (value - hi).astype(bf16).astype(f32)
        low = value - hi - mid
        base = jnp.where(row == at, hi, base)
        base = jnp.where(row == at + 1, mid, base)
        base = jnp.where(row == at + 2, low, base)
        return jnp.where((row >= ones_at) & (row < ones_at + 3), 1.0, base)

    source = fill(-2.0 * padded, 6, 3, square + core_square * 65536.0)
    target = fill(padded, 3, 6, square)
    return source.astype(bf16), target.astype(bf16)


def upward_body(
    dev_ref, rhs_ref, points_ref, bases_ref, up_leaf_ref, up_node_ref, up_top_ref,
    leaf_ref, node_ref, source_ref, target_ref, inner_ref, outer_ref, total,
):
    step = pl.program_id(0)
    last = pl.num_programs(0) - 1
    odd = lax.rem(dev_ref[0], 2) == 1
    pairs = []
    for b in range(8):
        base = bases_ref[b]
        coeff = dot_rows(rhs_ref[b], jnp.concatenate([base, base], axis=0)).astype(bf16)
        leaf_ref[b] = coeff
        source, target = coordinate_rows(points_ref[:, b, :])
        source_ref[b] = source
        target_ref[b] = target
        if b % 2 == 1:
            pairs.append(join(before, coeff))
        before = coeff
    up = up_leaf_ref[...].reshape(512, 64)
    node = dot(jnp.concatenate(pairs, axis=1), up).astype(bf16)
    node_ref[step] = twice(node)
    part = dot(node, up_node_ref[0])

    @pl.when(step == 0)
    def _():
        total[...] = part

    @pl.when(step > 0)
    def _():
        total[...] += part

    def edge(message, leaf):
        for j in range(4):
            message[LEAF_AT + j] = pairs[j]
        message[RHS_AT] = rhs_ref[leaf, :, :128]
        message[RHS_AT + 1] = rhs_ref[leaf, :, 128:]
        message[COORD_AT, 0:16, :] = source_ref[leaf, :, :128]
        message[COORD_AT, 16:32, :] = source_ref[leaf, :, 128:]
        message[COORD_AT, 32:48, :] = target_ref[leaf, :, :128]
        message[COORD_AT, 48:64, :] = target_ref[leaf, :, 128:]

    def edge_nodes(message, first):
        for j in range(2):
            message[NODE_AT + j] = join(node_ref[first + 2 * j], node_ref[first + 2 * j + 1])

    @pl.when((step == 0) & odd)
    def _():
        edge(inner_ref, 0)

    @pl.when((step == 0) & ~odd)
    def _():
        edge(outer_ref, 0)

    @pl.when((step == last) & odd)
    def _():
        edge(outer_ref, 7)
        edge_nodes(outer_ref, 4)
        edge_nodes(inner_ref, 0)

    @pl.when((step == last) & ~odd)
    def _():
        edge(inner_ref, 7)
        edge_nodes(inner_ref, 4)
        edge_nodes(outer_ref, 0)

    @pl.when(step == last)
    def _():
        coeff = total[...]
        inner_ref[CARRY_AT] = split(wide_dot(coeff, split(up_top_ref[0, 0])))
        inner_ref[COEFF_AT] = twice(coeff).astype(bf16)


def upward(dev, rhs, points, bases, up_leaf, up_node, up_top):
    leaves = rhs.shape[0]
    groups = up_node.shape[0]
    outs = [
        shape((leaves, 64, 128), bf16),
        shape((groups, 64, 128), bf16),
        shape((leaves, 16, 256), bf16),
        shape((leaves, 16, 256), bf16),
        shape((HALO_TILES + 2, 64, 128), bf16),
        shape((HALO_TILES, 64, 128), bf16),
    ]
    return call(
        upward_body,
        outs,
        (groups,),
        [scalars(), rows(rhs, 8), pl.BlockSpec((3, 8, 256), lambda i: (0, i, 0)), rows(bases, 8), rows(up_leaf, 8), rows(up_node, 1), whole(up_top)],
        [rows(outs[0], 8), whole(outs[1]), rows(outs[2], 8), rows(outs[3], 8), whole(outs[4]), whole(outs[5])],
        [pltpu.VMEM((64, 64), f32)],
        name="upward",
        mib=60,
    )(dev, rhs, points, bases, up_leaf, up_node, up_top)


def merge(own_ref, got_ref, carry_at, coeff_at, bit, hold):
    sums = own_ref[carry_at].astype(f32) + got_ref[carry_at].astype(f32)
    parent = fused_halves(sums)
    hold[bit] = own_ref[coeff_at]
    hold[1 - bit] = got_ref[coeff_at]
    return parent, join(hold[0], hold[1])


def ordered(own, got, bit, hold):
    hold[bit] = own
    hold[1 - bit] = got
    return hold[0], hold[1]


def bit_of(dev_ref, height):
    return (dev_ref[0] >> height) & 1


def carried(parent, up_top_ref, height):
    return split(wide_dot(parent, split(up_top_ref[0, height])))


def level_0_body(dev_ref, own, got, up_top_ref, out, hold):
    parent, pair = merge(own, got, CARRY_AT, COEFF_AT, bit_of(dev_ref, 0), hold)
    out[0] = carried(parent, up_top_ref, 1)
    out[1] = twice(parent).astype(bf16)
    out[2] = pair


def level_1_body(dev_ref, own, got, up_top_ref, out, hold):
    bit = bit_of(dev_ref, 1)
    parent, pair = merge(own, got, 0, 1, bit, hold)
    out[0] = carried(parent, up_top_ref, 2)
    out[1] = twice(parent).astype(bf16)
    out[2] = pair
    out[3], out[4] = ordered(own[2], got[2], bit, hold)


def level_2_body(dev_ref, own, got, up_top_ref, out, up_out, down_out, hold):
    bit = bit_of(dev_ref, 2)
    parent, pair = merge(own, got, 0, 1, bit, hold)
    out[0] = carried(parent, up_top_ref, 3)
    out[1] = twice(parent).astype(bf16)
    down_out[0] = ordered(own[3], got[3], bit, hold)[0]
    up_out[0] = ordered(own[4], got[4], bit, hold)[1]
    down_out[1], up_out[1] = ordered(own[2], got[2], bit, hold)
    down_out[2] = pair
    up_out[2] = pair


def level_3_body(dev_ref, own, got, up_top_ref, out, hold):
    parent, pair = merge(own, got, 0, 1, bit_of(dev_ref, 3), hold)
    out[0] = carried(parent, up_top_ref, 4)
    out[1] = twice(parent).astype(bf16)
    out[2] = pair


def level_4_body(dev_ref, own, got, near_out, far_out, across_out, hold):
    bit = bit_of(dev_ref, 4)
    parent, pair = merge(own, got, 0, 1, bit, hold)
    first, second = ordered(own[2], got[2], bit, hold)
    odd = bit_of(dev_ref, 5)
    near_out[0], far_out[0] = ordered(second, first, odd, hold)
    near_out[1] = pair
    far_out[1] = pair
    coeff = twice(parent).astype(bf16)
    far_out[2] = coeff
    across_out[0] = coeff


def level_call(body, dev, own, got, up_top, tiles, name):
    outs = [shape((count, 64, 128), bf16) for count in tiles]
    ins = [own, got] + ([] if up_top is None else [up_top])
    return call(
        body,
        outs,
        (1,),
        [scalars()] + [whole(a) for a in ins],
        [whole(a) for a in outs],
        [pltpu.VMEM((2, 64, 128), bf16)],
        name=name,
    )(dev, *ins)


def prepare_body(dev_ref, couple_ref, down_ref, couple_out, down_out):
    for height in range(6):
        odd = bit_of(dev_ref, height)
        even = 1 - odd
        picks = ((even, None), (1, odd), (2, even), (2 + even, None))
        for at, (slot, live) in enumerate(picks):
            matrix = couple_ref[0, height, slot]
            if live is not None:
                matrix = jnp.where(jnp.full(matrix.shape, live, jnp.int32) > 0, matrix, 0.0)
            couple_out[height, 64 * at : 64 * at + 64, :] = split(matrix)
    for height in range(5):
        down_out[height] = split(down_ref[0, height])


def prepare(dev, couple_top, down_top):
    outs = [shape((6, 256, 128), bf16), shape((5, 64, 128), bf16)]
    return call(
        prepare_body,
        outs,
        (1,),
        [scalars(), whole(couple_top), whole(down_top)],
        [whole(a) for a in outs],
        name="prepare",
    )(dev, couple_top, down_top)


def sides(dev_ref):
    odd = bit_of(dev_ref, 0)
    return 1 - odd, odd


def near_body(
    first, last, count, devices, dev_ref, rhs_ref, rhs_before, rhs_after, source_ref, target_ref,
    source_before, target_after, *rest,
):
    if first or last:
        inner_ref, outer_ref = rest[:2]
        rest = rest[2:]
    out_ref, kernels, rim_rhs, rim_source, rim_target = rest[-5:]
    step = pl.program_id(0)
    steps = pl.num_programs(0)
    rim_rhs[0] = rhs_before[0]
    rim_rhs[1] = rhs_after[0]
    rim_source[...] = source_before[0]
    rim_target[...] = target_after[0]

    if first or last:
        inner_at, _ = sides(dev_ref)

        def from_halo(side):
            def read(halo):
                rim_rhs[side, :, :128] = halo[RHS_AT]
                rim_rhs[side, :, 128:] = halo[RHS_AT + 1]

                @pl.when(dev_ref[0] != (0 if side == 0 else devices - 1))
                def _():
                    if side == 0:
                        rim_source[:, :128] = halo[COORD_AT, 0:16, :]
                        rim_source[:, 128:] = halo[COORD_AT, 16:32, :]
                    else:
                        rim_target[:, :128] = halo[COORD_AT, 32:48, :]
                        rim_target[:, 128:] = halo[COORD_AT, 48:64, :]

            at = step == (0 if side == 0 else steps - 1)

            @pl.when(at & (inner_at == side))
            def _():
                read(inner_ref)

            @pl.when(at & (inner_at != side))
            def _():
                read(outer_ref)

        if first:
            from_halo(0)
        if last:
            from_halo(1)

    def kernel_of(source, target):
        return lax.rsqrt(dot_columns(source, target)).astype(bf16)

    def build(s):
        after = target_ref[s + 1] if s + 1 < count else rim_target[...]
        kernels[s % 2] = kernel_of(source_ref[s], jnp.concatenate([target_ref[s], after], axis=1))

    before = kernel_of(rim_source[...], target_ref[0])
    build(0)
    out_ref[0] = dot(rim_rhs[0], before)
    for s in range(count):
        if s + 1 < count:
            build(s + 1)
        kernel = kernels[s % 2]
        after = rhs_ref[s + 1] if s + 1 < count else rim_rhs[1]
        out_ref[s] += dot(rhs_ref[s], kernel[:, :256]) + dot_rows(after, kernel[:, 256:])
        if s + 1 < count:
            out_ref[s + 1] = dot(rhs_ref[s], kernel[:, 256:])


def near(dev, rhs, source, target, begin, steps, halos, total, name, count=8):
    leaves = rhs.shape[0]
    first = begin == 0
    last = (begin + steps) * count == leaves
    at = lambda array: pl.BlockSpec((count,) + array.shape[1:], lambda i: (begin + i, 0, 0))
    before = lambda array: pl.BlockSpec(
        (1,) + array.shape[1:], lambda i: (jnp.maximum((begin + i) * count - 1, 0), 0, 0)
    )
    after = lambda array: pl.BlockSpec(
        (1,) + array.shape[1:], lambda i: (jnp.minimum((begin + i + 1) * count, leaves - 1), 0, 0)
    )
    args = [dev, rhs, rhs, rhs, source, target, source, target]
    specs = [scalars(), at(rhs), before(rhs), after(rhs), at(source), at(target), before(source), after(target)]
    if first or last:
        args += halos
        specs += [whole(a) for a in halos]
    aliases = {}
    if total is not None:
        aliases = {len(args): 0}
        args.append(total)
        specs.append(pl.BlockSpec(memory_space=pl.ANY))
    out = shape(rhs.shape, f32)
    return call(
        functools.partial(near_body, first, last, count, lax.axis_size("leaf")),
        out,
        (steps,),
        specs,
        at(out),
        [
            pltpu.VMEM((2, 256, 512), bf16),
            pltpu.VMEM((2, 64, 256), bf16),
            pltpu.VMEM((16, 256), bf16),
            pltpu.VMEM((16, 256), bf16),
        ],
        name=name,
        aliases=aliases,
    )(*args)


def couple_body(
    dev_ref, list_ref, count_ref, node_list_ref, node_count_ref, leaf_ref, node_ref, inner_ref,
    outer_ref, blocks_ref, node_blocks_ref, gain_ref, node_gain_ref, leaf_hold, node_hold,
):
    step = pl.program_id(0)
    leaves = leaf_ref.shape[0]
    groups = node_ref.shape[0]

    @pl.when(step == 0)
    def _():
        leaf_hold[W0 : W0 + leaves] = leaf_ref[...]
        node_hold[W1 : W1 + groups] = node_ref[...]
        leaf_hold[leaves + 2 * W0] = jnp.zeros((64, 128), bf16)
        node_hold[groups + 2 * W1] = jnp.zeros((64, 128), bf16)
        inner_side, outer_side = sides(dev_ref)
        for halo, side in ((inner_ref, inner_side), (outer_ref, outer_side)):

            def unpack(hold, at, tile):
                pair = halo[tile].astype(f32)
                turned = pltpu.roll(pair, 64, 1)
                low = low_lanes(pair.shape)
                hold[at] = jnp.where(low, pair, turned).astype(bf16)
                hold[at + 1] = jnp.where(low, turned, pair).astype(bf16)

            for j in range(4):
                unpack(leaf_hold, side * (leaves + W0) + 2 * j, LEAF_AT + j)
            for j in range(2):
                unpack(node_hold, side * (groups + W1) + 2 * j, NODE_AT + j)

    def picked(hold, lists, counts, row, first, slots, nothing):
        tiles = []
        for j in range(slots // 2):
            pair = []
            for k in (2 * j, 2 * j + 1):
                live = k < counts[row]
                pair.append(hold[jnp.where(live, lists[k, row] - first, nothing)])
            tiles.append(join(*pair))
        return jnp.concatenate(tiles, axis=1)

    for b in range(8):
        row = step * 8 + b
        values = picked(
            leaf_hold, list_ref, count_ref, row, dev_ref[0] * leaves - W0, 8, leaves + 2 * W0
        )
        gain_ref[b] = dot(values, blocks_ref[b].reshape(512, 64))
    values = picked(
        node_hold, node_list_ref, node_count_ref, step, dev_ref[0] * groups - W1, 4, groups + 2 * W1
    )
    node_gain_ref[0] = dot(values, node_blocks_ref[0].reshape(256, 64))


def couple(dev, lists, counts, node_lists, node_counts, leaf, node, inner, outer, blocks, node_blocks):
    leaves, groups = leaf.shape[0], node.shape[0]
    outs = [shape((leaves, 64, 64), f32), shape((groups, 64, 64), f32)]
    return call(
        couple_body,
        outs,
        (groups,),
        [scalars()] * 5
        + [whole(leaf), whole(node), whole(inner), whole(outer), rows(blocks, 8), rows(node_blocks, 1)],
        [rows(outs[0], 8), rows(outs[1], 1)],
        [
            pltpu.VMEM((leaves + 2 * W0 + 1, 64, 128), bf16),
            pltpu.VMEM((groups + 2 * W1 + 1, 64, 128), bf16),
        ],
        name="couple",
    )(dev, lists, counts, node_lists, node_counts, leaf, node, inner, outer, blocks, node_blocks)


def downward_body(
    dev_ref, pair_ref, four_ref, before_ref, after_ref, sixteen_ref, near_ref, far_ref, across_ref,
    couple_ref, down_ref, down_node_ref, node_gain_ref, gain_ref, transfer_ref, bases_ref,
    sum_ref, out_ref, bank, node_value,
):
    step = pl.program_id(0)

    @pl.when(step == 0)
    def _():
        bank[0] = jnp.zeros((64, 128), bf16)
        bank[1] = pair_ref[2]
        for j in range(3):
            bank[2 + j] = four_ref[2 + j]
            bank[5 + j] = before_ref[j]
            bank[8 + j] = after_ref[j]
        bank[11] = sixteen_ref[2]
        bank[12] = near_ref[0]
        bank[13] = near_ref[1]
        bank[14] = far_ref[0]
        bank[15] = far_ref[1]
        d = dev_ref[0]
        q = d >> 5
        odd = q & 1
        bank[16 + odd] = across_ref[0]
        bank[17 - odd] = far_ref[2]
        bank[16] = join(bank[16], bank[17])
        pick = jnp.where
        even = lambda value: (value & 1) == 0
        m = d >> 1
        left = [pick(even(m), pick((m & 3) == 2, 4, 5), 1)]
        right = [pick(even(m), 1, pick((m & 3) == 1, 3, 8))]
        m = d >> 2
        left.append(pick(even(m), 6, 2))
        right.append(pick(even(m), 2, 9))
        left.append(7)
        right.append(10)
        m = d >> 4
        left.append(pick(even(m), pick(odd == 1, 12, pick(q == 2, 14, 0)), 11))
        right.append(pick(even(m), 11, pick(odd == 0, 12, pick(q == 1, 14, 0))))
        left.append(pick(odd == 1, 13, pick(q == 2, 15, 0)))
        right.append(pick(odd == 0, 13, pick(q == 1, 15, 0)))
        left.append(pick(q >= 2, 16, 0))
        right.append(pick(q >= 2, 0, 16))
        gains = [
            fused_halves(
                dot(jnp.concatenate([bank[left[h]], bank[right[h]]], axis=1), couple_ref[h])
            )
            for h in range(6)
        ]
        value = gains[5]
        for h in range(4, -1, -1):
            value = gains[h] + wide_dot(value, down_ref[h])
        rounded = value.astype(bf16)
        for a in range(8):
            node_value[a] = (node_gain_ref[a] + dot(rounded, down_node_ref[a])).astype(bf16)

    value = node_value[step]
    for b in range(8):
        leaf_value = (gain_ref[b] + dot(value, transfer_ref[b])).astype(bf16)
        out_ref[b] = (sum_ref[b] + dot(leaf_value, bases_ref[b])).astype(bf16)


def downward(dev, received, couple_parts, down_parts, down_node, node_gain, gain, transfer, bases, near_sum):
    fixed = list(received) + [couple_parts, down_parts, down_node, node_gain]
    moving = [gain, transfer, bases, near_sum]
    out = shape(bases.shape, bf16)
    return call(
        downward_body,
        out,
        (down_node.shape[0],),
        [scalars()] + [whole(a) for a in fixed] + [rows(a, 8) for a in moving],
        rows(out, 8),
        [pltpu.VMEM((18, 64, 128), bf16), pltpu.VMEM((8, 64, 64), bf16)],
        name="downward",
    )(dev, *fixed, *moving)


def tied(*values):
    return lax.optimization_barrier(values)


def shards(
    rhs, points, upward_leaf_bases, downward_leaf_bases, up_leaf, leaf_down_transfer, couple_leaf,
    list_leaf, count_leaf, up_node, down_node, couple_node, list_node, count_node, up_top, down_top,
    couple_top,
):
    device = lax.axis_index("leaf")
    devices = lax.axis_size("leaf")
    dev = device.astype(jnp.int32).reshape(1)

    def exchange(block, mask):
        return lax.ppermute(block, "leaf", [(i, i ^ mask) for i in range(devices)])

    def shifted(block, distance):
        route = [(i, i + distance) for i in range(devices) if 0 <= i + distance < devices]
        return lax.ppermute(block, "leaf", route)

    leaf, node, source, target, inner_out, outer_out = upward(
        dev, rhs, jnp.transpose(points, (1, 0, 2)), upward_leaf_bases, up_leaf, up_node, up_top
    )
    inner = exchange(inner_out, 1)
    outer = lax.ppermute(
        outer_out, "leaf",
        [(i, i + 1) for i in range(1, devices - 1, 2)] + [(i + 1, i) for i in range(1, devices - 1, 2)],
    )
    near_sum = near(dev, rhs, source, target, 2, 2, [], None, "near_a")
    inner, near_sum = tied(inner, near_sum)
    (level_1,) = level_call(level_0_body, dev, inner_out, inner, up_top, [3], "level_0")
    pair = exchange(level_1, 2)
    near_sum, _ = tied(near_sum, level_1)
    near_sum = near(dev, rhs, source, target, 4, 2, [], near_sum, "near_b")
    pair, near_sum = tied(pair, near_sum)
    (level_2,) = level_call(level_1_body, dev, level_1, pair, up_top, [5], "level_1")
    four = exchange(level_2, 4)
    near_sum, _ = tied(near_sum, level_2)
    near_sum = near(dev, rhs, source, target, 0, 2, [inner, outer], near_sum, "near_c")
    four, near_sum = tied(four, near_sum)
    level_3, up_out, down_out = level_call(
        level_2_body, dev, level_2, four, up_top, [2, 3, 3], "level_2"
    )
    eight = exchange(level_3, 8)
    before = shifted(up_out, 8)
    after = shifted(down_out, -8)
    near_sum, _ = tied(near_sum, level_3)
    near_sum = near(dev, rhs, source, target, 6, 2, [inner, outer], near_sum, "near_d")
    eight, near_sum = tied(eight, near_sum)
    (level_4,) = level_call(level_3_body, dev, level_3, eight, up_top, [3], "level_3")
    sixteen = exchange(level_4, 16)
    leaf, _ = tied(leaf, level_4)
    gain, node_gain = couple(
        dev, list_leaf.T, count_leaf, list_node.T, count_node, leaf, node, inner, outer,
        couple_leaf, couple_node,
    )
    sixteen, gain = tied(sixteen, gain)
    near_out, far_out, across_out = level_call(
        level_4_body, dev, level_4, sixteen, None, [2, 3, 1], "level_4"
    )
    beside = exchange(near_out, 32)
    across = exchange(across_out, 64)
    far = exchange(far_out, 96)
    couple_top, _ = tied(couple_top, near_out)
    couple_parts, down_parts = prepare(dev, couple_top, down_top)
    beside, across, far, couple_parts = tied(beside, across, far, couple_parts)
    return downward(
        dev, (pair, four, before, after, sixteen, beside, far, across), couple_parts, down_parts,
        down_node, node_gain, gain, leaf_down_transfer, downward_leaf_bases, near_sum,
    )


def solution(mesh):
    placed = tuple(P("leaf") for _ in range(17))
    return jax.shard_map(
        shards, mesh=mesh, in_specs=placed, out_specs=P("leaf"), check_vma=False
    )
```

time: 323 us -> 68.5 us (0.21)
  the two profiles are of different devices: /device:TPU:95 before, /device:TPU:0 now
where the time goes in v1:
time: 68.5 us; the launch traced here: 68.2 us
  Pallas kernels  34.3 us (50%)
  starting transfers between devices  27.9 us (41%)
  waiting for transfers between devices  3.39 us (5%)
  local copies, waits for them, and re-layouts  2.18 us (3%)
    ppermute x8, starting transfers between devices, exchange(): return lax.ppermute(block, 'leaf', [(i, i ^ mask) for i in range(devices)])  23.5 us
    pallas_call x4, Pallas kernels, near(): call(functools.partial(near_body, first, last, count, lax.axis_size('leaf...  11.1 us
    pallas_call x1, Pallas kernels, upward(): call(upward_body, outs, (groups,), [scalars(), rows(rhs, 8), pl.BlockSpec...  9.11 us
    pallas_call x1, Pallas kernels, downward(): call(downward_body, out, (down_node.shape[0],), [scalars()] + [whole(a) f...  8.18 us
    ppermute x2, starting transfers between devices, shifted(): return lax.ppermute(block, 'leaf', route)  3.81 us
    pallas_call x1, Pallas kernels, couple(): call(couple_body, outs, (groups,), [scalars()] * 5 + [whole(leaf), whole(...  3.79 us
    ppermute x8, waiting for transfers between devices, exchange(): return lax.ppermute(block, 'leaf', [(i, i ^ mask) for i in range(devices)])  3.38 us
    unnamed x40, local copies, waits for them, and re-layouts  2.18 us
  transfers between devices with their start and end apart: 11, of which 2 were waited for; matrix products, arithmetic and copies ran while one was open for 0% of the time, Pallas kernels for 23%

profile of v1, /device:TPU:0, one launch (start us, length us, event | category | flops | bytes accessed | tf_op | source)
XLA Modules:
  0.0 68.2 jit_solution(7302184608439410963)
XLA Ops:
  0.0 9.1 %upward.1 = (bf16[64,64,128]{2,1,0:T(8,128)(2,1)}, bf16[8,64,128]{2,1,0:T(8,128)(2,1)}, bf16[64,16,256]{2,1,0:T(8,128)(2,1)}, bf16[64,16,256]{2,1,0:T(8,128)(2,1...) custom-call(s32[1]{0:T(128)} %bitcast.dev_ref, bf16[64,64,256]{2,1,0:T(8,128)(2,1)} %rhs_after.7, ...), custom_call_target="tpu_custom_call" | custom-call | tf_op jit(solution)/shard_map/upward/pallas_call | solution.py:194
  9.1 0.1 collective-permute-start
  9.2 0.7 collective-permute-start.3
  9.9 1.0 %copy-done.1 = bf16[64,16,256]{2,1,0:T(8,128)(2,1)S(1)} copy-done((bf16[64,16,256]{2,1,0:T(8,128)(2,1)S(1)}, bf16[64,16,256]{2,1,0:T(8,128)(2,1)}, u32[]{:S(2)}) %copy-start.1) | copy-done | bytes 524312
  10.9 1.0 %copy-done.3 = bf16[64,16,256]{2,1,0:T(8,128)(2,1)S(1)} copy-done((bf16[64,16,256]{2,1,0:T(8,128)(2,1)S(1)}, bf16[64,16,256]{2,1,0:T(8,128)(2,1)}, u32[]{:S(2)}) %copy-start.3) | copy-done | bytes 524312
  12.0 2.8 %near_a.1.rest_0_ = f32[64,64,256]{2,1,0:T(8,128)S(1)} custom-call(s32[1]{0:T(128)} %bitcast.dev_ref, bf16[64,64,256]{2,1,0:T(8,128)(2,1)S(1)} %copy-done, bf16[64,64,256]{2,1,0:T(8,128)(2,1)S(1)} %copy-done, bf16[64,64,256]{2,1,0:T(8,128)(2,1)S(1)} %copy-done, bf16[64,16,256]{2,1,0:T(8,128)(2,1)S(1)} %copy-done.1, bf16[64,16,256]{2,1,0:T(8,128)(2,1)S(1)} %copy-done.3, ...), custom_call_target="tpu_custom_call" | custom-call | tf_op jit(solution)/shard_map/near_a/pallas_call | solution.py:410
  14.8 0.4 level_0.1.own
  15.2 3.4 %collective-permute-start.1 = (bf16[3,64,128]{2,1,0:T(8,128)(2,1)S(1)}, bf16[3,64,128]{2,1,0:T(8,128)(2,1)S(1)}, u32[]{:S(2)}, u32[]{:S(2)}) collective-permute-start(bf16[3,64,128]{2,1,0:T(8,128)(2,1)S(1)} %level_0.1.own), channel_id=1, source_target_pairs={{0,2},{1,3},{2,0},{3,1},{4,6},{5,7},{6,4},{7,5},{8,10},{9,11},{10,... | collective-permute-start | bytes 147464 | tf_op jit(solution)/shard_map/ppermute | solution.py:587
  18.6 2.8 %near_b.1.rest_2_ = f32[64,64,256]{2,1,0:T(8,128)S(1)} custom-call(s32[1]{0:T(128)} %bitcast.dev_ref, bf16[64,64,256]{2,1,0:T(8,128)(2,1)S(1)} %copy-done, bf16[64,64,256]{2,1,0:T(8,128)(2,1)S(1)} %copy-done, bf16[64,64,256]{2,1,0:T(8,128)(2,1)S(1)} %copy-done, bf16[64,16,256]{2,1,0:T(8,128)(2,1)S(1)} %copy-done.2, ...), custom_call_target="tpu_custom_call", output_to_operand_aliasing={{}: (8, {})} | custom-call | tf_op jit(solution)/shard_map/near_b/pallas_call | solution.py:410
  21.4 0.4 level_1.1.own
  21.9 3.2 %collective-permute-start.2 = (bf16[5,64,128]{2,1,0:T(8,128)(2,1)S(1)}, bf16[5,64,128]{2,1,0:T(8,128)(2,1)S(1)}, u32[]{:S(2)}, u32[]{:S(2)}) collective-permute-start(bf16[5,64,128]{2,1,0:T(8,128)(2,1)S(1)} %level_1.1.own), channel_id=1, source_target_pairs={{0,4},{1,5},{2,6},{3,7},{4,0},{5,1},{6,2},{7,3},{8,12},{9,13},{10,... | collective-permute-start | bytes 245768 | tf_op jit(solution)/shard_map/ppermute | solution.py:587
  25.1 2.8 %near_c.1.rest_2_ = f32[64,64,256]{2,1,0:T(8,128)S(1)} custom-call(s32[1]{0:T(128)} %bitcast.dev_ref, bf16[64,64,256]{2,1,0:T(8,128)(2,1)S(1)} %copy-done, bf16[64,64,256]{2,1,0:T(8,128)(2,1)S(1)} %copy-done, bf16[64,64,256]{2,1,0:T(8,128)(2,1)S(1)} %copy-done, bf16[64,16,256]{2,1,0:T(8,128)(2,1)S(1)} %copy-done.2, ...), custom_call_target="tpu_custom_call", output_to_operand_aliasing={{}: (10, {})} | custom-call | tf_op jit(solution)/shard_map/near_c/pallas_call | solution.py:410
  27.9 0.6 collective-permute-done.2.got.four_ref
  28.6 0.4 level_2.1
  29.0 0.0 slice-start
  29.0 0.0 copy-start.9
  29.1 0.0 copy-start.14
  29.1 0.0 copy-start.17
  29.1 3.0 %collective-permute-start.6 = (bf16[2,64,128]{2,1,0:T(8,128)(2,1)S(1)}, bf16[2,64,128]{2,1,0:T(8,128)(2,1)S(1)}, u32[]{:S(2)}, u32[]{:S(2)}) collective-permute-start(bf16[2,64,128]{2,1,0:T(8,128)(2,1)S(1)} %get-tuple-element.53.own), channel_id=1, source_target_pairs={{0,8},{1,9},{2,10},{3,11},{4,12},{5,13},{6,14},{7,15},{8,0},{9,1},... | collective-permute-start | bytes 98312 | tf_op jit(solution)/shard_map/ppermute | solution.py:587
  32.1 2.8 %near_d.1.sum_ref = f32[64,64,256]{2,1,0:T(8,128)S(1)} custom-call(s32[1]{0:T(128)} %bitcast.dev_ref, bf16[64,64,256]{2,1,0:T(8,128)(2,1)S(1)} %copy-done, bf16[64,64,256]{2,1,0:T(8,128)(2,1)S(1)} %copy-done, bf16[64,64,256]{2,1,0:T(8,128)(2,1)S(1)} %copy-done, bf16[64,16,256]{2,1,0:T(8,128)(2,1)S(1)} %copy-done.2, ...), custom_call_target="tpu_custom_call", output_to_operand_aliasing={{}: (10, {})} | custom-call | tf_op jit(solution)/shard_map/near_d/pallas_call | solution.py:410
  34.9 0.4 level_3.1.own
  35.3 3.3 %collective-permute-start.7 = (bf16[3,64,128]{2,1,0:T(8,128)(2,1)S(1)}, bf16[3,64,128]{2,1,0:T(8,128)(2,1)S(1)}, u32[]{:S(2)}, u32[]{:S(2)}) collective-permute-start(bf16[3,64,128]{2,1,0:T(8,128)(2,1)S(1)} %level_3.1.own), channel_id=1, source_target_pairs={{0,16},{1,17},{2,18},{3,19},{4,20},{5,21},{6,22},{7,23},{8,24},{9,... | collective-permute-start | bytes 147464 | tf_op jit(solution)/shard_map/ppermute | solution.py:587
  38.7 3.8 %couple.1 = (f32[64,64,64]{2,1,0:T(8,128)S(1)}, f32[8,64,64]{2,1,0:T(8,128)S(1)}) custom-call(s32[1]{0:T(128)} %bitcast.dev_ref, s32[8,64]{1,0:T(8,128)S(1)} %bitcast.6, s32[64]{0:T(128)S(1)} %copy-done.16, s32[4,8]{1,0:T(4,128)S(1)} %bitcast.7, s32[8]{0:T(128)S(1)} %copy-done.17, bf16[64,64,128]{2,1,0:T(8,128)(2,1)S(1)} %copy-done.7, ...), custom_call_target="tpu_custom_call" | custom-call | tf_op jit(solution)/shard_map/couple/pallas_call | solution.py:481
  42.5 0.2 level_4.1
  42.7 4.7 %collective-permute-start.10 = (bf16[3,64,128]{2,1,0:T(8,128)(2,1)S(1)}, bf16[3,64,128]{2,1,0:T(8,128)(2,1)S(1)}, u32[]{:S(2)}, u32[]{:S(2)}) collective-permute-start(bf16[3,64,128]{2,1,0:T(8,128)(2,1)S(1)} %get-tuple-element.64), channel_id=1, source_target_pairs={{0,96},{1,97},{2,98},{3,99},{4,100},{5,101},{6,102},{7,103},{8,104... | collective-permute-start | bytes 147464 | tf_op jit(solution)/shard_map/ppermute | solution.py:587
  47.4 2.5 %collective-permute-start.4 = (bf16[3,64,128]{2,1,0:T(8,128)(2,1)S(1)}, bf16[3,64,128]{2,1,0:T(8,128)(2,1)S(1)}, u32[]{:S(2)}, u32[]{:S(2)}) collective-permute-start(bf16[3,64,128]{2,1,0:T(8,128)(2,1)S(1)} %get-tuple-element.51), channel_id=1, source_target_pairs={{0,8},{1,9},{2,10},{3,11},{4,12},{5,13},{6,14},{7,15},{8,16},{9,17... | collective-permute-start | bytes 147464 | tf_op jit(solution)/shard_map/ppermute | solution.py:591
  50.0 1.3 %collective-permute-start.5 = (bf16[3,64,128]{2,1,0:T(8,128)(2,1)S(1)}, bf16[3,64,128]{2,1,0:T(8,128)(2,1)S(1)}, u32[]{:S(2)}, u32[]{:S(2)}) collective-permute-start(bf16[3,64,128]{2,1,0:T(8,128)(2,1)S(1)} %get-tuple-element.52), channel_id=1, source_target_pairs={{8,0},{9,1},{10,2},{11,3},{12,4},{13,5},{14,6},{15,7},{16,8},{17,9... | collective-permute-start | bytes 147464 | tf_op jit(solution)/shard_map/ppermute | solution.py:591
  51.3 3.4 %collective-permute-start.8 = (bf16[2,64,128]{2,1,0:T(8,128)(2,1)S(1)}, bf16[2,64,128]{2,1,0:T(8,128)(2,1)S(1)}, u32[]{:S(2)}, u32[]{:S(2)}) collective-permute-start(bf16[2,64,128]{2,1,0:T(8,128)(2,1)S(1)} %get-tuple-element.62), channel_id=1, source_target_pairs={{0,32},{1,33},{2,34},{3,35},{4,36},{5,37},{6,38},{7,39},{8,40},{9,... | collective-permute-start | bytes 98312 | tf_op jit(solution)/shard_map/ppermute | solution.py:587
  54.7 2.3 %collective-permute-start.9 = (bf16[1,64,128]{2,1,0:T(8,128)(2,1)S(1)}, bf16[1,64,128]{2,1,0:T(8,128)(2,1)S(1)}, u32[]{:S(2)}, u32[]{:S(2)}) collective-permute-start(bf16[1,64,128]{2,1,0:T(8,128)(2,1)S(1)} %get-tuple-element.63), channel_id=1, source_target_pairs={{0,64},{1,65},{2,66},{3,67},{4,68},{5,69},{6,70},{7,71},{8,72},{9,... | collective-permute-start | bytes 49160 | tf_op jit(solution)/shard_map/ppermute | solution.py:587
  57.0 0.2 prepare.1
  57.2 2.7 %collective-permute-done.9.across_ref = bf16[1,64,128]{2,1,0:T(8,128)(2,1)S(1)} collective-permute-done((bf16[1,64,128]{2,1,0:T(8,128)(2,1)S(1)}, bf16[1,64,128]{2,1,0:T(8,128)(2,1)S(1)}, u32[]{:S(2)}, u32[]{:S(2)}) %collective-permute-start.9) | collective-permute-done | bytes 16416 | tf_op jit(solution)/shard_map/ppermute | solution.py:587
  60.0 8.2 %downward.1 = bf16[64,64,256]{2,1,0:T(8,128)(2,1)} custom-call(s32[1]{0:T(128)} %bitcast.dev_ref, bf16[3,64,128]{2,1,0:T(8,128)(2,1)S(1)} %collective-permute-done.1.got.pair_ref, bf16[5,64,128]{2,1,0:T(8,128)(2,1)S(1)} %collective-permute-done.2.got.four_ref, bf16[3,64,128]{2,1,0:T(8,128)(2,1)S(1)} %collective-permute-done.4.before_ref, ...), custom_call_target="tpu_custom_call" | custom-call | tf_op jit(solution)/shard_map/downward/pallas_call | solution.py:562
  (44 shorter events, 0.1 us)
Async XLA Ops:
  0.0 9.9 %copy-start = (bf16[64,64,256]{2,1,0:T(8,128)(2,1)S(1)}, bf16[64,64,256]{2,1,0:T(8,128)(2,1)}, u32[]{:S(2)}) copy-start(bf16[64,64,256]{2,1,0:T(8,128)(2,1)} %rhs_after.7) | copy-start | bytes 6291460
  9.1 5.6 %collective-permute-start = (bf16[11,64,128]{2,1,0:T(8,128)(2,1)}, bf16[11,64,128]{2,1,0:T(8,128)(2,1)S(1)}, u32[]{:S(2)}, u32[]{:S(2)}) collective-permute-start(bf16[11,64,128]{2,1,0:T(8,128)(2,1)} %get-tuple-element.40.own), channel_id=1, source_target_pairs={{0,1},{1,0},{2,3},{3,2},{4,5},{5,4},{6,7},{7,6},{8,9},{9,8},{10,11... | collective-permute-start | bytes 540680 | tf_op jit(solution)/shard_map/ppermute | solution.py:587
  9.2 15.9 %collective-permute-start.3 = (bf16[9,64,128]{2,1,0:T(8,128)(2,1)}, bf16[9,64,128]{2,1,0:T(8,128)(2,1)S(1)}, u32[]{:S(2)}, u32[]{:S(2)}) collective-permute-start(bf16[9,64,128]{2,1,0:T(8,128)(2,1)} %get-tuple-element.47), channel_id=1, source_target_pairs={{1,2},{3,4},{5,6},{7,8},{9,10},{11,12},{13,14},{15,16},{17,18},{19... | collective-permute-start | bytes 442376 | tf_op jit(solution)/shard_map/ppermute | solution.py:597
  9.9 1.0 %copy-start.1 = (bf16[64,16,256]{2,1,0:T(8,128)(2,1)S(1)}, bf16[64,16,256]{2,1,0:T(8,128)(2,1)}, u32[]{:S(2)}) copy-start(bf16[64,16,256]{2,1,0:T(8,128)(2,1)} %get-tuple-element.41.source_ref.source_before) | copy-start | bytes 1572868
  10.9 1.0 %copy-start.3 = (bf16[64,16,256]{2,1,0:T(8,128)(2,1)S(1)}, bf16[64,16,256]{2,1,0:T(8,128)(2,1)}, u32[]{:S(2)}) copy-start(bf16[64,16,256]{2,1,0:T(8,128)(2,1)} %get-tuple-element.42.target_ref.target_after) | copy-start | bytes 1572868
  12.0 2.8 %copy-start.4 = (f32[1,5,64,64]{3,2,1,0:T(8,128)S(1)}, f32[1,5,64,64]{3,2,1,0:T(8,128)}, u32[]{:S(2)}) copy-start(f32[1,5,64,64]{3,2,1,0:T(8,128)} %up_top_ref.9) | copy-start | bytes 245764
  12.0 2.8 %copy-start.10 = (bf16[11,64,128]{2,1,0:T(8,128)(2,1)S(1)}, bf16[11,64,128]{2,1,0:T(8,128)(2,1)}, u32[]{:S(2)}) copy-start(bf16[11,64,128]{2,1,0:T(8,128)(2,1)} %get-tuple-element.40.own) | copy-start | bytes 540676
  12.0 6.7 %copy-start.2 = (bf16[64,16,256]{2,1,0:T(8,128)(2,1)S(1)}, bf16[64,16,256]{2,1,0:T(8,128)(2,1)}, u32[]{:S(2)}) copy-start(bf16[64,16,256]{2,1,0:T(8,128)(2,1)} %get-tuple-element.41.source_ref.source_before) | copy-start | bytes 1572868
  15.2 6.2 %collective-permute-start.1 = (bf16[3,64,128]{2,1,0:T(8,128)(2,1)S(1)}, bf16[3,64,128]{2,1,0:T(8,128)(2,1)S(1)}, u32[]{:S(2)}, u32[]{:S(2)}) collective-permute-start(bf16[3,64,128]{2,1,0:T(8,128)(2,1)S(1)} %level_0.1.own), channel_id=1, source_target_pairs={{0,2},{1,3},{2,0},{3,1},{4,6},{5,7},{6,4},{7,5},{8,10},{9,11},{10,... | collective-permute-start | bytes 147464 | tf_op jit(solution)/shard_map/ppermute | solution.py:587
  21.9 6.7 %collective-permute-start.2 = (bf16[5,64,128]{2,1,0:T(8,128)(2,1)S(1)}, bf16[5,64,128]{2,1,0:T(8,128)(2,1)S(1)}, u32[]{:S(2)}, u32[]{:S(2)}) collective-permute-start(bf16[5,64,128]{2,1,0:T(8,128)(2,1)S(1)} %level_1.1.own), channel_id=1, source_target_pairs={{0,4},{1,5},{2,6},{3,7},{4,0},{5,1},{6,2},{7,3},{8,12},{9,13},{10,... | collective-permute-start | bytes 245768 | tf_op jit(solution)/shard_map/ppermute | solution.py:587
  29.0 9.6 %slice-start = ((s8[8388608]{0:T(1024)(128)(4,1)}), s8[4194304]{0:T(1024)(128)(4,1)S(1)}, s32[]{:S(2)}) async-start(s8[8388608]{0:T(1024)(128)(4,1)} %bitcast.4), calls=%async_computation | async-start | bytes 8388608
  29.0 9.6 %slice-start.1 = ((s8[8388608]{0:T(1024)(128)(4,1)}), s8[4194304]{0:T(1024)(128)(4,1)S(1)}, s32[]{:S(2)}) async-start(s8[8388608]{0:T(1024)(128)(4,1)} %bitcast.4), calls=%async_computation.1 | async-start | bytes 8388608
  29.0 9.6 %copy-start.7 = (bf16[64,64,128]{2,1,0:T(8,128)(2,1)S(1)}, bf16[64,64,128]{2,1,0:T(8,128)(2,1)}, u32[]{:S(2)}) copy-start(bf16[64,64,128]{2,1,0:T(8,128)(2,1)} %get-tuple-element.58.leaf_ref) | copy-start | bytes 3145732
  29.0 9.6 %copy-start.9 = (bf16[8,4,64,64]{3,2,1,0:T(8,128)(2,1)S(1)}, bf16[8,4,64,64]{3,2,1,0:T(8,128)(2,1)}, u32[]{:S(2)}) copy-start(bf16[8,4,64,64]{3,2,1,0:T(8,128)(2,1)} %node_blocks_ref.1) | copy-start | bytes 786436
  29.0 9.6 %copy-start.13 = (bf16[8,64,128]{2,1,0:T(8,128)(2,1)S(1)}, bf16[8,64,128]{2,1,0:T(8,128)(2,1)}, u32[]{:S(2)}) copy-start(bf16[8,64,128]{2,1,0:T(8,128)(2,1)} %get-tuple-element.59.node_ref) | copy-start | bytes 393220
  29.1 9.6 %copy-start.14 = (s32[64,8]{0,1:T(8,128)S(1)}, s32[64,8]{0,1:T(8,128)}, u32[]{:S(2)}) copy-start(s32[64,8]{0,1:T(8,128)} %param.24) | copy-start | bytes 6148
  29.1 9.6 %copy-start.15 = (s32[8,4]{0,1:T(4,128)S(1)}, s32[8,4]{0,1:T(4,128)}, u32[]{:S(2)}) copy-start(s32[8,4]{0,1:T(4,128)} %param.29) | copy-start | bytes 388
  29.1 9.6 %copy-start.16 = (s32[64]{0:T(128)S(1)}, s32[64]{0:T(128)}, u32[]{:S(2)}) copy-start(s32[64]{0:T(128)} %count_ref.1) | copy-start | bytes 772
  29.1 9.6 %copy-start.17 = (s32[8]{0:T(128)S(1)}, s32[8]{0:T(128)}, u32[]{:S(2)}) copy-start(s32[8]{0:T(128)} %node_count_ref.1) | copy-start | bytes 100
  29.1 5.8 %collective-permute-start.6 = (bf16[2,64,128]{2,1,0:T(8,128)(2,1)S(1)}, bf16[2,64,128]{2,1,0:T(8,128)(2,1)S(1)}, u32[]{:S(2)}, u32[]{:S(2)}) collective-permute-start(bf16[2,64,128]{2,1,0:T(8,128)(2,1)S(1)} %get-tuple-element.53.own), channel_id=1, source_target_pairs={{0,8},{1,9},{2,10},{3,11},{4,12},{5,13},{6,14},{7,15},{8,0},{9,1},... | collective-permute-start | bytes 98312 | tf_op jit(solution)/shard_map/ppermute | solution.py:587
  35.3 7.2 %collective-permute-start.7 = (bf16[3,64,128]{2,1,0:T(8,128)(2,1)S(1)}, bf16[3,64,128]{2,1,0:T(8,128)(2,1)S(1)}, u32[]{:S(2)}, u32[]{:S(2)}) collective-permute-start(bf16[3,64,128]{2,1,0:T(8,128)(2,1)S(1)} %level_3.1.own), channel_id=1, source_target_pairs={{0,16},{1,17},{2,18},{3,19},{4,20},{5,21},{6,22},{7,23},{8,24},{9,... | collective-permute-start | bytes 147464 | tf_op jit(solution)/shard_map/ppermute | solution.py:587
  38.7 18.3 %copy-start.8 = (f32[1,6,4,64,64]{4,3,2,1,0:T(8,128)S(1)}, f32[1,6,4,64,64]{4,3,2,1,0:T(8,128)}, u32[]{:S(2)}) copy-start(f32[1,6,4,64,64]{4,3,2,1,0:T(8,128)} %couple_ref) | copy-start | bytes 1179652
  38.7 18.3 %copy-start.11 = (f32[1,5,64,64]{3,2,1,0:T(8,128)S(1)}, f32[1,5,64,64]{3,2,1,0:T(8,128)}, u32[]{:S(2)}) copy-start(f32[1,5,64,64]{3,2,1,0:T(8,128)} %down_ref.1) | copy-start | bytes 245764
  38.7 21.3 %copy-start.5 = (bf16[64,64,256]{2,1,0:T(8,128)(2,1)S(1)}, bf16[64,64,256]{2,1,0:T(8,128)(2,1)}, u32[]{:S(2)}) copy-start(bf16[64,64,256]{2,1,0:T(8,128)(2,1)} %bases_ref.3) | copy-start | bytes 6291460
  38.7 21.3 %copy-start.6 = (bf16[64,64,64]{2,1,0:T(8,128)(2,1)S(1)}, bf16[64,64,64]{2,1,0:T(8,128)(2,1)}, u32[]{:S(2)}) copy-start(bf16[64,64,64]{2,1,0:T(8,128)(2,1)} %transfer_ref.1) | copy-start | bytes 1572868
  38.7 21.3 %copy-start.12 = (bf16[8,64,64]{2,1,0:T(8,128)(2,1)S(1)}, bf16[8,64,64]{2,1,0:T(8,128)(2,1)}, u32[]{:S(2)}) copy-start(bf16[8,64,64]{2,1,0:T(8,128)(2,1)} %down_node_ref.1) | copy-start | bytes 196612
  42.7 17.2 %collective-permute-start.10 = (bf16[3,64,128]{2,1,0:T(8,128)(2,1)S(1)}, bf16[3,64,128]{2,1,0:T(8,128)(2,1)S(1)}, u32[]{:S(2)}, u32[]{:S(2)}) collective-permute-start(bf16[3,64,128]{2,1,0:T(8,128)(2,1)S(1)} %get-tuple-element.64), channel_id=1, source_target_pairs={{0,96},{1,97},{2,98},{3,99},{4,100},{5,101},{6,102},{7,103},{8,104... | collective-permute-start | bytes 147464 | tf_op jit(solution)/shard_map/ppermute | solution.py:587
  47.4 12.5 %collective-permute-start.4 = (bf16[3,64,128]{2,1,0:T(8,128)(2,1)S(1)}, bf16[3,64,128]{2,1,0:T(8,128)(2,1)S(1)}, u32[]{:S(2)}, u32[]{:S(2)}) collective-permute-start(bf16[3,64,128]{2,1,0:T(8,128)(2,1)S(1)} %get-tuple-element.51), channel_id=1, source_target_pairs={{0,8},{1,9},{2,10},{3,11},{4,12},{5,13},{6,14},{7,15},{8,16},{9,17... | collective-permute-start | bytes 147464 | tf_op jit(solution)/shard_map/ppermute | solution.py:591
  50.0 10.0 %collective-permute-start.5 = (bf16[3,64,128]{2,1,0:T(8,128)(2,1)S(1)}, bf16[3,64,128]{2,1,0:T(8,128)(2,1)S(1)}, u32[]{:S(2)}, u32[]{:S(2)}) collective-permute-start(bf16[3,64,128]{2,1,0:T(8,128)(2,1)S(1)} %get-tuple-element.52), channel_id=1, source_target_pairs={{8,0},{9,1},{10,2},{11,3},{12,4},{13,5},{14,6},{15,7},{16,8},{17,9... | collective-permute-start | bytes 147464 | tf_op jit(solution)/shard_map/ppermute | solution.py:591
  51.3 8.7 %collective-permute-start.8 = (bf16[2,64,128]{2,1,0:T(8,128)(2,1)S(1)}, bf16[2,64,128]{2,1,0:T(8,128)(2,1)S(1)}, u32[]{:S(2)}, u32[]{:S(2)}) collective-permute-start(bf16[2,64,128]{2,1,0:T(8,128)(2,1)S(1)} %get-tuple-element.62), channel_id=1, source_target_pairs={{0,32},{1,33},{2,34},{3,35},{4,36},{5,37},{6,38},{7,39},{8,40},{9,... | collective-permute-start | bytes 98312 | tf_op jit(solution)/shard_map/ppermute | solution.py:587
  54.7 5.2 %collective-permute-start.9 = (bf16[1,64,128]{2,1,0:T(8,128)(2,1)S(1)}, bf16[1,64,128]{2,1,0:T(8,128)(2,1)S(1)}, u32[]{:S(2)}, u32[]{:S(2)}) collective-permute-start(bf16[1,64,128]{2,1,0:T(8,128)(2,1)S(1)} %get-tuple-element.63), channel_id=1, source_target_pairs={{0,64},{1,65},{2,66},{3,67},{4,68},{5,69},{6,70},{7,71},{8,72},{9,... | collective-permute-start | bytes 49160 | tf_op jit(solution)/shard_map/ppermute | solution.py:587

commit v2 on v0

v2 whole, which is shorter than its diff:
```python
import functools

import jax
import jax.numpy as jnp
from jax import lax
from jax.experimental import pallas as pl
from jax.experimental.pallas import tpu as pltpu
from jax.sharding import PartitionSpec as P

bf16 = jnp.bfloat16
f32 = jnp.float32
core_square = 0.0004
W0 = 8
W1 = 4
LEAF_AT, NODE_AT, RHS_AT, COORD_AT, HALO_TILES = 0, 4, 6, 8, 9
CARRY_AT, COEFF_AT = 9, 10
CHUNKS = 4
PARTNERS = (2, 6, 8, 24, 32, 96)


def dot(a, b):
    return jnp.dot(a, b, preferred_element_type=f32)


def dot_rows(a, b):
    return lax.dot_general(a, b, (((1,), (1,)), ((), ())), preferred_element_type=f32)


def dot_columns(a, b):
    return lax.dot_general(a, b, (((0,), (0,)), ((), ())), preferred_element_type=f32)


def low_lanes(shape):
    return lax.broadcasted_iota(jnp.int32, shape, len(shape) - 1) < shape[-1] // 2


def join(low, high):
    return jnp.where(low_lanes(low.shape), low.astype(f32), high.astype(f32)).astype(bf16)


def twice(block):
    return jnp.concatenate([block, block], axis=1)


def split(wide):
    hi = wide.astype(bf16).astype(f32)
    return jnp.concatenate([hi, wide - hi], axis=1).astype(bf16)


def fused_halves(block):
    half = block.shape[1] // 2
    return block[:, :half] + block[:, half:]


def wide_dot(left, matrix_parts):
    weights = jnp.concatenate([matrix_parts, matrix_parts], axis=0)
    return fused_halves(dot(split(left), weights))


def call(body, out_shape, in_specs, out_specs, scratch=(), name=None, aliases=None, mib=24):
    return pl.pallas_call(
        body,
        out_shape=out_shape,
        in_specs=in_specs,
        out_specs=out_specs,
        scratch_shapes=list(scratch),
        input_output_aliases=aliases or {},
        compiler_params=pltpu.CompilerParams(vmem_limit_bytes=mib * 2**20),
        name=name,
    )


def held(*arrays):
    return [pl.BlockSpec(memory_space=pltpu.VMEM) for _ in arrays]


def stored(*arrays):
    return [pl.BlockSpec(memory_space=pltpu.HBM) for _ in arrays]


def scalars(count=1):
    return [pl.BlockSpec(memory_space=pltpu.SMEM)] * count


def shape(dims, dtype):
    return jax.ShapeDtypeStruct(dims, dtype)


def three_parts(value):
    hi = value.astype(bf16).astype(f32)
    mid = (value - hi).astype(bf16).astype(f32)
    return hi, mid, value - hi - mid


class Coordinates:
    def __init__(self, points, group):
        self.scaled = [points[j, group * 8 : group * 8 + 8, :].astype(f32) * 256.0 for j in range(3)]
        square = sum(x * x for x in self.scaled)
        self.parts = three_parts(square)
        self.plus_core = three_parts(square + core_square * 65536.0)

    def rows(self, b):
        row = lax.broadcasted_iota(jnp.int32, (16, self.scaled[0].shape[1]), 0)

        def stacked(values, ones_at):
            rows = jnp.where((row >= ones_at) & (row < ones_at + 3), 1.0, 0.0)
            for at, value in values:
                rows = jnp.where(row == at, value[b : b + 1], rows)
            return rows.astype(bf16)

        source = stacked(
            [(j, -2.0 * self.scaled[j]) for j in range(3)] + [(6 + j, self.plus_core[j]) for j in range(3)], 3
        )
        target = stacked(
            [(j, self.scaled[j]) for j in range(3)] + [(3 + j, self.parts[j]) for j in range(3)], 6
        )
        return source, target


def upward_body(
    dev_ref, rhs_ref, points_ref, bases_ref, up_leaf_ref, up_node_ref, up_top_ref,
    leaf_ref, node_ref, inner_ref, outer_ref,
    rhs, bases, up_leaf, points, up_node, up_top, sems, more_sems,
):
    groups = up_node_ref.shape[0]
    odd = lax.rem(dev_ref[0], 2) == 1

    leaves = rhs_ref.shape[0]
    chunk = leaves // CHUNKS

    def moves(c):
        at = pl.ds(c * chunk, chunk)
        return [
            pltpu.make_async_copy(rhs_ref.at[at], rhs.at[at], sems.at[0, c]),
            pltpu.make_async_copy(bases_ref.at[at], bases.at[at], sems.at[1, c]),
        ]

    others = [
        pltpu.make_async_copy(points_ref, points, more_sems.at[0]),
        pltpu.make_async_copy(up_node_ref, up_node, more_sems.at[1]),
        pltpu.make_async_copy(up_top_ref.at[0, 0], up_top, more_sems.at[2]),
        pltpu.make_async_copy(up_leaf_ref, up_leaf, more_sems.at[3]),
    ]
    others[0].start()
    for c in range(CHUNKS):
        for move in moves(c):
            move.start()
        if c == 0:
            others[3].start()
    others[1].start()
    others[2].start()
    for c in range(CHUNKS):
        for move in moves(c):
            move.wait()
        for leaf in range(c * chunk, (c + 1) * chunk):
            base = bases[leaf]
            leaf_ref[leaf] = dot_rows(rhs[leaf], jnp.concatenate([base, base], axis=0)).astype(bf16)

    others[3].wait()
    others[1].wait()
    nodes = []
    for g in range(groups):
        pairs = [join(leaf_ref[g * 8 + 2 * j], leaf_ref[g * 8 + 2 * j + 1]) for j in range(4)]
        up = up_leaf[g * 8 : g * 8 + 8].reshape(512, 64)
        nodes.append(twice(dot(jnp.concatenate(pairs, axis=1), up)).astype(bf16))
        node_ref[g] = nodes[g]
    pairs = [join(nodes[2 * j], nodes[2 * j + 1]) for j in range(groups // 2)]
    coeff = dot(jnp.concatenate(pairs, axis=1), up_node[...].reshape(groups * 64, 64))
    others[0].wait()
    others[2].wait()
    inner_ref[CARRY_AT] = split(wide_dot(coeff, split(up_top[...])))
    inner_ref[COEFF_AT] = twice(coeff).astype(bf16)

    def edge(message, first_leaf, leaf, first_node):
        for j in range(4):
            message[LEAF_AT + j] = join(leaf_ref[first_leaf + 2 * j], leaf_ref[first_leaf + 2 * j + 1])
        for j in range(2):
            message[NODE_AT + j] = join(node_ref[first_node + 2 * j], node_ref[first_node + 2 * j + 1])
        message[RHS_AT] = rhs[leaf, :, :128]
        message[RHS_AT + 1] = rhs[leaf, :, 128:]
        source, target = Coordinates(points, leaf // 8).rows(leaf % 8)
        message[COORD_AT, 0:16, :] = source[:, :128]
        message[COORD_AT, 16:32, :] = source[:, 128:]
        message[COORD_AT, 32:48, :] = target[:, :128]
        message[COORD_AT, 48:64, :] = target[:, 128:]

    @pl.when(odd)
    def _():
        edge(inner_ref, 0, 0, 0)
        edge(outer_ref, leaves - W0, leaves - 1, groups - W1)

    @pl.when(~odd)
    def _():
        edge(outer_ref, 0, 0, 0)
        edge(inner_ref, leaves - W0, leaves - 1, groups - W1)


def upward(dev, rhs, points, bases, up_leaf, up_node, up_top):
    leaves = rhs.shape[0]
    groups = up_node.shape[0]
    outs = [
        shape((leaves, 64, 128), bf16),
        shape((groups, 64, 128), bf16),
        shape((HALO_TILES + 2, 64, 128), bf16),
        shape((HALO_TILES, 64, 128), bf16),
    ]
    ins = [rhs, points, bases, up_leaf, up_node, up_top]
    return call(
        upward_body,
        outs,
        scalars() + stored(*ins),
        held(*outs),
        [
            pltpu.VMEM(rhs.shape, bf16),
            pltpu.VMEM(bases.shape, bf16),
            pltpu.VMEM(up_leaf.shape, bf16),
            pltpu.VMEM(points.shape, bf16),
            pltpu.VMEM(up_node.shape, bf16),
            pltpu.VMEM((64, 64), f32),
            pltpu.SemaphoreType.DMA((2, CHUNKS)),
            pltpu.SemaphoreType.DMA((4,)),
        ],
        name="upward",
        mib=56,
    )(dev, *ins)


def lowest(round_at):
    return 0 if round_at < 3 else 3


def fixed_tiles(round_at):
    return 2 if round_at < 5 else 6 - round_at


def first_at(height, round_at):
    if round_at == 6:
        return height - lowest(round_at)
    return fixed_tiles(round_at) + 2 * (height - lowest(round_at))


def last_at(height, round_at):
    if round_at == 6:
        return height - lowest(round_at)
    return fixed_tiles(round_at) + min(1 + 2 * (height - lowest(round_at)), 2 * (round_at - 1 - lowest(round_at)))


def tiles_of(round_at):
    heights = round_at - lowest(round_at)
    if round_at == 3:
        return fixed_tiles(round_at) + 3
    return fixed_tiles(round_at) + (heights if round_at == 6 else max(2 * heights - 1, 0))


def bit_of(dev_ref, height):
    return (dev_ref[0] >> height) & 1


def level_body(k, dev_ref, own, got, up_top_ref, out, *rest):
    hold = rest[-1]
    bit = bit_of(dev_ref, k)
    carry_at, coeff_at = (CARRY_AT, COEFF_AT) if k == 0 else (0, fixed_tiles(k) - 1)
    hold[bit, 0] = own[coeff_at]
    hold[1 - bit, 0] = got[coeff_at]
    pair = join(hold[0, 0], hold[1, 0])
    heights = range(lowest(k), k)
    for height in heights:
        hold[bit, 1 + height] = own[first_at(height, k)]
        hold[1 - bit, 1 + height] = got[first_at(height, k)]
        hold[bit, 7 + height] = own[last_at(height, k)]
        hold[1 - bit, 7 + height] = got[last_at(height, k)]
    if k < 5:
        parent = fused_halves(own[carry_at].astype(f32) + got[carry_at].astype(f32))
        if k < 4:
            out[0] = split(wide_dot(parent, split(up_top_ref[0, k + 1])))
        out[fixed_tiles(k + 1) - 1] = twice(parent).astype(bf16)
    if k == 2:
        side_out = rest[0]
        upper = bit_of(dev_ref, 3)
        for height in heights:
            hold[0, 7 + height] = hold[1, 7 + height]
            hold[1, 7 + height] = hold[0, 1 + height]
            out[fixed_tiles(3) + height] = hold[upper, 7 + height]
            side_out[height] = hold[1 - upper, 7 + height]
        out[fixed_tiles(3) + k] = pair
        side_out[k] = pair
    elif k < 5:
        for height in heights:
            out[first_at(height, k + 1)] = hold[0, 1 + height]
            out[last_at(height, k + 1)] = hold[1, 7 + height]
        out[first_at(k, k + 1)] = pair
    else:
        upper = bit_of(dev_ref, 6)
        for height in heights:
            hold[0, 7 + height] = hold[1, 7 + height]
            hold[1, 7 + height] = hold[0, 1 + height]
            out[first_at(height, 6)] = hold[upper, 7 + height]
        out[first_at(k, 6)] = pair


def level_call(k, dev, own, got, up_top):
    outs = [shape((tiles_of(k + 1), 64, 128), bf16)]
    if k == 2:
        outs += [shape((3, 64, 128), bf16)]
    ins = [own, got, up_top]
    return call(
        functools.partial(level_body, k),
        outs,
        scalars() + held(*ins),
        held(*outs),
        [pltpu.VMEM((2, 13, 64, 128), bf16)],
        name="level_%d" % k,
    )(dev, *ins)


def prepare_body(dev_ref, couple_ref, down_ref, couple_out, down_out):
    for height in range(6):
        odd = bit_of(dev_ref, height)
        even = 1 - odd
        picks = ((even, None), (1, odd), (2, even), (2 + even, None))
        for at, (slot, live) in enumerate(picks):
            matrix = couple_ref[0, height, slot]
            if live is not None:
                matrix = jnp.where(jnp.full(matrix.shape, live, jnp.int32) > 0, matrix, 0.0)
            couple_out[height, 64 * at : 64 * at + 64, :] = split(matrix)
    for height in range(5):
        down_out[height] = split(down_ref[0, height])


def prepare(dev, couple_top, down_top):
    outs = [shape((6, 256, 128), bf16), shape((5, 64, 128), bf16)]
    return call(
        prepare_body,
        outs,
        scalars() + held(couple_top, down_top),
        held(*outs),
        name="prepare",
    )(dev, couple_top, down_top)


def sides(dev_ref):
    odd = bit_of(dev_ref, 0)
    return 1 - odd, odd


def near_body(first, count, edges, devices, dev_ref, rhs_ref, points_ref, *rest):
    out_ref, kernels, rim_rhs, rim_source, rim_target = rest[-5:]
    leaves = rhs_ref.shape[0]

    def kernel_of(source, target):
        return lax.rsqrt(dot_columns(source, target)).astype(bf16)

    known = {}

    def rows(s):
        if s not in known:
            if s // 8 not in known.setdefault("groups", {}):
                known["groups"][s // 8] = Coordinates(points_ref, s // 8)
            known[s] = known["groups"][s // 8].rows(s % 8)
        return known[s]

    def build(s):
        source, target = rows(s)
        if s + 1 < leaves:
            targets = jnp.concatenate([target, rows(s + 1)[1]], axis=1)
            kernels[s % 2] = kernel_of(source, targets)
        else:
            kernels[s % 2, :, :256] = kernel_of(source, target)

    if edges:
        inner_ref, outer_ref = rest[:2]
        inner_at, outer_at = sides(dev_ref)
        rim_rhs[...] = jnp.zeros(rim_rhs.shape, bf16)
        rim_source[...] = rows(0)[0]
        rim_target[...] = rows(leaves - 1)[1]
        for halo, side in ((inner_ref, inner_at), (outer_ref, outer_at)):

            @pl.when((side == 0) & (dev_ref[0] > 0))
            def _():
                rim_rhs[0, :, :128] = halo[RHS_AT]
                rim_rhs[0, :, 128:] = halo[RHS_AT + 1]
                rim_source[:, :128] = halo[COORD_AT, 0:16, :]
                rim_source[:, 128:] = halo[COORD_AT, 16:32, :]

            @pl.when((side == 1) & (dev_ref[0] < devices - 1))
            def _():
                rim_rhs[1, :, :128] = halo[RHS_AT]
                rim_rhs[1, :, 128:] = halo[RHS_AT + 1]
                rim_target[:, :128] = halo[COORD_AT, 32:48, :]
                rim_target[:, 128:] = halo[COORD_AT, 48:64, :]

    build(first)
    for s in range(first, first + count):
        if s + 1 < first + count:
            build(s + 1)
        kernel = kernels[s % 2]
        own = dot(rhs_ref[s], kernel[:, :256])
        if s + 1 < leaves:
            own += dot_rows(rhs_ref[s + 1], kernel[:, 256:])
            out_ref[s + 1] = dot(rhs_ref[s], kernel[:, 256:])
        out_ref[s] = own if s == 0 else out_ref[s] + own

    if edges:
        before = kernel_of(rim_source[...], rows(0)[1])
        after = kernel_of(rows(leaves - 1)[0], rim_target[...])
        out_ref[0] += dot(rim_rhs[0], before)
        out_ref[leaves - 1] += dot_rows(rim_rhs[1], after)


def near(dev, rhs, points, first, count, halos, total):
    args = [rhs, points] + halos
    out = shape(rhs.shape, f32)
    aliases = {}
    if total is not None:
        aliases = {len(args) + 1: 0}
        args.append(total)
    return call(
        functools.partial(near_body, first, count, len(halos) > 0, lax.axis_size("leaf")),
        out,
        scalars() + held(*args),
        held(out)[0],
        [
            pltpu.VMEM((2, 256, 512), bf16),
            pltpu.VMEM((2, 64, 256), bf16),
            pltpu.VMEM((16, 256), bf16),
            pltpu.VMEM((16, 256), bf16),
        ],
        name="near_%d" % first,
        aliases=aliases,
    )(dev, *args)


def couple_body(
    dev_ref, list_ref, count_ref, node_list_ref, node_count_ref, leaf_ref, node_ref, inner_ref,
    outer_ref, blocks_ref, node_blocks_ref, gain_ref, node_gain_ref, leaf_hold, node_hold,
):
    leaves = leaf_ref.shape[0]
    groups = node_ref.shape[0]
    low = low_lanes((64, 128))

    def keep(hold, at, doubled):
        doubled = doubled.astype(f32)
        hold[0, at] = jnp.where(low, doubled, 0.0).astype(bf16)
        hold[1, at] = jnp.where(low, 0.0, doubled).astype(bf16)

    for leaf in range(leaves):
        keep(leaf_hold, W0 + leaf, leaf_ref[leaf])
    for node in range(groups):
        keep(node_hold, W1 + node, node_ref[node])
    nothing = jnp.zeros((64, 128), f32)
    keep(leaf_hold, leaves + 2 * W0, nothing)
    keep(node_hold, groups + 2 * W1, nothing)
    inner_side, outer_side = sides(dev_ref)
    for halo, side in ((inner_ref, inner_side), (outer_ref, outer_side)):

        def unpack(hold, at, tile):
            pair = halo[tile].astype(f32)
            turned = pltpu.roll(pair, 64, 1)
            keep(hold, at, jnp.where(low, pair, turned))
            keep(hold, at + 1, jnp.where(low, turned, pair))

        for j in range(4):
            unpack(leaf_hold, side * (leaves + W0) + 2 * j, LEAF_AT + j)
        for j in range(2):
            unpack(node_hold, side * (groups + W1) + 2 * j, NODE_AT + j)

    def picked(hold, lists, counts, row, first, slots, nothing):
        count = counts[row]
        at = [jnp.where(k < count, lists[k, row] - first, nothing) for k in range(slots)]
        return jnp.concatenate(
            [hold[0, at[2 * j]] + hold[1, at[2 * j + 1]] for j in range(slots // 2)], axis=1
        )

    def group(g, _):
        for b in range(8):
            row = g * 8 + b
            values = picked(
                leaf_hold, list_ref, count_ref, row, dev_ref[0] * leaves - W0, 8, leaves + 2 * W0
            )
            gain_ref[row] = dot(values, blocks_ref[row].reshape(512, 64))
        values = picked(
            node_hold, node_list_ref, node_count_ref, g, dev_ref[0] * groups - W1, 4, groups + 2 * W1
        )
        node_gain_ref[g] = dot(values, node_blocks_ref[g].reshape(256, 64))
        return 0

    for g in range(groups):
        group(g, 0)


def couple(dev, lists, counts, node_lists, node_counts, leaf, node, inner, outer, blocks, node_blocks):
    leaves, groups = leaf.shape[0], node.shape[0]
    outs = [shape((leaves, 64, 64), f32), shape((groups, 64, 64), f32)]
    ins = [leaf, node, inner, outer, blocks, node_blocks]
    return call(
        couple_body,
        outs,
        scalars(5) + held(*ins),
        held(*outs),
        [
            pltpu.VMEM((2, leaves + 2 * W0 + 1, 64, 128), bf16),
            pltpu.VMEM((2, groups + 2 * W1 + 1, 64, 128), bf16),
        ],
        name="couple",
    )(dev, lists, counts, node_lists, node_counts, *ins)


def downward_body(
    devices, dev_ref, side_ref, got_1, got_2, got_3, got_4, got_5, got_6, couple_ref, down_ref,
    down_node_ref, node_gain_ref, gain_ref, transfer_ref, bases_ref, sum_ref, out_ref, bank, out, sems,
):
    d = dev_ref[0]
    bank[0] = jnp.zeros((64, 128), bf16)
    for height in range(3):
        upper = bit_of(dev_ref, 3)
        bank[4 - 3 * upper + height] = got_3[fixed_tiles(3) + height]
        bank[1 + 3 * upper + height] = side_ref[height]
    start = {}
    at = 7
    for k, got in ((1, got_1), (2, got_2), (4, got_4), (5, got_5), (6, got_6)):
        start[k] = at - fixed_tiles(k)
        for tile in range(fixed_tiles(k), got.shape[0]):
            bank[at] = got[tile]
            at += 1
    gains = []
    for height in range(6):
        own = d >> (height + 1)
        left = right = 0
        if height < 3:
            left = jnp.where(d >= 8, 1 + height, 0)
            right = jnp.where(d < devices - 8, 4 + height, 0)
        for k in range(2 if height < 3 else 6, height, -1):
            bit = (own >> (k - height - 1)) & 1
            left = jnp.where(bit == 1, start[k] + last_at(height, k), left)
            right = jnp.where(bit == 0, start[k] + first_at(height, k), right)
        tiles = jnp.concatenate([bank[left], bank[right]], axis=1)
        gains.append(fused_halves(dot(tiles, couple_ref[height])))
    value = gains[5]
    for height in range(4, -1, -1):
        value = gains[height] + wide_dot(value, down_ref[height])
    rounded = value.astype(bf16)
    groups = down_node_ref.shape[0]

    def move(g):
        at = pl.ds(g * 8, 8)
        return pltpu.make_async_copy(out.at[at], out_ref.at[at], sems.at[g])

    node_values = [(node_gain_ref[g] + dot(rounded, down_node_ref[g])).astype(bf16) for g in range(groups)]
    for g in range(groups):
        bank[g, :, :64] = node_values[g]

    def group(g, _):
        node_value = bank[g, :, :64]
        leaf_values = [
            (gain_ref[g * 8 + b] + dot(node_value, transfer_ref[g * 8 + b])).astype(bf16) for b in range(8)
        ]
        for b in range(8):
            leaf = g * 8 + b
            out[leaf] = (sum_ref[leaf] + dot(leaf_values[b], bases_ref[leaf])).astype(bf16)
        move(g).start()
        return 0

    for g in range(groups):
        group(g, 0)
    for g in range(groups):
        move(g).wait()


def downward(dev, received, couple_parts, down_parts, down_node, node_gain, gain, transfer, bases, near_sum):
    ins = list(received) + [couple_parts, down_parts, down_node, node_gain, gain, transfer, bases, near_sum]
    out = shape(bases.shape, bf16)
    return call(
        functools.partial(downward_body, lax.axis_size("leaf")),
        out,
        scalars() + held(*ins),
        stored(out)[0],
        [
            pltpu.VMEM((7 + sum(tiles_of(k) - fixed_tiles(k) for k in range(1, 7)), 64, 128), bf16),
            pltpu.VMEM(out.shape, bf16),
            pltpu.SemaphoreType.DMA((down_node.shape[0],)),
        ],
        name="downward",
    )(dev, *ins)


def tied(*values):
    return lax.optimization_barrier(values)


def shards(
    rhs, points, upward_leaf_bases, downward_leaf_bases, up_leaf, leaf_down_transfer, couple_leaf,
    list_leaf, count_leaf, up_node, down_node, couple_node, list_node, count_node, up_top, down_top,
    couple_top,
):
    device = lax.axis_index("leaf")
    devices = lax.axis_size("leaf")
    dev = device.astype(jnp.int32).reshape(1)

    def beside(block, size):
        def partner(i):
            other = i + size if i // size % 2 == 1 else i - size
            return other if 0 <= other < devices else i

        return lax.ppermute(block, "leaf", [(i, partner(i)) for i in range(devices)])

    def exchange(block, mask):
        return lax.ppermute(block, "leaf", [(i, i ^ mask) for i in range(devices)])

    points = jnp.transpose(points, (1, 0, 2))
    leaf, node, inner_out, outer_out = upward(
        dev, rhs, points, upward_leaf_bases, up_leaf, up_node, up_top
    )
    inner = exchange(inner_out, 1)
    outer = beside(outer_out, 1)
    near_sum = near(dev, rhs, points, 0, parts[0], [], None)
    done = parts[0]
    own, got = inner_out, inner
    received = []
    for k in range(6):
        if k == 1:
            got, outer, near_sum = tied(got, outer, near_sum)
        else:
            got, near_sum = tied(got, near_sum)
        own, *edges = level_call(k, dev, own, got, up_top)
        got = exchange(own, PARTNERS[k])
        if k == 2:
            side = beside(edges[0], 8)
        received.append(got)
        near_sum, leaf, own = tied(near_sum, leaf, own)
        if k < 5:
            near_sum = near(
                dev, rhs, points, done, parts[k + 1], [inner, outer] if k == 4 else [], near_sum
            )
            done += parts[k + 1]
        if k == 3:
            side, near_sum = tied(side, near_sum)
    gain, node_gain = couple(
        dev, list_leaf.T, count_leaf, list_node.T, count_node, leaf, node, inner, outer,
        couple_leaf, couple_node,
    )
    couple_top, _ = tied(couple_top, own)
    couple_parts, down_parts = prepare(dev, couple_top, down_top)
    received[5], gain, couple_parts = tied(received[5], gain, couple_parts)
    return downward(
        dev, [side] + received, couple_parts, down_parts,
        down_node, node_gain, gain, leaf_down_transfer, downward_leaf_bases, near_sum,
    )


parts = (10, 12, 14, 8, 10, 10)


def solution(mesh):
    placed = tuple(P("leaf") for _ in range(17))
    return jax.shard_map(
        shards, mesh=mesh, in_specs=placed, out_specs=P("leaf"), check_vma=False
    )
```

time: 323 us -> 52.6 us (0.16)
  the two profiles are of different devices: /device:TPU:95 before, /device:TPU:0 now
where the time goes in v2:
time: 52.6 us; the launch traced here: 52.4 us
  Pallas kernels  25.6 us (49%)
  starting transfers between devices  24.7 us (47%)
  waiting for transfers between devices  1.49 us (3%)
  between operations  0.54 us (1%)
    ppermute x7, starting transfers between devices, exchange(): return lax.ppermute(block, 'leaf', [(i, i ^ mask) for i in range(devices)])  22.4 us
    pallas_call x6, Pallas kernels, near(): call(functools.partial(near_body, first, count, len(halos) > 0, lax.axis_...  10.9 us
    pallas_call x1, Pallas kernels, upward(): call(upward_body, outs, scalars() + stored(*ins), held(*outs), [pltpu.VME...  5.43 us
    pallas_call x1, Pallas kernels, downward(): call(functools.partial(downward_body, lax.axis_size('leaf')), out, scalar...  4.22 us
    pallas_call x1, Pallas kernels, couple(): call(couple_body, outs, scalars(5) + held(*ins), held(*outs), [pltpu.VMEM...  2.87 us
    ppermute x2, starting transfers between devices, beside(): lax.ppermute(block, 'leaf', [(i, partner(i)) for i in range(devices)])  2.36 us
    pallas_call x6, Pallas kernels, level_call(): call(functools.partial(level_body, k), outs, scalars() + held(*ins), held...  1.85 us
    ppermute x7, waiting for transfers between devices, exchange(): return lax.ppermute(block, 'leaf', [(i, i ^ mask) for i in range(devices)])  1.49 us
  transfers between devices with their start and end apart: 9, of which 5 were waited for; matrix products, arithmetic and copies ran while one was open for 0% of the time, Pallas kernels for 28%

profile of v2, /device:TPU:0, one launch (start us, length us, event | category | flops | bytes accessed | tf_op | source)
XLA Modules:
  0.0 52.4 jit_solution(17117809393585701483)
XLA Ops:
  0.0 5.4 %upward.1 = (bf16[64,64,128]{2,1,0:T(8,128)(2,1)}, bf16[8,64,128]{2,1,0:T(8,128)(2,1)}, bf16[11,64,128]{2,1,0:T(8,128)(2,1)}, bf16[9,64,128]{2,1,0:T(8,128)(2,1)}) custom-call(s32[1]{0:T(128)} %bitcast.dev_ref, bf16[64,64,256]{2,1,0:T(8,128)(2,1)} %rhs_ref.13, bf16[3,64,256]{2,1,0:T(8,128)(2,1)} %bitcast.6, bf16[64,64,256]{2,1,0:T(8,128)(2,1)} %bases_ref.2, ...), custom_call_target="tpu_custom_call" | custom-call | tf_op jit(solution)/shard_map/upward/pallas_call | solution.py:208
  5.4 0.0 copy-start.1
  5.5 0.1 collective-permute-start
  5.6 1.7 %collective-permute-start.2 = (bf16[9,64,128]{2,1,0:T(8,128)(2,1)}, bf16[9,64,128]{2,1,0:T(8,128)(2,1)S(1)}, u32[]{:S(2)}, u32[]{:S(2)}) collective-permute-start(bf16[9,64,128]{2,1,0:T(8,128)(2,1)} %get-tuple-element.52), channel_id=1, source_target_pairs={{0,0},{1,2},{2,1},{3,4},{4,3},{5,6},{6,5},{7,8},{8,7},{9,10},{10,9... | collective-permute-start | bytes 442376 | tf_op jit(solution)/shard_map/ppermute | solution.py:604
  7.3 1.7 %near_0.1.rest_0_ = f32[64,64,256]{2,1,0:T(8,128)S(1)} custom-call(s32[1]{0:T(128)} %bitcast.dev_ref, bf16[64,64,256]{2,1,0:T(8,128)(2,1)S(1)} %copy-done, bf16[3,64,256]{2,1,0:T(8,128)(2,1)S(1)} %bitcast.7), custom_call_target="tpu_custom_call" | custom-call | tf_op jit(solution)/shard_map/near_0/pallas_call | solution.py:417
  9.0 0.4 level_0.1.own
  9.4 2.4 %collective-permute-start.1 = (bf16[3,64,128]{2,1,0:T(8,128)(2,1)S(1)}, bf16[3,64,128]{2,1,0:T(8,128)(2,1)S(1)}, u32[]{:S(2)}, u32[]{:S(2)}) collective-permute-start(bf16[3,64,128]{2,1,0:T(8,128)(2,1)S(1)} %level_0.1.own), channel_id=1, source_target_pairs={{0,2},{1,3},{2,0},{3,1},{4,6},{5,7},{6,4},{7,5},{8,10},{9,11},{10,... | collective-permute-start | bytes 147464 | tf_op jit(solution)/shard_map/ppermute | solution.py:607
  11.8 1.9 %near_10.1.rest_0_ = f32[64,64,256]{2,1,0:T(8,128)S(1)} custom-call(s32[1]{0:T(128)} %bitcast.dev_ref, bf16[64,64,256]{2,1,0:T(8,128)(2,1)S(1)} %copy-done, bf16[3,64,256]{2,1,0:T(8,128)(2,1)S(1)} %bitcast.8, f32[64,64,256]{2,1,0:T(8,128)S(1)} %near_0.1.rest_0_), custom_call_target="tpu_custom_call", output_to_operand_aliasing={{}: (3, {})} | custom-call | tf_op jit(solution)/shard_map/near_10/pallas_call | solution.py:417
  13.7 0.1 collective-permute-done.1.got.got_1
  13.9 0.4 level_1.1.own
  14.3 4.1 %collective-permute-start.3 = (bf16[5,64,128]{2,1,0:T(8,128)(2,1)S(1)}, bf16[5,64,128]{2,1,0:T(8,128)(2,1)S(1)}, u32[]{:S(2)}, u32[]{:S(2)}) collective-permute-start(bf16[5,64,128]{2,1,0:T(8,128)(2,1)S(1)} %level_1.1.own), channel_id=1, source_target_pairs={{0,6},{1,7},{2,4},{3,5},{4,2},{5,3},{6,0},{7,1},{8,14},{9,15},{10,... | collective-permute-start | bytes 245768 | tf_op jit(solution)/shard_map/ppermute | solution.py:607
  18.4 2.2 %near_22.1.rest_0_ = f32[64,64,256]{2,1,0:T(8,128)S(1)} custom-call(s32[1]{0:T(128)} %bitcast.dev_ref, bf16[64,64,256]{2,1,0:T(8,128)(2,1)S(1)} %copy-done, bf16[3,64,256]{2,1,0:T(8,128)(2,1)S(1)} %bitcast.9, f32[64,64,256]{2,1,0:T(8,128)S(1)} %near_10.1.rest_0_), custom_call_target="tpu_custom_call", output_to_operand_aliasing={{}: (3, {})} | custom-call | tf_op jit(solution)/shard_map/near_22/pallas_call | solution.py:417
  20.6 0.4 collective-permute-done.3.got.got_2
  21.0 0.4 level_2.1
  21.4 3.4 %collective-permute-start.5 = (bf16[5,64,128]{2,1,0:T(8,128)(2,1)S(1)}, bf16[5,64,128]{2,1,0:T(8,128)(2,1)S(1)}, u32[]{:S(2)}, u32[]{:S(2)}) collective-permute-start(bf16[5,64,128]{2,1,0:T(8,128)(2,1)S(1)} %get-tuple-element.70.own), channel_id=1, source_target_pairs={{0,8},{1,9},{2,10},{3,11},{4,12},{5,13},{6,14},{7,15},{8,0},{9,1},... | collective-permute-start | bytes 245768 | tf_op jit(solution)/shard_map/ppermute | solution.py:607
  24.8 1.4 %near_36.1.rest_0_ = f32[64,64,256]{2,1,0:T(8,128)S(1)} custom-call(s32[1]{0:T(128)} %bitcast.dev_ref, bf16[64,64,256]{2,1,0:T(8,128)(2,1)S(1)} %copy-done, bf16[3,64,256]{2,1,0:T(8,128)(2,1)S(1)} %bitcast.10, f32[64,64,256]{2,1,0:T(8,128)S(1)} %near_22.1.rest_0_), custom_call_target="tpu_custom_call", output_to_operand_aliasing={{}: (3, {})} | custom-call | tf_op jit(solution)/shard_map/near_36/pallas_call | solution.py:417
  26.2 0.7 %collective-permute-start.4 = (bf16[3,64,128]{2,1,0:T(8,128)(2,1)S(1)}, bf16[3,64,128]{2,1,0:T(8,128)(2,1)S(1)}, u32[]{:S(2)}, u32[]{:S(2)}) collective-permute-start(bf16[3,64,128]{2,1,0:T(8,128)(2,1)S(1)} %get-tuple-element.63), channel_id=1, source_target_pairs={{0,0},{1,1},{2,2},{3,3},{4,4},{5,5},{6,6},{7,7},{8,16},{9,17},{10,... | collective-permute-start | bytes 147464 | tf_op jit(solution)/shard_map/ppermute | solution.py:604
  26.9 0.3 collective-permute-done.5.got.got_3
  27.3 0.4 level_3.1.own
  27.7 6.1 %collective-permute-start.6 = (bf16[3,64,128]{2,1,0:T(8,128)(2,1)S(1)}, bf16[3,64,128]{2,1,0:T(8,128)(2,1)S(1)}, u32[]{:S(2)}, u32[]{:S(2)}) collective-permute-start(bf16[3,64,128]{2,1,0:T(8,128)(2,1)S(1)} %level_3.1.own), channel_id=1, source_target_pairs={{0,24},{1,25},{2,26},{3,27},{4,28},{5,29},{6,30},{7,31},{8,16},{9,... | collective-permute-start | bytes 147464 | tf_op jit(solution)/shard_map/ppermute | solution.py:607
  33.8 1.7 %near_44.1.rest_2_ = f32[64,64,256]{2,1,0:T(8,128)S(1)} custom-call(s32[1]{0:T(128)} %bitcast.dev_ref, bf16[64,64,256]{2,1,0:T(8,128)(2,1)S(1)} %copy-done, bf16[3,64,256]{2,1,0:T(8,128)(2,1)S(1)} %bitcast.11, f32[64,64,256]{2,1,0:T(8,128)S(1)} %near_36.1.rest_0_), custom_call_target="tpu_custom_call", output_to_operand_aliasing={{}: (3, {})} | custom-call | tf_op jit(solution)/shard_map/near_44/pallas_call | solution.py:417
  35.5 0.4 collective-permute-done.6.got.got_4
  35.9 0.2 level_4.1.own
  36.0 0.0 slice-start.1
  36.1 0.0 copy-start.7
  36.1 2.0 %collective-permute-start.7 = (bf16[4,64,128]{2,1,0:T(8,128)(2,1)S(1)}, bf16[4,64,128]{2,1,0:T(8,128)(2,1)S(1)}, u32[]{:S(2)}, u32[]{:S(2)}) collective-permute-start(bf16[4,64,128]{2,1,0:T(8,128)(2,1)S(1)} %level_4.1.own), channel_id=1, source_target_pairs={{0,32},{1,33},{2,34},{3,35},{4,36},{5,37},{6,38},{7,39},{8,40},{9,... | collective-permute-start | bytes 196616 | tf_op jit(solution)/shard_map/ppermute | solution.py:607
  38.1 2.1 %near_54.1.sum_ref = f32[64,64,256]{2,1,0:T(8,128)S(1)} custom-call(s32[1]{0:T(128)} %bitcast.dev_ref, bf16[64,64,256]{2,1,0:T(8,128)(2,1)S(1)} %copy-done, bf16[3,64,256]{2,1,0:T(8,128)(2,1)S(1)} %bitcast.12, bf16[11,64,128]{2,1,0:T(8,128)(2,1)S(1)} %collective-permute-done.got.rest_0_.inner_ref, ...), custom_call_target="tpu_custom_call", output_to_operand_aliasing={{}: (5, {})} | custom-call | tf_op jit(solution)/shard_map/near_54/pallas_call | solution.py:417
  40.3 0.2 collective-permute-done.7.got.got_5
  40.5 4.2 %collective-permute-start.8 = (bf16[3,64,128]{2,1,0:T(8,128)(2,1)S(1)}, bf16[3,64,128]{2,1,0:T(8,128)(2,1)S(1)}, u32[]{:S(2)}, u32[]{:S(2)}) collective-permute-start(bf16[3,64,128]{2,1,0:T(8,128)(2,1)S(1)} %level_5.1), channel_id=1, source_target_pairs={{0,96},{1,97},{2,98},{3,99},{4,100},{5,101},{6,102},{7,103},{8,104... | collective-permute-start | bytes 147464 | tf_op jit(solution)/shard_map/ppermute | solution.py:607
  44.7 0.2 prepare.1
  45.1 2.9 %couple.1 = (f32[64,64,64]{2,1,0:T(8,128)S(1)}, f32[8,64,64]{2,1,0:T(8,128)S(1)}) custom-call(s32[1]{0:T(128)} %bitcast.dev_ref, s32[8,64]{1,0:T(8,128)S(1)} %bitcast.13, s32[64]{0:T(128)S(1)} %copy-done.14, s32[4,8]{1,0:T(4,128)S(1)} %bitcast.14, s32[8]{0:T(128)S(1)} %copy-done.15, bf16[64,64,128]{2,1,0:T(8,128)(2,1)S(1)} %copy-done.5, ...), custom_call_target="tpu_custom_call" | custom-call | tf_op jit(solution)/shard_map/couple/pallas_call | solution.py:495
  48.0 4.2 %downward.1 = bf16[64,64,256]{2,1,0:T(8,128)(2,1)} custom-call(s32[1]{0:T(128)} %bitcast.dev_ref, bf16[3,64,128]{2,1,0:T(8,128)(2,1)S(1)} %collective-permute-done.4.side_ref, bf16[3,64,128]{2,1,0:T(8,128)(2,1)S(1)} %collective-permute-done.1.got.got_1, bf16[5,64,128]{2,1,0:T(8,128)(2,1)S(1)} %collective-permute-done.3.got.got_2, ...), custom_call_target="tpu_custom_call" | custom-call | tf_op jit(solution)/shard_map/downward/pallas_call | solution.py:572
  (39 shorter events, 0.1 us)
Async XLA Ops:
  0.0 7.3 %copy-start.2 = (bf16[64,3,256]{2,0,1:T(8,128)(2,1)S(1)}, bf16[64,3,256]{2,0,1:T(8,128)(2,1)}, u32[]{:S(2)}) copy-start(bf16[64,3,256]{2,0,1:T(8,128)(2,1)} %param.18) | copy-start | bytes 294916
  0.0 7.3 %copy-start = (bf16[64,64,256]{2,1,0:T(8,128)(2,1)S(1)}, bf16[64,64,256]{2,1,0:T(8,128)(2,1)}, u32[]{:S(2)}) copy-start(bf16[64,64,256]{2,1,0:T(8,128)(2,1)} %rhs_ref.13) | copy-start | bytes 6291460
  5.4 3.5 %copy-start.1 = (f32[1,5,64,64]{3,2,1,0:T(8,128)S(1)}, f32[1,5,64,64]{3,2,1,0:T(8,128)}, u32[]{:S(2)}) copy-start(f32[1,5,64,64]{3,2,1,0:T(8,128)} %up_top_ref.13) | copy-start | bytes 245764
  5.5 3.5 %copy-start.8 = (bf16[11,64,128]{2,1,0:T(8,128)(2,1)S(1)}, bf16[11,64,128]{2,1,0:T(8,128)(2,1)}, u32[]{:S(2)}) copy-start(bf16[11,64,128]{2,1,0:T(8,128)(2,1)} %get-tuple-element.50.own) | copy-start | bytes 540676
  5.5 3.5 %collective-permute-start = (bf16[11,64,128]{2,1,0:T(8,128)(2,1)}, bf16[11,64,128]{2,1,0:T(8,128)(2,1)S(1)}, u32[]{:S(2)}, u32[]{:S(2)}) collective-permute-start(bf16[11,64,128]{2,1,0:T(8,128)(2,1)} %get-tuple-element.50.own), channel_id=1, source_target_pairs={{0,1},{1,0},{2,3},{3,2},{4,5},{5,4},{6,7},{7,6},{8,9},{9,8},{10,11... | collective-permute-start | bytes 540680 | tf_op jit(solution)/shard_map/ppermute | solution.py:607
  5.6 8.2 %collective-permute-start.2 = (bf16[9,64,128]{2,1,0:T(8,128)(2,1)}, bf16[9,64,128]{2,1,0:T(8,128)(2,1)S(1)}, u32[]{:S(2)}, u32[]{:S(2)}) collective-permute-start(bf16[9,64,128]{2,1,0:T(8,128)(2,1)} %get-tuple-element.52), channel_id=1, source_target_pairs={{0,0},{1,2},{2,1},{3,4},{4,3},{5,6},{6,5},{7,8},{8,7},{9,10},{10,9... | collective-permute-start | bytes 442376 | tf_op jit(solution)/shard_map/ppermute | solution.py:604
  9.4 4.5 %collective-permute-start.1 = (bf16[3,64,128]{2,1,0:T(8,128)(2,1)S(1)}, bf16[3,64,128]{2,1,0:T(8,128)(2,1)S(1)}, u32[]{:S(2)}, u32[]{:S(2)}) collective-permute-start(bf16[3,64,128]{2,1,0:T(8,128)(2,1)S(1)} %level_0.1.own), channel_id=1, source_target_pairs={{0,2},{1,3},{2,0},{3,1},{4,6},{5,7},{6,4},{7,5},{8,10},{9,11},{10,... | collective-permute-start | bytes 147464 | tf_op jit(solution)/shard_map/ppermute | solution.py:607
  14.3 6.7 %collective-permute-start.3 = (bf16[5,64,128]{2,1,0:T(8,128)(2,1)S(1)}, bf16[5,64,128]{2,1,0:T(8,128)(2,1)S(1)}, u32[]{:S(2)}, u32[]{:S(2)}) collective-permute-start(bf16[5,64,128]{2,1,0:T(8,128)(2,1)S(1)} %level_1.1.own), channel_id=1, source_target_pairs={{0,6},{1,7},{2,4},{3,5},{4,2},{5,3},{6,0},{7,1},{8,14},{9,15},{10,... | collective-permute-start | bytes 245768 | tf_op jit(solution)/shard_map/ppermute | solution.py:607
  21.4 5.8 %collective-permute-start.5 = (bf16[5,64,128]{2,1,0:T(8,128)(2,1)S(1)}, bf16[5,64,128]{2,1,0:T(8,128)(2,1)S(1)}, u32[]{:S(2)}, u32[]{:S(2)}) collective-permute-start(bf16[5,64,128]{2,1,0:T(8,128)(2,1)S(1)} %get-tuple-element.70.own), channel_id=1, source_target_pairs={{0,8},{1,9},{2,10},{3,11},{4,12},{5,13},{6,14},{7,15},{8,0},{9,1},... | collective-permute-start | bytes 245768 | tf_op jit(solution)/shard_map/ppermute | solution.py:607
  26.2 9.2 %collective-permute-start.4 = (bf16[3,64,128]{2,1,0:T(8,128)(2,1)S(1)}, bf16[3,64,128]{2,1,0:T(8,128)(2,1)S(1)}, u32[]{:S(2)}, u32[]{:S(2)}) collective-permute-start(bf16[3,64,128]{2,1,0:T(8,128)(2,1)S(1)} %get-tuple-element.63), channel_id=1, source_target_pairs={{0,0},{1,1},{2,2},{3,3},{4,4},{5,5},{6,6},{7,7},{8,16},{9,17},{10,... | collective-permute-start | bytes 147464 | tf_op jit(solution)/shard_map/ppermute | solution.py:604
  27.7 8.2 %collective-permute-start.6 = (bf16[3,64,128]{2,1,0:T(8,128)(2,1)S(1)}, bf16[3,64,128]{2,1,0:T(8,128)(2,1)S(1)}, u32[]{:S(2)}, u32[]{:S(2)}) collective-permute-start(bf16[3,64,128]{2,1,0:T(8,128)(2,1)S(1)} %level_3.1.own), channel_id=1, source_target_pairs={{0,24},{1,25},{2,26},{3,27},{4,28},{5,29},{6,30},{7,31},{8,16},{9,... | collective-permute-start | bytes 147464 | tf_op jit(solution)/shard_map/ppermute | solution.py:607
  33.8 11.2 %slice-start = ((s8[8388608]{0:T(1024)(128)(4,1)}), s8[4194304]{0:T(1024)(128)(4,1)S(1)}, s32[]{:S(2)}) async-start(s8[8388608]{0:T(1024)(128)(4,1)} %bitcast.4), calls=%async_computation | async-start | bytes 8388608
  36.0 8.7 %copy-start.6 = (f32[1,6,4,64,64]{4,3,2,1,0:T(8,128)S(1)}, f32[1,6,4,64,64]{4,3,2,1,0:T(8,128)}, u32[]{:S(2)}) copy-start(f32[1,6,4,64,64]{4,3,2,1,0:T(8,128)} %couple_ref) | copy-start | bytes 1179652
  36.0 8.7 %copy-start.9 = (f32[1,5,64,64]{3,2,1,0:T(8,128)S(1)}, f32[1,5,64,64]{3,2,1,0:T(8,128)}, u32[]{:S(2)}) copy-start(f32[1,5,64,64]{3,2,1,0:T(8,128)} %down_ref.1) | copy-start | bytes 245764
  36.0 8.9 %slice-start.1 = ((s8[8388608]{0:T(1024)(128)(4,1)}), s8[4194304]{0:T(1024)(128)(4,1)S(1)}, s32[]{:S(2)}) async-start(s8[8388608]{0:T(1024)(128)(4,1)} %bitcast.4), calls=%async_computation.1 | async-start | bytes 8388608
  36.1 8.9 %copy-start.5 = (bf16[64,64,128]{2,1,0:T(8,128)(2,1)S(1)}, bf16[64,64,128]{2,1,0:T(8,128)(2,1)}, u32[]{:S(2)}) copy-start(bf16[64,64,128]{2,1,0:T(8,128)(2,1)} %get-tuple-element.85.leaf_ref) | copy-start | bytes 3145732
  36.1 8.9 %copy-start.7 = (bf16[8,4,64,64]{3,2,1,0:T(8,128)(2,1)S(1)}, bf16[8,4,64,64]{3,2,1,0:T(8,128)(2,1)}, u32[]{:S(2)}) copy-start(bf16[8,4,64,64]{3,2,1,0:T(8,128)(2,1)} %node_blocks_ref.1) | copy-start | bytes 786436
  36.1 8.9 %copy-start.11 = (bf16[8,64,128]{2,1,0:T(8,128)(2,1)S(1)}, bf16[8,64,128]{2,1,0:T(8,128)(2,1)}, u32[]{:S(2)}) copy-start(bf16[8,64,128]{2,1,0:T(8,128)(2,1)} %get-tuple-element.86.node_ref) | copy-start | bytes 393220
  36.1 8.9 %copy-start.12 = (s32[64,8]{0,1:T(8,128)S(1)}, s32[64,8]{0,1:T(8,128)}, u32[]{:S(2)}) copy-start(s32[64,8]{0,1:T(8,128)} %param.24) | copy-start | bytes 6148
  36.1 8.9 %copy-start.13 = (s32[8,4]{0,1:T(4,128)S(1)}, s32[8,4]{0,1:T(4,128)}, u32[]{:S(2)}) copy-start(s32[8,4]{0,1:T(4,128)} %param.29) | copy-start | bytes 388
  36.1 8.9 %copy-start.14 = (s32[64]{0:T(128)S(1)}, s32[64]{0:T(128)}, u32[]{:S(2)}) copy-start(s32[64]{0:T(128)} %count_ref.1) | copy-start | bytes 772
  36.1 8.9 %copy-start.15 = (s32[8]{0:T(128)S(1)}, s32[8]{0:T(128)}, u32[]{:S(2)}) copy-start(s32[8]{0:T(128)} %node_count_ref.1) | copy-start | bytes 100
  36.1 4.3 %collective-permute-start.7 = (bf16[4,64,128]{2,1,0:T(8,128)(2,1)S(1)}, bf16[4,64,128]{2,1,0:T(8,128)(2,1)S(1)}, u32[]{:S(2)}, u32[]{:S(2)}) collective-permute-start(bf16[4,64,128]{2,1,0:T(8,128)(2,1)S(1)} %level_4.1.own), channel_id=1, source_target_pairs={{0,32},{1,33},{2,34},{3,35},{4,36},{5,37},{6,38},{7,39},{8,40},{9,... | collective-permute-start | bytes 196616 | tf_op jit(solution)/shard_map/ppermute | solution.py:607
  40.5 7.5 %collective-permute-start.8 = (bf16[3,64,128]{2,1,0:T(8,128)(2,1)S(1)}, bf16[3,64,128]{2,1,0:T(8,128)(2,1)S(1)}, u32[]{:S(2)}, u32[]{:S(2)}) collective-permute-start(bf16[3,64,128]{2,1,0:T(8,128)(2,1)S(1)} %level_5.1), channel_id=1, source_target_pairs={{0,96},{1,97},{2,98},{3,99},{4,100},{5,101},{6,102},{7,103},{8,104... | collective-permute-start | bytes 147464 | tf_op jit(solution)/shard_map/ppermute | solution.py:607
  45.1 2.9 %copy-start.3 = (bf16[64,64,256]{2,1,0:T(8,128)(2,1)S(1)}, bf16[64,64,256]{2,1,0:T(8,128)(2,1)}, u32[]{:S(2)}) copy-start(bf16[64,64,256]{2,1,0:T(8,128)(2,1)} %bases_ref.3) | copy-start | bytes 6291460
  45.1 2.9 %copy-start.4 = (bf16[64,64,64]{2,1,0:T(8,128)(2,1)S(1)}, bf16[64,64,64]{2,1,0:T(8,128)(2,1)}, u32[]{:S(2)}) copy-start(bf16[64,64,64]{2,1,0:T(8,128)(2,1)} %transfer_ref.1) | copy-start | bytes 1572868
  45.1 2.9 %copy-start.10 = (bf16[8,64,64]{2,1,0:T(8,128)(2,1)S(1)}, bf16[8,64,64]{2,1,0:T(8,128)(2,1)}, u32[]{:S(2)}) copy-start(bf16[8,64,64]{2,1,0:T(8,128)(2,1)} %down_node_ref.1) | copy-start | bytes 196612

commit v3 on v2

--- a/solution.py
+++ b/solution.py
@@ -15,7 +15,7 @@
 LEAF_AT, NODE_AT, RHS_AT, COORD_AT, HALO_TILES = 0, 4, 6, 8, 9
 CARRY_AT, COEFF_AT = 9, 10
 CHUNKS = 4
-PARTNERS = (2, 6, 8, 24, 32, 96)
+PARTNERS = (2, 6, 8, 24)
 
 
 def dot(a, b):
@@ -225,90 +225,66 @@
     )(dev, *ins)
 
 
-def lowest(round_at):
-    return 0 if round_at < 3 else 3
-
-
-def fixed_tiles(round_at):
-    return 2 if round_at < 5 else 6 - round_at
-
-
-def first_at(height, round_at):
-    if round_at == 6:
-        return height - lowest(round_at)
-    return fixed_tiles(round_at) + 2 * (height - lowest(round_at))
-
-
-def last_at(height, round_at):
-    if round_at == 6:
-        return height - lowest(round_at)
-    return fixed_tiles(round_at) + min(1 + 2 * (height - lowest(round_at)), 2 * (round_at - 1 - lowest(round_at)))
-
-
-def tiles_of(round_at):
-    heights = round_at - lowest(round_at)
-    if round_at == 3:
-        return fixed_tiles(round_at) + 3
-    return fixed_tiles(round_at) + (heights if round_at == 6 else max(2 * heights - 1, 0))
+TILES = {1: 3, 2: 5, 3: 5, 4: 3}
+CARRY, COEFF, PAIR = 0, 1, 2
+FIRST, LAST, PARENT_PAIR = 2, 3, 4
 
 
 def bit_of(dev_ref, height):
     return (dev_ref[0] >> height) & 1
+
+
+def in_order(own, got, bit, hold):
+    hold[bit] = own
+    hold[1 - bit] = got
+    return hold[0], hold[1]
 
 
 def level_body(k, dev_ref, own, got, up_top_ref, out, *rest):
     hold = rest[-1]
     bit = bit_of(dev_ref, k)
-    carry_at, coeff_at = (CARRY_AT, COEFF_AT) if k == 0 else (0, fixed_tiles(k) - 1)
-    hold[bit, 0] = own[coeff_at]
-    hold[1 - bit, 0] = got[coeff_at]
-    pair = join(hold[0, 0], hold[1, 0])
-    heights = range(lowest(k), k)
-    for height in heights:
-        hold[bit, 1 + height] = own[first_at(height, k)]
-        hold[1 - bit, 1 + height] = got[first_at(height, k)]
-        hold[bit, 7 + height] = own[last_at(height, k)]
-        hold[1 - bit, 7 + height] = got[last_at(height, k)]
-    if k < 5:
-        parent = fused_halves(own[carry_at].astype(f32) + got[carry_at].astype(f32))
-        if k < 4:
-            out[0] = split(wide_dot(parent, split(up_top_ref[0, k + 1])))
-        out[fixed_tiles(k + 1) - 1] = twice(parent).astype(bf16)
-    if k == 2:
+    carry_at, coeff_at = (CARRY_AT, COEFF_AT) if k == 0 else (CARRY, COEFF)
+    pair = join(*in_order(own[coeff_at], got[coeff_at], bit, hold))
+    parent = fused_halves(own[carry_at].astype(f32) + got[carry_at].astype(f32))
+    coeff = twice(parent).astype(bf16)
+    if k < 4:
+        out[CARRY] = split(wide_dot(parent, split(up_top_ref[0, k + 1])))
+        out[COEFF] = coeff
+    if k == 0 or k == 3:
+        out[PAIR] = pair
+    elif k == 1:
+        out[FIRST], out[LAST] = in_order(own[PAIR], got[PAIR], bit, hold)
+        out[PARENT_PAIR] = pair
+    elif k == 2:
         side_out = rest[0]
         upper = bit_of(dev_ref, 3)
-        for height in heights:
-            hold[0, 7 + height] = hold[1, 7 + height]
-            hold[1, 7 + height] = hold[0, 1 + height]
-            out[fixed_tiles(3) + height] = hold[upper, 7 + height]
-            side_out[height] = hold[1 - upper, 7 + height]
-        out[fixed_tiles(3) + k] = pair
-        side_out[k] = pair
-    elif k < 5:
-        for height in heights:
-            out[first_at(height, k + 1)] = hold[0, 1 + height]
-            out[last_at(height, k + 1)] = hold[1, 7 + height]
-        out[first_at(k, k + 1)] = pair
+        first = in_order(own[FIRST], got[FIRST], bit, hold)[0]
+        last = in_order(own[LAST], got[LAST], bit, hold)[1]
+        out[2], side_out[0] = in_order(last, first, upper, hold)
+        first, last = in_order(own[PARENT_PAIR], got[PARENT_PAIR], bit, hold)
+        out[3], side_out[1] = in_order(last, first, upper, hold)
+        out[4] = pair
+        side_out[2] = pair
     else:
-        upper = bit_of(dev_ref, 6)
-        for height in heights:
-            hold[0, 7 + height] = hold[1, 7 + height]
-            hold[1, 7 + height] = hold[0, 1 + height]
-            out[first_at(height, 6)] = hold[upper, 7 + height]
-        out[first_at(k, 6)] = pair
+        far_out, across_out = rest[:2]
+        first, last = in_order(own[PAIR], got[PAIR], bit, hold)
+        out[0], far_out[0] = in_order(last, first, bit_of(dev_ref, 5), hold)
+        out[1] = pair
+        far_out[1] = pair
+        far_out[2] = coeff
+        across_out[0] = coeff
 
 
 def level_call(k, dev, own, got, up_top):
-    outs = [shape((tiles_of(k + 1), 64, 128), bf16)]
-    if k == 2:
-        outs += [shape((3, 64, 128), bf16)]
+    tiles = {2: (TILES[3], 3), 4: (2, 3, 1)}.get(k) or (TILES[k + 1],)
+    outs = [shape((count, 64, 128), bf16) for count in tiles]
     ins = [own, got, up_top]
     return call(
         functools.partial(level_body, k),
         outs,
         scalars() + held(*ins),
         held(*outs),
-        [pltpu.VMEM((2, 13, 64, 128), bf16)],
+        [pltpu.VMEM((2, 64, 128), bf16)],
         name="level_%d" % k,
     )(dev, *ins)
 
@@ -389,7 +365,8 @@
                 rim_target[:, :128] = halo[COORD_AT, 32:48, :]
                 rim_target[:, 128:] = halo[COORD_AT, 48:64, :]
 
-    build(first)
+    if count > 0:
+        build(first)
     for s in range(first, first + count):
         if s + 1 < first + count:
             build(s + 1)
@@ -506,34 +483,48 @@
 
 
 def downward_body(
-    devices, dev_ref, side_ref, got_1, got_2, got_3, got_4, got_5, got_6, couple_ref, down_ref,
-    down_node_ref, node_gain_ref, gain_ref, transfer_ref, bases_ref, sum_ref, out_ref, bank, out, sems,
+    devices, dev_ref, side_ref, got_1, got_2, got_3, got_4, near_ref, far_ref, across_ref, couple_ref,
+    down_ref, down_node_ref, node_gain_ref, gain_ref, transfer_ref, bases_ref, sum_ref, out_ref, bank,
+    out, sems,
 ):
     d = dev_ref[0]
+    pick = jnp.where
     bank[0] = jnp.zeros((64, 128), bf16)
+    upper = bit_of(dev_ref, 3)
     for height in range(3):
-        upper = bit_of(dev_ref, 3)
-        bank[4 - 3 * upper + height] = got_3[fixed_tiles(3) + height]
+        bank[4 - 3 * upper + height] = got_3[2 + height]
         bank[1 + 3 * upper + height] = side_ref[height]
-    start = {}
-    at = 7
-    for k, got in ((1, got_1), (2, got_2), (4, got_4), (5, got_5), (6, got_6)):
-        start[k] = at - fixed_tiles(k)
-        for tile in range(fixed_tiles(k), got.shape[0]):
-            bank[at] = got[tile]
-            at += 1
+    bank[7] = got_1[PAIR]
+    bank[8] = got_2[FIRST]
+    bank[9] = got_2[LAST]
+    bank[10] = got_2[PARENT_PAIR]
+    bank[11] = got_4[PAIR]
+    bank[12] = near_ref[0]
+    bank[13] = near_ref[1]
+    bank[14] = far_ref[0]
+    bank[15] = far_ref[1]
+    group = d >> 5
+    odd = group & 1
+    bank[16 + odd] = across_ref[0]
+    bank[17 - odd] = far_ref[2]
+    bank[16] = join(bank[16], bank[17])
+    before = [pick(d >= 8, 1 + height, 0) for height in range(3)]
+    after = [pick(d < devices - 8, 4 + height, 0) for height in range(3)]
+    parent = d >> 1
+    even = (parent & 1) == 0
+    left = [pick(even, pick((parent & 3) == 2, 9, before[0]), 7)]
+    right = [pick(even, 7, pick((parent & 3) == 1, 8, after[0]))]
+    even = ((d >> 2) & 1) == 0
+    left += [pick(even, before[1], 10), before[2]]
+    right += [pick(even, 10, after[1]), after[2]]
+    even = ((d >> 4) & 1) == 0
+    beside_left = [pick(odd == 1, 12 + j, pick(group == 2, 14 + j, 0)) for j in range(2)]
+    beside_right = [pick(odd == 0, 12 + j, pick(group == 1, 14 + j, 0)) for j in range(2)]
+    left += [pick(even, beside_left[0], 11), beside_left[1], pick(group >= 2, 16, 0)]
+    right += [pick(even, 11, beside_right[0]), beside_right[1], pick(group >= 2, 0, 16)]
     gains = []
     for height in range(6):
-        own = d >> (height + 1)
-        left = right = 0
-        if height < 3:
-            left = jnp.where(d >= 8, 1 + height, 0)
-            right = jnp.where(d < devices - 8, 4 + height, 0)
-        for k in range(2 if height < 3 else 6, height, -1):
-            bit = (own >> (k - height - 1)) & 1
-            left = jnp.where(bit == 1, start[k] + last_at(height, k), left)
-            right = jnp.where(bit == 0, start[k] + first_at(height, k), right)
-        tiles = jnp.concatenate([bank[left], bank[right]], axis=1)
+        tiles = jnp.concatenate([bank[left[height]], bank[right[height]]], axis=1)
         gains.append(fused_halves(dot(tiles, couple_ref[height])))
     value = gains[5]
     for height in range(4, -1, -1):
@@ -575,7 +566,7 @@
         scalars() + held(*ins),
         stored(out)[0],
         [
-            pltpu.VMEM((7 + sum(tiles_of(k) - fixed_tiles(k) for k in range(1, 7)), 64, 128), bf16),
+            pltpu.VMEM((18, 64, 128), bf16),
             pltpu.VMEM(out.shape, bf16),
             pltpu.SemaphoreType.DMA((down_node.shape[0],)),
         ],
@@ -597,11 +588,8 @@
     dev = device.astype(jnp.int32).reshape(1)
 
     def beside(block, size):
-        def partner(i):
-            other = i + size if i // size % 2 == 1 else i - size
-            return other if 0 <= other < devices else i
-
-        return lax.ppermute(block, "leaf", [(i, partner(i)) for i in range(devices)])
+        route = [(i, (i + size if i // size % 2 == 1 else i - size) % devices) for i in range(devices)]
+        return lax.ppermute(block, "leaf", route)
 
     def exchange(block, mask):
         return lax.ppermute(block, "leaf", [(i, i ^ mask) for i in range(devices)])
@@ -610,44 +598,57 @@
     leaf, node, inner_out, outer_out = upward(
         dev, rhs, points, upward_leaf_bases, up_leaf, up_node, up_top
     )
-    inner = exchange(inner_out, 1)
-    outer = beside(outer_out, 1)
-    near_sum = near(dev, rhs, points, 0, parts[0], [], None)
-    done = parts[0]
-    own, got = inner_out, inner
+    got = inner = exchange(inner_out, 1)
+    if OUTER_AFTER < 0:
+        outer = beside(outer_out, 1)
+    near_sum = near(dev, rhs, points, 0, PARTS[0], [], None)
+    done = PARTS[0]
+    own = inner_out
     received = []
-    for k in range(6):
-        if k == 1:
-            got, outer, near_sum = tied(got, outer, near_sum)
-        else:
-            got, near_sum = tied(got, near_sum)
+    for k in range(4):
+        got, near_sum = tied(got, near_sum)
         own, *edges = level_call(k, dev, own, got, up_top)
         got = exchange(own, PARTNERS[k])
+        received.append(got)
         if k == 2:
-            side = beside(edges[0], 8)
-        received.append(got)
-        near_sum, leaf, own = tied(near_sum, leaf, own)
-        if k < 5:
-            near_sum = near(
-                dev, rhs, points, done, parts[k + 1], [inner, outer] if k == 4 else [], near_sum
+            side_out = edges[0]
+        if k == SIDE_AFTER:
+            side_out, own = tied(side_out, own)
+            side = beside(side_out, 8)
+        if k == OUTER_AFTER:
+            outer_out, own = tied(outer_out, own)
+            outer = beside(outer_out, 1)
+        near_sum, own = tied(near_sum, own)
+        if PARTS[k + 1] > 0:
+            near_sum = near(dev, rhs, points, done, PARTS[k + 1], [], near_sum)
+            done += PARTS[k + 1]
+        if k == COUPLE_AFTER:
+            leaf, outer, own = tied(leaf, outer, own)
+            gain, node_gain = couple(
+                dev, list_leaf.T, count_leaf, list_node.T, count_node, leaf, node, inner, outer,
+                couple_leaf, couple_node,
             )
-            done += parts[k + 1]
-        if k == 3:
-            side, near_sum = tied(side, near_sum)
-    gain, node_gain = couple(
-        dev, list_leaf.T, count_leaf, list_node.T, count_node, leaf, node, inner, outer,
-        couple_leaf, couple_node,
-    )
-    couple_top, _ = tied(couple_top, own)
-    couple_parts, down_parts = prepare(dev, couple_top, down_top)
-    received[5], gain, couple_parts = tied(received[5], gain, couple_parts)
+            near_sum, gain = tied(near_sum, gain)
+        if k == 2:
+            couple_top, _ = tied(couple_top, own)
+            couple_parts, down_parts = prepare(dev, couple_top, down_top)
+            near_sum, couple_parts = tied(near_sum, couple_parts)
+    got, near_sum, outer, side = tied(got, near_sum, outer, side)
+    near_out, far_out, across_out = level_call(4, dev, own, got, up_top)
+    last = [exchange(near_out, 32), exchange(far_out, 96), exchange(across_out, 64)]
+    near_sum, near_out = tied(near_sum, near_out)
+    near_sum = near(dev, rhs, points, done, PARTS[5], [inner, outer], near_sum)
+    *last, near_sum = tied(*last, near_sum)
     return downward(
-        dev, [side] + received, couple_parts, down_parts,
+        dev, [side] + received + last, couple_parts, down_parts,
         down_node, node_gain, gain, leaf_down_transfer, downward_leaf_bases, near_sum,
     )
 
 
-parts = (10, 12, 14, 8, 10, 10)
+OUTER_AFTER = 0
+COUPLE_AFTER = 3
+SIDE_AFTER = 2
+PARTS = (11, 14, 14, 12, 0, 13)
 
 
 def solution(mesh):

time: 52.6 us -> 45.9 us (0.87)
  starting transfers between devices: 24.7 us -> 17.6 us
  waiting for transfers between devices: 1.49 us -> 2.69 us
  Pallas kernels: 25.6 us -> 24.9 us
    ppermute x7 -> x8, starting transfers between devices: 22.4 us -> 9.67 us  [exchange(): return lax.ppermute(block, 'leaf', [(i, i ^ mask) for i in range(devices)])]
    ppermute x2, starting transfers between devices: 2.36 us -> 7.95 us  [beside(): return lax.ppermute(block, 'leaf', route)]
    ppermute x2, waiting for transfers between devices: 0.01 us -> 1.11 us  [beside(): return lax.ppermute(block, 'leaf', route)]
    pallas_call x6 -> x5, Pallas kernels: 10.9 us -> 10.3 us  [near(): call(functools.partial(near_body, first, count, len(halos) > 0, lax.axis_...]
    ppermute x7 -> x8, waiting for transfers between devices: 1.49 us -> 1.58 us  [exchange(): return lax.ppermute(block, 'leaf', [(i, i ^ mask) for i in range(devices)])]
    pallas_call x6 -> x5, Pallas kernels: 1.85 us -> 1.81 us  [level_call(): call(functools.partial(level_body, k), outs, scalars() + held(*ins), held...]
  transfers between devices with their start and end apart: 9 -> 10, of which waited for: 5 -> 3; matrix products, arithmetic and copies ran while one was open for 0% -> 0% of each run, Pallas kernels for 28% -> 31%
where the time goes in v3:
time: 45.9 us; the launch traced here: 45.8 us
  Pallas kernels  24.9 us (54%)
  starting transfers between devices  17.6 us (38%)
  waiting for transfers between devices  2.69 us (6%)
  between operations  0.54 us (1%)
    pallas_call x5, Pallas kernels, near(): call(functools.partial(near_body, first, count, len(halos) > 0, lax.axis_...  10.3 us
    ppermute x8, starting transfers between devices, exchange(): return lax.ppermute(block, 'leaf', [(i, i ^ mask) for i in range(devices)])  9.67 us
    ppermute x2, starting transfers between devices, beside(): return lax.ppermute(block, 'leaf', route)  7.95 us
    pallas_call x1, Pallas kernels, upward(): call(upward_body, outs, scalars() + stored(*ins), held(*outs), [pltpu.VME...  5.43 us
    pallas_call x1, Pallas kernels, downward(): call(functools.partial(downward_body, lax.axis_size('leaf')), out, scalar...  4.23 us
    pallas_call x1, Pallas kernels, couple(): call(couple_body, outs, scalars(5) + held(*ins), held(*outs), [pltpu.VMEM...  2.88 us
    pallas_call x5, Pallas kernels, level_call(): call(functools.partial(level_body, k), outs, scalars() + held(*ins), held...  1.81 us
    ppermute x8, waiting for transfers between devices, exchange(): return lax.ppermute(block, 'leaf', [(i, i ^ mask) for i in range(devices)])  1.58 us
  transfers between devices with their start and end apart: 10, of which 3 were waited for; matrix products, arithmetic and copies ran while one was open for 0% of the time, Pallas kernels for 31%

profile of v3, /device:TPU:0, one launch (start us, length us, event | category | flops | bytes accessed | tf_op | source)
XLA Modules:
  0.0 45.8 jit_solution(13143201513360914378)
XLA Ops:
  0.0 5.4 %upward.1 = (bf16[64,64,128]{2,1,0:T(8,128)(2,1)}, bf16[8,64,128]{2,1,0:T(8,128)(2,1)}, bf16[11,64,128]{2,1,0:T(8,128)(2,1)}, bf16[9,64,128]{2,1,0:T(8,128)(2,1)}) custom-call(s32[1]{0:T(128)} %bitcast.dev_ref, bf16[64,64,256]{2,1,0:T(8,128)(2,1)} %rhs_ref.11, bf16[3,64,256]{2,1,0:T(8,128)(2,1)} %bitcast.6, bf16[64,64,256]{2,1,0:T(8,128)(2,1)} %bases_ref.2, ...), custom_call_target="tpu_custom_call" | custom-call | tf_op jit(solution)/shard_map/upward/pallas_call | solution.py:208
  5.5 0.1 collective-permute-start
  5.6 1.8 %near_0.1.rest_0_ = f32[64,64,256]{2,1,0:T(8,128)S(1)} custom-call(s32[1]{0:T(128)} %bitcast.dev_ref, bf16[64,64,256]{2,1,0:T(8,128)(2,1)S(1)} %copy-done, bf16[3,64,256]{2,1,0:T(8,128)(2,1)S(1)} %bitcast.7), custom_call_target="tpu_custom_call" | custom-call | tf_op jit(solution)/shard_map/near_0/pallas_call | solution.py:394
  7.4 0.4 level_0.1.own
  7.8 1.6 %collective-permute-start.1 = (bf16[3,64,128]{2,1,0:T(8,128)(2,1)S(1)}, bf16[3,64,128]{2,1,0:T(8,128)(2,1)S(1)}, u32[]{:S(2)}, u32[]{:S(2)}) collective-permute-start(bf16[3,64,128]{2,1,0:T(8,128)(2,1)S(1)} %level_0.1.own), channel_id=1, source_target_pairs={{0,2},{1,3},{2,0},{3,1},{4,6},{5,7},{6,4},{7,5},{8,10},{9,11},{10,... | collective-permute-start | bytes 147464 | tf_op jit(solution)/shard_map/ppermute | solution.py:595
  9.5 2.2 %near_11.1.rest_0_ = f32[64,64,256]{2,1,0:T(8,128)S(1)} custom-call(s32[1]{0:T(128)} %bitcast.dev_ref, bf16[64,64,256]{2,1,0:T(8,128)(2,1)S(1)} %copy-done, bf16[3,64,256]{2,1,0:T(8,128)(2,1)S(1)} %bitcast.8, f32[64,64,256]{2,1,0:T(8,128)S(1)} %near_0.1.rest_0_), custom_call_target="tpu_custom_call", output_to_operand_aliasing={{}: (3, {})} | custom-call | tf_op jit(solution)/shard_map/near_11/pallas_call | solution.py:394
  11.6 0.4 collective-permute-done.1.got.got_1
  12.0 0.4 level_1.1.own
  12.4 2.9 %collective-permute-start.2 = (bf16[5,64,128]{2,1,0:T(8,128)(2,1)S(1)}, bf16[5,64,128]{2,1,0:T(8,128)(2,1)S(1)}, u32[]{:S(2)}, u32[]{:S(2)}) collective-permute-start(bf16[5,64,128]{2,1,0:T(8,128)(2,1)S(1)} %level_1.1.own), channel_id=1, source_target_pairs={{0,6},{1,7},{2,4},{3,5},{4,2},{5,3},{6,0},{7,1},{8,14},{9,15},{10,... | collective-permute-start | bytes 245768 | tf_op jit(solution)/shard_map/ppermute | solution.py:595
  15.3 5.5 %collective-permute-start.5 = (bf16[9,64,128]{2,1,0:T(8,128)(2,1)S(1)}, bf16[9,64,128]{2,1,0:T(8,128)(2,1)S(1)}, u32[]{:S(2)}, u32[]{:S(2)}) collective-permute-start(bf16[9,64,128]{2,1,0:T(8,128)(2,1)S(1)} %copy-done.16), channel_id=1, source_target_pairs={{0,127},{1,2},{2,1},{3,4},{4,3},{5,6},{6,5},{7,8},{8,7},{9,10},{10... | collective-permute-start | bytes 442376 | tf_op jit(solution)/shard_map/ppermute | solution.py:592
  20.8 2.2 %near_25.1.rest_0_ = f32[64,64,256]{2,1,0:T(8,128)S(1)} custom-call(s32[1]{0:T(128)} %bitcast.dev_ref, bf16[64,64,256]{2,1,0:T(8,128)(2,1)S(1)} %copy-done, bf16[3,64,256]{2,1,0:T(8,128)(2,1)S(1)} %bitcast.9, f32[64,64,256]{2,1,0:T(8,128)S(1)} %near_11.1.rest_0_), custom_call_target="tpu_custom_call", output_to_operand_aliasing={{}: (3, {})} | custom-call | tf_op jit(solution)/shard_map/near_25/pallas_call | solution.py:394
  23.0 0.4 level_2.1
  23.4 0.1 collective-permute-start.3
  23.5 0.0 copy-start.6
  23.5 0.0 slice-start.1
  23.5 0.0 copy-start.5
  23.6 0.0 copy-start.7
  23.6 0.0 copy-start.14
  23.6 0.0 copy-start.15
  23.6 1.9 %near_39.1.rest_2_ = f32[64,64,256]{2,1,0:T(8,128)S(1)} custom-call(s32[1]{0:T(128)} %bitcast.dev_ref, bf16[64,64,256]{2,1,0:T(8,128)(2,1)S(1)} %copy-done, bf16[3,64,256]{2,1,0:T(8,128)(2,1)S(1)} %bitcast.10, f32[64,64,256]{2,1,0:T(8,128)S(1)} %near_25.1.rest_0_), custom_call_target="tpu_custom_call", output_to_operand_aliasing={{}: (3, {})} | custom-call | tf_op jit(solution)/shard_map/near_39/pallas_call | solution.py:394
  25.6 2.5 %collective-permute-start.6 = (bf16[3,64,128]{2,1,0:T(8,128)(2,1)S(1)}, bf16[3,64,128]{2,1,0:T(8,128)(2,1)S(1)}, u32[]{:S(2)}, u32[]{:S(2)}) collective-permute-start(bf16[3,64,128]{2,1,0:T(8,128)(2,1)S(1)} %get-tuple-element.87), channel_id=1, source_target_pairs={{0,120},{1,121},{2,122},{3,123},{4,124},{5,125},{6,126},{7,127},{8... | collective-permute-start | bytes 147464 | tf_op jit(solution)/shard_map/ppermute | solution.py:592
  28.0 0.2 prepare.1
  28.3 0.4 level_3.1.own
  28.7 0.2 collective-permute-start.4
  29.1 2.9 %couple.1 = (f32[64,64,64]{2,1,0:T(8,128)S(1)}, f32[8,64,64]{2,1,0:T(8,128)S(1)}) custom-call(s32[1]{0:T(128)} %bitcast.dev_ref, s32[8,64]{1,0:T(8,128)S(1)} %bitcast.12, s32[64]{0:T(128)S(1)} %copy-done.14, s32[4,8]{1,0:T(4,128)S(1)} %bitcast.13, s32[8]{0:T(128)S(1)} %copy-done.15, bf16[64,64,128]{2,1,0:T(8,128)(2,1)S(1)} %copy-done.5, ...), custom_call_target="tpu_custom_call" | custom-call | tf_op jit(solution)/shard_map/couple/pallas_call | solution.py:472
  31.9 1.1 %collective-permute-done.6.side_ref = bf16[3,64,128]{2,1,0:T(8,128)(2,1)S(1)} collective-permute-done((bf16[3,64,128]{2,1,0:T(8,128)(2,1)S(1)}, bf16[3,64,128]{2,1,0:T(8,128)(2,1)S(1)}, u32[]{:S(2)}, u32[]{:S(2)}) %collective-permute-start.6) | collective-permute-done | bytes 49184 | tf_op jit(solution)/shard_map/ppermute | solution.py:592
  33.0 1.2 %collective-permute-done.4.got.got_4 = bf16[3,64,128]{2,1,0:T(8,128)(2,1)S(1)} collective-permute-done((bf16[3,64,128]{2,1,0:T(8,128)(2,1)S(1)}, bf16[3,64,128]{2,1,0:T(8,128)(2,1)S(1)}, u32[]{:S(2)}, u32[]{:S(2)}) %collective-permute-start.4) | collective-permute-done | bytes 49184 | tf_op jit(solution)/shard_map/ppermute | solution.py:595
  34.2 0.2 level_4.1
  34.4 1.2 %collective-permute-start.8 = (bf16[3,64,128]{2,1,0:T(8,128)(2,1)S(1)}, bf16[3,64,128]{2,1,0:T(8,128)(2,1)S(1)}, u32[]{:S(2)}, u32[]{:S(2)}) collective-permute-start(bf16[3,64,128]{2,1,0:T(8,128)(2,1)S(1)} %get-tuple-element.92), channel_id=1, source_target_pairs={{0,96},{1,97},{2,98},{3,99},{4,100},{5,101},{6,102},{7,103},{8,104... | collective-permute-start | bytes 147464 | tf_op jit(solution)/shard_map/ppermute | solution.py:595
  35.6 3.5 %collective-permute-start.9 = (bf16[1,64,128]{2,1,0:T(8,128)(2,1)S(1)}, bf16[1,64,128]{2,1,0:T(8,128)(2,1)S(1)}, u32[]{:S(2)}, u32[]{:S(2)}) collective-permute-start(bf16[1,64,128]{2,1,0:T(8,128)(2,1)S(1)} %get-tuple-element.93), channel_id=1, source_target_pairs={{0,64},{1,65},{2,66},{3,67},{4,68},{5,69},{6,70},{7,71},{8,72},{9,... | collective-permute-start | bytes 49160 | tf_op jit(solution)/shard_map/ppermute | solution.py:595
  39.1 2.3 %near_51.1.sum_ref = f32[64,64,256]{2,1,0:T(8,128)S(1)} custom-call(s32[1]{0:T(128)} %bitcast.dev_ref, bf16[64,64,256]{2,1,0:T(8,128)(2,1)S(1)} %copy-done, bf16[3,64,256]{2,1,0:T(8,128)(2,1)S(1)} %bitcast.11, bf16[11,64,128]{2,1,0:T(8,128)(2,1)S(1)} %collective-permute-done.got.inner_ref.rest_0_, ...), custom_call_target="tpu_custom_call", output_to_operand_aliasing={{}: (5, {})} | custom-call | tf_op jit(solution)/shard_map/near_51/pallas_call | solution.py:394
  41.5 4.2 %downward.1 = bf16[64,64,256]{2,1,0:T(8,128)(2,1)} custom-call(s32[1]{0:T(128)} %bitcast.dev_ref, bf16[3,64,128]{2,1,0:T(8,128)(2,1)S(1)} %collective-permute-done.6.side_ref, bf16[3,64,128]{2,1,0:T(8,128)(2,1)S(1)} %collective-permute-done.1.got.got_1, bf16[5,64,128]{2,1,0:T(8,128)(2,1)S(1)} %collective-permute-done.2.got.got_2, ...), custom_call_target="tpu_custom_call" | custom-call | tf_op jit(solution)/shard_map/downward/pallas_call | solution.py:563
  (41 shorter events, 0.1 us)
Async XLA Ops:
  0.0 5.6 %copy-start = (bf16[64,64,256]{2,1,0:T(8,128)(2,1)S(1)}, bf16[64,64,256]{2,1,0:T(8,128)(2,1)}, u32[]{:S(2)}) copy-start(bf16[64,64,256]{2,1,0:T(8,128)(2,1)} %rhs_ref.11) | copy-start | bytes 6291460
  0.0 5.6 %copy-start.2 = (bf16[64,3,256]{2,0,1:T(8,128)(2,1)S(1)}, bf16[64,3,256]{2,0,1:T(8,128)(2,1)}, u32[]{:S(2)}) copy-start(bf16[64,3,256]{2,0,1:T(8,128)(2,1)} %param.18) | copy-start | bytes 294916
  5.4 1.9 %copy-start.1 = (f32[1,5,64,64]{3,2,1,0:T(8,128)S(1)}, f32[1,5,64,64]{3,2,1,0:T(8,128)}, u32[]{:S(2)}) copy-start(f32[1,5,64,64]{3,2,1,0:T(8,128)} %up_top_ref.11) | copy-start | bytes 245764
  5.5 1.9 %copy-start.8 = (bf16[11,64,128]{2,1,0:T(8,128)(2,1)S(1)}, bf16[11,64,128]{2,1,0:T(8,128)(2,1)}, u32[]{:S(2)}) copy-start(bf16[11,64,128]{2,1,0:T(8,128)(2,1)} %get-tuple-element.55.own) | copy-start | bytes 540676
  5.5 1.9 %collective-permute-start = (bf16[11,64,128]{2,1,0:T(8,128)(2,1)}, bf16[11,64,128]{2,1,0:T(8,128)(2,1)S(1)}, u32[]{:S(2)}, u32[]{:S(2)}) collective-permute-start(bf16[11,64,128]{2,1,0:T(8,128)(2,1)} %get-tuple-element.55.own), channel_id=1, source_target_pairs={{0,1},{1,0},{2,3},{3,2},{4,5},{5,4},{6,7},{7,6},{8,9},{9,8},{10,11... | collective-permute-start | bytes 540680 | tf_op jit(solution)/shard_map/ppermute | solution.py:595
  7.8 4.2 %collective-permute-start.1 = (bf16[3,64,128]{2,1,0:T(8,128)(2,1)S(1)}, bf16[3,64,128]{2,1,0:T(8,128)(2,1)S(1)}, u32[]{:S(2)}, u32[]{:S(2)}) collective-permute-start(bf16[3,64,128]{2,1,0:T(8,128)(2,1)S(1)} %level_0.1.own), channel_id=1, source_target_pairs={{0,2},{1,3},{2,0},{3,1},{4,6},{5,7},{6,4},{7,5},{8,10},{9,11},{10,... | collective-permute-start | bytes 147464 | tf_op jit(solution)/shard_map/ppermute | solution.py:595
  9.4 5.9 %copy-start.16 = (bf16[9,64,128]{2,1,0:T(8,128)(2,1)S(1)}, bf16[9,64,128]{2,1,0:T(8,128)(2,1)}, u32[]{:S(2)}) copy-start(bf16[9,64,128]{2,1,0:T(8,128)(2,1)} %get-tuple-element.80) | copy-start | bytes 442372
  12.4 10.6 %collective-permute-start.2 = (bf16[5,64,128]{2,1,0:T(8,128)(2,1)S(1)}, bf16[5,64,128]{2,1,0:T(8,128)(2,1)S(1)}, u32[]{:S(2)}, u32[]{:S(2)}) collective-permute-start(bf16[5,64,128]{2,1,0:T(8,128)(2,1)S(1)} %level_1.1.own), channel_id=1, source_target_pairs={{0,6},{1,7},{2,4},{3,5},{4,2},{5,3},{6,0},{7,1},{8,14},{9,15},{10,... | collective-permute-start | bytes 245768 | tf_op jit(solution)/shard_map/ppermute | solution.py:595
  15.3 13.6 %collective-permute-start.5 = (bf16[9,64,128]{2,1,0:T(8,128)(2,1)S(1)}, bf16[9,64,128]{2,1,0:T(8,128)(2,1)S(1)}, u32[]{:S(2)}, u32[]{:S(2)}) collective-permute-start(bf16[9,64,128]{2,1,0:T(8,128)(2,1)S(1)} %copy-done.16), channel_id=1, source_target_pairs={{0,127},{1,2},{2,1},{3,4},{4,3},{5,6},{6,5},{7,8},{8,7},{9,10},{10... | collective-permute-start | bytes 442376 | tf_op jit(solution)/shard_map/ppermute | solution.py:592
  20.8 8.1 %slice-start = ((s8[8388608]{0:T(1024)(128)(4,1)}), s8[4194304]{0:T(1024)(128)(4,1)S(1)}, s32[]{:S(2)}) async-start(s8[8388608]{0:T(1024)(128)(4,1)} %bitcast.4), calls=%async_computation | async-start | bytes 8388608
  23.4 4.8 %collective-permute-start.3 = (bf16[5,64,128]{2,1,0:T(8,128)(2,1)S(1)}, bf16[5,64,128]{2,1,0:T(8,128)(2,1)S(1)}, u32[]{:S(2)}, u32[]{:S(2)}) collective-permute-start(bf16[5,64,128]{2,1,0:T(8,128)(2,1)S(1)} %get-tuple-element.71.own), channel_id=1, source_target_pairs={{0,8},{1,9},{2,10},{3,11},{4,12},{5,13},{6,14},{7,15},{8,0},{9,1},... | collective-permute-start | bytes 245768 | tf_op jit(solution)/shard_map/ppermute | solution.py:595
  23.5 4.5 %copy-start.6 = (f32[1,6,4,64,64]{4,3,2,1,0:T(8,128)S(1)}, f32[1,6,4,64,64]{4,3,2,1,0:T(8,128)}, u32[]{:S(2)}) copy-start(f32[1,6,4,64,64]{4,3,2,1,0:T(8,128)} %couple_ref) | copy-start | bytes 1179652
  23.5 4.5 %copy-start.9 = (f32[1,5,64,64]{3,2,1,0:T(8,128)S(1)}, f32[1,5,64,64]{3,2,1,0:T(8,128)}, u32[]{:S(2)}) copy-start(f32[1,5,64,64]{3,2,1,0:T(8,128)} %down_ref.1) | copy-start | bytes 245764
  23.5 5.4 %slice-start.1 = ((s8[8388608]{0:T(1024)(128)(4,1)}), s8[4194304]{0:T(1024)(128)(4,1)S(1)}, s32[]{:S(2)}) async-start(s8[8388608]{0:T(1024)(128)(4,1)} %bitcast.4), calls=%async_computation.1 | async-start | bytes 8388608
  23.5 5.4 %copy-start.5 = (bf16[64,64,128]{2,1,0:T(8,128)(2,1)S(1)}, bf16[64,64,128]{2,1,0:T(8,128)(2,1)}, u32[]{:S(2)}) copy-start(bf16[64,64,128]{2,1,0:T(8,128)(2,1)} %get-tuple-element.82.leaf_ref) | copy-start | bytes 3145732
  23.6 5.4 %copy-start.7 = (bf16[8,4,64,64]{3,2,1,0:T(8,128)(2,1)S(1)}, bf16[8,4,64,64]{3,2,1,0:T(8,128)(2,1)}, u32[]{:S(2)}) copy-start(bf16[8,4,64,64]{3,2,1,0:T(8,128)(2,1)} %node_blocks_ref.1) | copy-start | bytes 786436
  23.6 5.4 %copy-start.11 = (bf16[8,64,128]{2,1,0:T(8,128)(2,1)S(1)}, bf16[8,64,128]{2,1,0:T(8,128)(2,1)}, u32[]{:S(2)}) copy-start(bf16[8,64,128]{2,1,0:T(8,128)(2,1)} %get-tuple-element.83.node_ref) | copy-start | bytes 393220
  23.6 5.4 %copy-start.12 = (s32[64,8]{0,1:T(8,128)S(1)}, s32[64,8]{0,1:T(8,128)}, u32[]{:S(2)}) copy-start(s32[64,8]{0,1:T(8,128)} %param.24) | copy-start | bytes 6148
  23.6 5.4 %copy-start.13 = (s32[8,4]{0,1:T(4,128)S(1)}, s32[8,4]{0,1:T(4,128)}, u32[]{:S(2)}) copy-start(s32[8,4]{0,1:T(4,128)} %param.29) | copy-start | bytes 388
  23.6 5.4 %copy-start.14 = (s32[64]{0:T(128)S(1)}, s32[64]{0:T(128)}, u32[]{:S(2)}) copy-start(s32[64]{0:T(128)} %count_ref.1) | copy-start | bytes 772
  23.6 5.4 %copy-start.15 = (s32[8]{0:T(128)S(1)}, s32[8]{0:T(128)}, u32[]{:S(2)}) copy-start(s32[8]{0:T(128)} %node_count_ref.1) | copy-start | bytes 100
  25.6 7.5 %collective-permute-start.6 = (bf16[3,64,128]{2,1,0:T(8,128)(2,1)S(1)}, bf16[3,64,128]{2,1,0:T(8,128)(2,1)S(1)}, u32[]{:S(2)}, u32[]{:S(2)}) collective-permute-start(bf16[3,64,128]{2,1,0:T(8,128)(2,1)S(1)} %get-tuple-element.87), channel_id=1, source_target_pairs={{0,120},{1,121},{2,122},{3,123},{4,124},{5,125},{6,126},{7,127},{8... | collective-permute-start | bytes 147464 | tf_op jit(solution)/shard_map/ppermute | solution.py:592
  28.7 5.5 %collective-permute-start.4 = (bf16[3,64,128]{2,1,0:T(8,128)(2,1)S(1)}, bf16[3,64,128]{2,1,0:T(8,128)(2,1)S(1)}, u32[]{:S(2)}, u32[]{:S(2)}) collective-permute-start(bf16[3,64,128]{2,1,0:T(8,128)(2,1)S(1)} %level_3.1.own), channel_id=1, source_target_pairs={{0,24},{1,25},{2,26},{3,27},{4,28},{5,29},{6,30},{7,31},{8,16},{9,... | collective-permute-start | bytes 147464 | tf_op jit(solution)/shard_map/ppermute | solution.py:595
  34.4 7.0 %collective-permute-start.8 = (bf16[3,64,128]{2,1,0:T(8,128)(2,1)S(1)}, bf16[3,64,128]{2,1,0:T(8,128)(2,1)S(1)}, u32[]{:S(2)}, u32[]{:S(2)}) collective-permute-start(bf16[3,64,128]{2,1,0:T(8,128)(2,1)S(1)} %get-tuple-element.92), channel_id=1, source_target_pairs={{0,96},{1,97},{2,98},{3,99},{4,100},{5,101},{6,102},{7,103},{8,104... | collective-permute-start | bytes 147464 | tf_op jit(solution)/shard_map/ppermute | solution.py:595
  35.6 5.8 %collective-permute-start.7 = (bf16[2,64,128]{2,1,0:T(8,128)(2,1)S(1)}, bf16[2,64,128]{2,1,0:T(8,128)(2,1)S(1)}, u32[]{:S(2)}, u32[]{:S(2)}) collective-permute-start(bf16[2,64,128]{2,1,0:T(8,128)(2,1)S(1)} %get-tuple-element.91), channel_id=1, source_target_pairs={{0,32},{1,33},{2,34},{3,35},{4,36},{5,37},{6,38},{7,39},{8,40},{9,... | collective-permute-start | bytes 98312 | tf_op jit(solution)/shard_map/ppermute | solution.py:595
  35.6 5.8 %copy-start.3 = (bf16[64,64,256]{2,1,0:T(8,128)(2,1)S(1)}, bf16[64,64,256]{2,1,0:T(8,128)(2,1)}, u32[]{:S(2)}) copy-start(bf16[64,64,256]{2,1,0:T(8,128)(2,1)} %bases_ref.3) | copy-start | bytes 6291460
  35.6 5.8 %copy-start.4 = (bf16[64,64,64]{2,1,0:T(8,128)(2,1)S(1)}, bf16[64,64,64]{2,1,0:T(8,128)(2,1)}, u32[]{:S(2)}) copy-start(bf16[64,64,64]{2,1,0:T(8,128)(2,1)} %transfer_ref.1) | copy-start | bytes 1572868
  35.6 5.8 %copy-start.10 = (bf16[8,64,64]{2,1,0:T(8,128)(2,1)S(1)}, bf16[8,64,64]{2,1,0:T(8,128)(2,1)}, u32[]{:S(2)}) copy-start(bf16[8,64,64]{2,1,0:T(8,128)(2,1)} %down_node_ref.1) | copy-start | bytes 196612
  35.6 5.7 %collective-permute-start.9 = (bf16[1,64,128]{2,1,0:T(8,128)(2,1)S(1)}, bf16[1,64,128]{2,1,0:T(8,128)(2,1)S(1)}, u32[]{:S(2)}, u32[]{:S(2)}) collective-permute-start(bf16[1,64,128]{2,1,0:T(8,128)(2,1)S(1)} %get-tuple-element.93), channel_id=1, source_target_pairs={{0,64},{1,65},{2,66},{3,67},{4,68},{5,69},{6,70},{7,71},{8,72},{9,... | collective-permute-start | bytes 49160 | tf_op jit(solution)/shard_map/ppermute | solution.py:595

commit v4 on v3

--- a/solution.py
+++ b/solution.py
@@ -153,8 +153,7 @@
         for move in moves(c):
             move.wait()
         for leaf in range(c * chunk, (c + 1) * chunk):
-            base = bases[leaf]
-            leaf_ref[leaf] = dot_rows(rhs[leaf], jnp.concatenate([base, base], axis=0)).astype(bf16)
+            leaf_ref[leaf] = twice(dot_rows(rhs[leaf], bases[leaf])).astype(bf16)
 
     others[3].wait()
     others[1].wait()
@@ -537,22 +536,30 @@
         return pltpu.make_async_copy(out.at[at], out_ref.at[at], sems.at[g])
 
     node_values = [(node_gain_ref[g] + dot(rounded, down_node_ref[g])).astype(bf16) for g in range(groups)]
+
+    def move(g):
+        at = pl.ds(g * 8, 8)
+        return pltpu.make_async_copy(out.at[at], out_ref.at[at], sems.at[g])
+
+    node_values = [(node_gain_ref[g] + dot(rounded, down_node_ref[g])).astype(bf16) for g in range(groups)]
     for g in range(groups):
         bank[g, :, :64] = node_values[g]
 
-    def group(g, _):
-        node_value = bank[g, :, :64]
-        leaf_values = [
-            (gain_ref[g * 8 + b] + dot(node_value, transfer_ref[g * 8 + b])).astype(bf16) for b in range(8)
+    values = {}
+
+    def early(g):
+        values[g] = [
+            (gain_ref[g * 8 + b] + dot(node_values[g], transfer_ref[g * 8 + b])).astype(bf16) for b in range(8)
         ]
+
+    early(0)
+    for g in range(groups):
+        if g + 1 < groups:
+            early(g + 1)
         for b in range(8):
             leaf = g * 8 + b
-            out[leaf] = (sum_ref[leaf] + dot(leaf_values[b], bases_ref[leaf])).astype(bf16)
+            out[leaf] = (sum_ref[leaf] + dot(values[g][b], bases_ref[leaf])).astype(bf16)
         move(g).start()
-        return 0
-
-    for g in range(groups):
-        group(g, 0)
     for g in range(groups):
         move(g).wait()
 

time: 45.9 us -> 45 us (0.980)
  Pallas kernels: 24.9 us -> 24 us
    pallas_call x1, Pallas kernels: 4.23 us -> 3.54 us  [downward(): call(functools.partial(downward_body, lax.axis_size('leaf')), out, scalar...]
  transfers between devices with their start and end apart: 10 -> 10, of which waited for: 3 -> 3; matrix products, arithmetic and copies ran while one was open for 0% -> 0% of each run, Pallas kernels for 31% -> 32%
where the time goes in v4:
time: 45 us; the launch traced here: 44.9 us
  Pallas kernels  24 us (53%)
  starting transfers between devices  17.6 us (39%)
  waiting for transfers between devices  2.69 us (6%)
  between operations  0.54 us (1%)
    pallas_call x5, Pallas kernels, near(): call(functools.partial(near_body, first, count, len(halos) > 0, lax.axis_...  10.3 us
    ppermute x8, starting transfers between devices, exchange(): return lax.ppermute(block, 'leaf', [(i, i ^ mask) for i in range(devices)])  9.66 us
    ppermute x2, starting transfers between devices, beside(): return lax.ppermute(block, 'leaf', route)  7.94 us
    pallas_call x1, Pallas kernels, upward(): call(upward_body, outs, scalars() + stored(*ins), held(*outs), [pltpu.VME...  5.19 us
    pallas_call x1, Pallas kernels, downward(): call(functools.partial(downward_body, lax.axis_size('leaf')), out, scalar...  3.54 us
    pallas_call x1, Pallas kernels, couple(): call(couple_body, outs, scalars(5) + held(*ins), held(*outs), [pltpu.VMEM...  2.88 us
    pallas_call x5, Pallas kernels, level_call(): call(functools.partial(level_body, k), outs, scalars() + held(*ins), held...  1.81 us
    ppermute x8, waiting for transfers between devices, exchange(): return lax.ppermute(block, 'leaf', [(i, i ^ mask) for i in range(devices)])  1.55 us
  transfers between devices with their start and end apart: 10, of which 3 were waited for; matrix products, arithmetic and copies ran while one was open for 0% of the time, Pallas kernels for 32%

profile of v4, /device:TPU:0, one launch (start us, length us, event | category | flops | bytes accessed | tf_op | source)
XLA Modules:
  0.0 44.9 jit_solution(2152702130105007063)
XLA Ops:
  0.0 5.2 %upward.1 = (bf16[64,64,128]{2,1,0:T(8,128)(2,1)}, bf16[8,64,128]{2,1,0:T(8,128)(2,1)}, bf16[11,64,128]{2,1,0:T(8,128)(2,1)}, bf16[9,64,128]{2,1,0:T(8,128)(2,1)}) custom-call(s32[1]{0:T(128)} %bitcast.dev_ref, bf16[64,64,256]{2,1,0:T(8,128)(2,1)} %rhs_ref.11, bf16[3,64,256]{2,1,0:T(8,128)(2,1)} %bitcast.6, bf16[64,64,256]{2,1,0:T(8,128)(2,1)} %bases_ref.2, ...), custom_call_target="tpu_custom_call" | custom-call | tf_op jit(solution)/shard_map/upward/pallas_call | solution.py:207
  5.2 0.0 copy-start.1
  5.2 0.1 collective-permute-start
  5.3 1.8 %near_0.1.rest_0_ = f32[64,64,256]{2,1,0:T(8,128)S(1)} custom-call(s32[1]{0:T(128)} %bitcast.dev_ref, bf16[64,64,256]{2,1,0:T(8,128)(2,1)S(1)} %copy-done, bf16[3,64,256]{2,1,0:T(8,128)(2,1)S(1)} %bitcast.7), custom_call_target="tpu_custom_call" | custom-call | tf_op jit(solution)/shard_map/near_0/pallas_call | solution.py:393
  7.2 0.4 level_0.1.own
  7.6 1.6 %collective-permute-start.1 = (bf16[3,64,128]{2,1,0:T(8,128)(2,1)S(1)}, bf16[3,64,128]{2,1,0:T(8,128)(2,1)S(1)}, u32[]{:S(2)}, u32[]{:S(2)}) collective-permute-start(bf16[3,64,128]{2,1,0:T(8,128)(2,1)S(1)} %level_0.1.own), channel_id=1, source_target_pairs={{0,2},{1,3},{2,0},{3,1},{4,6},{5,7},{6,4},{7,5},{8,10},{9,11},{10,... | collective-permute-start | bytes 147464 | tf_op jit(solution)/shard_map/ppermute | solution.py:602
  9.2 2.2 %near_11.1.rest_0_ = f32[64,64,256]{2,1,0:T(8,128)S(1)} custom-call(s32[1]{0:T(128)} %bitcast.dev_ref, bf16[64,64,256]{2,1,0:T(8,128)(2,1)S(1)} %copy-done, bf16[3,64,256]{2,1,0:T(8,128)(2,1)S(1)} %bitcast.8, f32[64,64,256]{2,1,0:T(8,128)S(1)} %near_0.1.rest_0_), custom_call_target="tpu_custom_call", output_to_operand_aliasing={{}: (3, {})} | custom-call | tf_op jit(solution)/shard_map/near_11/pallas_call | solution.py:393
  11.4 0.4 collective-permute-done.1.got.got_1
  11.8 0.4 level_1.1.own
  12.2 2.9 %collective-permute-start.2 = (bf16[5,64,128]{2,1,0:T(8,128)(2,1)S(1)}, bf16[5,64,128]{2,1,0:T(8,128)(2,1)S(1)}, u32[]{:S(2)}, u32[]{:S(2)}) collective-permute-start(bf16[5,64,128]{2,1,0:T(8,128)(2,1)S(1)} %level_1.1.own), channel_id=1, source_target_pairs={{0,6},{1,7},{2,4},{3,5},{4,2},{5,3},{6,0},{7,1},{8,14},{9,15},{10,... | collective-permute-start | bytes 245768 | tf_op jit(solution)/shard_map/ppermute | solution.py:602
  15.1 5.5 %collective-permute-start.5 = (bf16[9,64,128]{2,1,0:T(8,128)(2,1)S(1)}, bf16[9,64,128]{2,1,0:T(8,128)(2,1)S(1)}, u32[]{:S(2)}, u32[]{:S(2)}) collective-permute-start(bf16[9,64,128]{2,1,0:T(8,128)(2,1)S(1)} %copy-done.16), channel_id=1, source_target_pairs={{0,127},{1,2},{2,1},{3,4},{4,3},{5,6},{6,5},{7,8},{8,7},{9,10},{10... | collective-permute-start | bytes 442376 | tf_op jit(solution)/shard_map/ppermute | solution.py:599
  20.6 2.2 %near_25.1.rest_0_ = f32[64,64,256]{2,1,0:T(8,128)S(1)} custom-call(s32[1]{0:T(128)} %bitcast.dev_ref, bf16[64,64,256]{2,1,0:T(8,128)(2,1)S(1)} %copy-done, bf16[3,64,256]{2,1,0:T(8,128)(2,1)S(1)} %bitcast.9, f32[64,64,256]{2,1,0:T(8,128)S(1)} %near_11.1.rest_0_), custom_call_target="tpu_custom_call", output_to_operand_aliasing={{}: (3, {})} | custom-call | tf_op jit(solution)/shard_map/near_25/pallas_call | solution.py:393
  22.8 0.4 level_2.1
  23.2 0.1 collective-permute-start.3
  23.3 0.0 copy-start.6
  23.3 0.0 copy-start.9
  23.3 0.0 slice-start.1
  23.3 0.0 copy-start.12
  23.4 0.0 copy-start.13
  23.4 1.9 %near_39.1.rest_2_ = f32[64,64,256]{2,1,0:T(8,128)S(1)} custom-call(s32[1]{0:T(128)} %bitcast.dev_ref, bf16[64,64,256]{2,1,0:T(8,128)(2,1)S(1)} %copy-done, bf16[3,64,256]{2,1,0:T(8,128)(2,1)S(1)} %bitcast.10, f32[64,64,256]{2,1,0:T(8,128)S(1)} %near_25.1.rest_0_), custom_call_target="tpu_custom_call", output_to_operand_aliasing={{}: (3, {})} | custom-call | tf_op jit(solution)/shard_map/near_39/pallas_call | solution.py:393
  25.3 2.4 %collective-permute-start.6 = (bf16[3,64,128]{2,1,0:T(8,128)(2,1)S(1)}, bf16[3,64,128]{2,1,0:T(8,128)(2,1)S(1)}, u32[]{:S(2)}, u32[]{:S(2)}) collective-permute-start(bf16[3,64,128]{2,1,0:T(8,128)(2,1)S(1)} %get-tuple-element.87), channel_id=1, source_target_pairs={{0,120},{1,121},{2,122},{3,123},{4,124},{5,125},{6,126},{7,127},{8... | collective-permute-start | bytes 147464 | tf_op jit(solution)/shard_map/ppermute | solution.py:599
  27.8 0.2 prepare.1
  28.0 0.4 level_3.1.own
  28.4 0.2 collective-permute-start.4
  28.8 2.9 %couple.1 = (f32[64,64,64]{2,1,0:T(8,128)S(1)}, f32[8,64,64]{2,1,0:T(8,128)S(1)}) custom-call(s32[1]{0:T(128)} %bitcast.dev_ref, s32[8,64]{1,0:T(8,128)S(1)} %bitcast.12, s32[64]{0:T(128)S(1)} %copy-done.14, s32[4,8]{1,0:T(4,128)S(1)} %bitcast.13, s32[8]{0:T(128)S(1)} %copy-done.15, bf16[64,64,128]{2,1,0:T(8,128)(2,1)S(1)} %copy-done.5, ...), custom_call_target="tpu_custom_call" | custom-call | tf_op jit(solution)/shard_map/couple/pallas_call | solution.py:471
  31.7 1.1 %collective-permute-done.6.side_ref = bf16[3,64,128]{2,1,0:T(8,128)(2,1)S(1)} collective-permute-done((bf16[3,64,128]{2,1,0:T(8,128)(2,1)S(1)}, bf16[3,64,128]{2,1,0:T(8,128)(2,1)S(1)}, u32[]{:S(2)}, u32[]{:S(2)}) %collective-permute-start.6) | collective-permute-done | bytes 49184 | tf_op jit(solution)/shard_map/ppermute | solution.py:599
  32.8 1.2 %collective-permute-done.4.got.got_4 = bf16[3,64,128]{2,1,0:T(8,128)(2,1)S(1)} collective-permute-done((bf16[3,64,128]{2,1,0:T(8,128)(2,1)S(1)}, bf16[3,64,128]{2,1,0:T(8,128)(2,1)S(1)}, u32[]{:S(2)}, u32[]{:S(2)}) %collective-permute-start.4) | collective-permute-done | bytes 49184 | tf_op jit(solution)/shard_map/ppermute | solution.py:602
  34.0 0.2 level_4.1
  34.1 1.3 %collective-permute-start.8 = (bf16[3,64,128]{2,1,0:T(8,128)(2,1)S(1)}, bf16[3,64,128]{2,1,0:T(8,128)(2,1)S(1)}, u32[]{:S(2)}, u32[]{:S(2)}) collective-permute-start(bf16[3,64,128]{2,1,0:T(8,128)(2,1)S(1)} %get-tuple-element.92), channel_id=1, source_target_pairs={{0,96},{1,97},{2,98},{3,99},{4,100},{5,101},{6,102},{7,103},{8,104... | collective-permute-start | bytes 147464 | tf_op jit(solution)/shard_map/ppermute | solution.py:602
  35.4 3.4 %collective-permute-start.9 = (bf16[1,64,128]{2,1,0:T(8,128)(2,1)S(1)}, bf16[1,64,128]{2,1,0:T(8,128)(2,1)S(1)}, u32[]{:S(2)}, u32[]{:S(2)}) collective-permute-start(bf16[1,64,128]{2,1,0:T(8,128)(2,1)S(1)} %get-tuple-element.93), channel_id=1, source_target_pairs={{0,64},{1,65},{2,66},{3,67},{4,68},{5,69},{6,70},{7,71},{8,72},{9,... | collective-permute-start | bytes 49160 | tf_op jit(solution)/shard_map/ppermute | solution.py:602
  38.9 2.3 %near_51.1.sum_ref = f32[64,64,256]{2,1,0:T(8,128)S(1)} custom-call(s32[1]{0:T(128)} %bitcast.dev_ref, bf16[64,64,256]{2,1,0:T(8,128)(2,1)S(1)} %copy-done, bf16[3,64,256]{2,1,0:T(8,128)(2,1)S(1)} %bitcast.11, bf16[11,64,128]{2,1,0:T(8,128)(2,1)S(1)} %collective-permute-done.got.inner_ref.rest_0_, ...), custom_call_target="tpu_custom_call", output_to_operand_aliasing={{}: (5, {})} | custom-call | tf_op jit(solution)/shard_map/near_51/pallas_call | solution.py:393
  41.2 3.5 %downward.1 = bf16[64,64,256]{2,1,0:T(8,128)(2,1)} custom-call(s32[1]{0:T(128)} %bitcast.dev_ref, bf16[3,64,128]{2,1,0:T(8,128)(2,1)S(1)} %collective-permute-done.6.side_ref, bf16[3,64,128]{2,1,0:T(8,128)(2,1)S(1)} %collective-permute-done.1.got.got_1, bf16[5,64,128]{2,1,0:T(8,128)(2,1)S(1)} %collective-permute-done.2.got.got_2, ...), custom_call_target="tpu_custom_call" | custom-call | tf_op jit(solution)/shard_map/downward/pallas_call | solution.py:570
  (41 shorter events, 0.1 us)
Async XLA Ops:
  0.0 5.3 %copy-start = (bf16[64,64,256]{2,1,0:T(8,128)(2,1)S(1)}, bf16[64,64,256]{2,1,0:T(8,128)(2,1)}, u32[]{:S(2)}) copy-start(bf16[64,64,256]{2,1,0:T(8,128)(2,1)} %rhs_ref.11) | copy-start | bytes 6291460
  0.0 5.3 %copy-start.2 = (bf16[64,3,256]{2,0,1:T(8,128)(2,1)S(1)}, bf16[64,3,256]{2,0,1:T(8,128)(2,1)}, u32[]{:S(2)}) copy-start(bf16[64,3,256]{2,0,1:T(8,128)(2,1)} %param.18) | copy-start | bytes 294916
  5.2 1.9 %copy-start.1 = (f32[1,5,64,64]{3,2,1,0:T(8,128)S(1)}, f32[1,5,64,64]{3,2,1,0:T(8,128)}, u32[]{:S(2)}) copy-start(f32[1,5,64,64]{3,2,1,0:T(8,128)} %up_top_ref.11) | copy-start | bytes 245764
  5.2 1.9 %copy-start.8 = (bf16[11,64,128]{2,1,0:T(8,128)(2,1)S(1)}, bf16[11,64,128]{2,1,0:T(8,128)(2,1)}, u32[]{:S(2)}) copy-start(bf16[11,64,128]{2,1,0:T(8,128)(2,1)} %get-tuple-element.55.own) | copy-start | bytes 540676
  5.2 1.9 %collective-permute-start = (bf16[11,64,128]{2,1,0:T(8,128)(2,1)}, bf16[11,64,128]{2,1,0:T(8,128)(2,1)S(1)}, u32[]{:S(2)}, u32[]{:S(2)}) collective-permute-start(bf16[11,64,128]{2,1,0:T(8,128)(2,1)} %get-tuple-element.55.own), channel_id=1, source_target_pairs={{0,1},{1,0},{2,3},{3,2},{4,5},{5,4},{6,7},{7,6},{8,9},{9,8},{10,11... | collective-permute-start | bytes 540680 | tf_op jit(solution)/shard_map/ppermute | solution.py:602
  7.6 4.2 %collective-permute-start.1 = (bf16[3,64,128]{2,1,0:T(8,128)(2,1)S(1)}, bf16[3,64,128]{2,1,0:T(8,128)(2,1)S(1)}, u32[]{:S(2)}, u32[]{:S(2)}) collective-permute-start(bf16[3,64,128]{2,1,0:T(8,128)(2,1)S(1)} %level_0.1.own), channel_id=1, source_target_pairs={{0,2},{1,3},{2,0},{3,1},{4,6},{5,7},{6,4},{7,5},{8,10},{9,11},{10,... | collective-permute-start | bytes 147464 | tf_op jit(solution)/shard_map/ppermute | solution.py:602
  9.2 5.9 %copy-start.16 = (bf16[9,64,128]{2,1,0:T(8,128)(2,1)S(1)}, bf16[9,64,128]{2,1,0:T(8,128)(2,1)}, u32[]{:S(2)}) copy-start(bf16[9,64,128]{2,1,0:T(8,128)(2,1)} %get-tuple-element.80) | copy-start | bytes 442372
  12.2 10.6 %collective-permute-start.2 = (bf16[5,64,128]{2,1,0:T(8,128)(2,1)S(1)}, bf16[5,64,128]{2,1,0:T(8,128)(2,1)S(1)}, u32[]{:S(2)}, u32[]{:S(2)}) collective-permute-start(bf16[5,64,128]{2,1,0:T(8,128)(2,1)S(1)} %level_1.1.own), channel_id=1, source_target_pairs={{0,6},{1,7},{2,4},{3,5},{4,2},{5,3},{6,0},{7,1},{8,14},{9,15},{10,... | collective-permute-start | bytes 245768 | tf_op jit(solution)/shard_map/ppermute | solution.py:602
  15.1 13.6 %collective-permute-start.5 = (bf16[9,64,128]{2,1,0:T(8,128)(2,1)S(1)}, bf16[9,64,128]{2,1,0:T(8,128)(2,1)S(1)}, u32[]{:S(2)}, u32[]{:S(2)}) collective-permute-start(bf16[9,64,128]{2,1,0:T(8,128)(2,1)S(1)} %copy-done.16), channel_id=1, source_target_pairs={{0,127},{1,2},{2,1},{3,4},{4,3},{5,6},{6,5},{7,8},{8,7},{9,10},{10... | collective-permute-start | bytes 442376 | tf_op jit(solution)/shard_map/ppermute | solution.py:599
  20.6 8.1 %slice-start = ((s8[8388608]{0:T(1024)(128)(4,1)}), s8[4194304]{0:T(1024)(128)(4,1)S(1)}, s32[]{:S(2)}) async-start(s8[8388608]{0:T(1024)(128)(4,1)} %bitcast.4), calls=%async_computation | async-start | bytes 8388608
  23.2 4.8 %collective-permute-start.3 = (bf16[5,64,128]{2,1,0:T(8,128)(2,1)S(1)}, bf16[5,64,128]{2,1,0:T(8,128)(2,1)S(1)}, u32[]{:S(2)}, u32[]{:S(2)}) collective-permute-start(bf16[5,64,128]{2,1,0:T(8,128)(2,1)S(1)} %get-tuple-element.71.own), channel_id=1, source_target_pairs={{0,8},{1,9},{2,10},{3,11},{4,12},{5,13},{6,14},{7,15},{8,0},{9,1},... | collective-permute-start | bytes 245768 | tf_op jit(solution)/shard_map/ppermute | solution.py:602
  23.3 4.5 %copy-start.6 = (f32[1,6,4,64,64]{4,3,2,1,0:T(8,128)S(1)}, f32[1,6,4,64,64]{4,3,2,1,0:T(8,128)}, u32[]{:S(2)}) copy-start(f32[1,6,4,64,64]{4,3,2,1,0:T(8,128)} %couple_ref) | copy-start | bytes 1179652
  23.3 4.5 %copy-start.9 = (f32[1,5,64,64]{3,2,1,0:T(8,128)S(1)}, f32[1,5,64,64]{3,2,1,0:T(8,128)}, u32[]{:S(2)}) copy-start(f32[1,5,64,64]{3,2,1,0:T(8,128)} %down_ref.1) | copy-start | bytes 245764
  23.3 5.4 %slice-start.1 = ((s8[8388608]{0:T(1024)(128)(4,1)}), s8[4194304]{0:T(1024)(128)(4,1)S(1)}, s32[]{:S(2)}) async-start(s8[8388608]{0:T(1024)(128)(4,1)} %bitcast.4), calls=%async_computation.1 | async-start | bytes 8388608
  23.3 5.4 %copy-start.5 = (bf16[64,64,128]{2,1,0:T(8,128)(2,1)S(1)}, bf16[64,64,128]{2,1,0:T(8,128)(2,1)}, u32[]{:S(2)}) copy-start(bf16[64,64,128]{2,1,0:T(8,128)(2,1)} %get-tuple-element.82.leaf_ref) | copy-start | bytes 3145732
  23.3 5.4 %copy-start.7 = (bf16[8,4,64,64]{3,2,1,0:T(8,128)(2,1)S(1)}, bf16[8,4,64,64]{3,2,1,0:T(8,128)(2,1)}, u32[]{:S(2)}) copy-start(bf16[8,4,64,64]{3,2,1,0:T(8,128)(2,1)} %node_blocks_ref.1) | copy-start | bytes 786436
  23.3 5.4 %copy-start.11 = (bf16[8,64,128]{2,1,0:T(8,128)(2,1)S(1)}, bf16[8,64,128]{2,1,0:T(8,128)(2,1)}, u32[]{:S(2)}) copy-start(bf16[8,64,128]{2,1,0:T(8,128)(2,1)} %get-tuple-element.83.node_ref) | copy-start | bytes 393220
  23.3 5.4 %copy-start.12 = (s32[64,8]{0,1:T(8,128)S(1)}, s32[64,8]{0,1:T(8,128)}, u32[]{:S(2)}) copy-start(s32[64,8]{0,1:T(8,128)} %param.24) | copy-start | bytes 6148
  23.4 5.4 %copy-start.13 = (s32[8,4]{0,1:T(4,128)S(1)}, s32[8,4]{0,1:T(4,128)}, u32[]{:S(2)}) copy-start(s32[8,4]{0,1:T(4,128)} %param.29) | copy-start | bytes 388
  23.4 5.4 %copy-start.14 = (s32[64]{0:T(128)S(1)}, s32[64]{0:T(128)}, u32[]{:S(2)}) copy-start(s32[64]{0:T(128)} %count_ref.1) | copy-start | bytes 772
  23.4 5.4 %copy-start.15 = (s32[8]{0:T(128)S(1)}, s32[8]{0:T(128)}, u32[]{:S(2)}) copy-start(s32[8]{0:T(128)} %node_count_ref.1) | copy-start | bytes 100
  25.3 7.5 %collective-permute-start.6 = (bf16[3,64,128]{2,1,0:T(8,128)(2,1)S(1)}, bf16[3,64,128]{2,1,0:T(8,128)(2,1)S(1)}, u32[]{:S(2)}, u32[]{:S(2)}) collective-permute-start(bf16[3,64,128]{2,1,0:T(8,128)(2,1)S(1)} %get-tuple-element.87), channel_id=1, source_target_pairs={{0,120},{1,121},{2,122},{3,123},{4,124},{5,125},{6,126},{7,127},{8... | collective-permute-start | bytes 147464 | tf_op jit(solution)/shard_map/ppermute | solution.py:599
  28.4 5.5 %collective-permute-start.4 = (bf16[3,64,128]{2,1,0:T(8,128)(2,1)S(1)}, bf16[3,64,128]{2,1,0:T(8,128)(2,1)S(1)}, u32[]{:S(2)}, u32[]{:S(2)}) collective-permute-start(bf16[3,64,128]{2,1,0:T(8,128)(2,1)S(1)} %level_3.1.own), channel_id=1, source_target_pairs={{0,24},{1,25},{2,26},{3,27},{4,28},{5,29},{6,30},{7,31},{8,16},{9,... | collective-permute-start | bytes 147464 | tf_op jit(solution)/shard_map/ppermute | solution.py:602
  34.1 7.0 %collective-permute-start.8 = (bf16[3,64,128]{2,1,0:T(8,128)(2,1)S(1)}, bf16[3,64,128]{2,1,0:T(8,128)(2,1)S(1)}, u32[]{:S(2)}, u32[]{:S(2)}) collective-permute-start(bf16[3,64,128]{2,1,0:T(8,128)(2,1)S(1)} %get-tuple-element.92), channel_id=1, source_target_pairs={{0,96},{1,97},{2,98},{3,99},{4,100},{5,101},{6,102},{7,103},{8,104... | collective-permute-start | bytes 147464 | tf_op jit(solution)/shard_map/ppermute | solution.py:602
  35.4 5.7 %collective-permute-start.7 = (bf16[2,64,128]{2,1,0:T(8,128)(2,1)S(1)}, bf16[2,64,128]{2,1,0:T(8,128)(2,1)S(1)}, u32[]{:S(2)}, u32[]{:S(2)}) collective-permute-start(bf16[2,64,128]{2,1,0:T(8,128)(2,1)S(1)} %get-tuple-element.91), channel_id=1, source_target_pairs={{0,32},{1,33},{2,34},{3,35},{4,36},{5,37},{6,38},{7,39},{8,40},{9,... | collective-permute-start | bytes 98312 | tf_op jit(solution)/shard_map/ppermute | solution.py:602
  35.4 5.8 %copy-start.3 = (bf16[64,64,256]{2,1,0:T(8,128)(2,1)S(1)}, bf16[64,64,256]{2,1,0:T(8,128)(2,1)}, u32[]{:S(2)}) copy-start(bf16[64,64,256]{2,1,0:T(8,128)(2,1)} %bases_ref.3) | copy-start | bytes 6291460
  35.4 5.8 %copy-start.4 = (bf16[64,64,64]{2,1,0:T(8,128)(2,1)S(1)}, bf16[64,64,64]{2,1,0:T(8,128)(2,1)}, u32[]{:S(2)}) copy-start(bf16[64,64,64]{2,1,0:T(8,128)(2,1)} %transfer_ref.1) | copy-start | bytes 1572868
  35.4 5.8 %copy-start.10 = (bf16[8,64,64]{2,1,0:T(8,128)(2,1)S(1)}, bf16[8,64,64]{2,1,0:T(8,128)(2,1)}, u32[]{:S(2)}) copy-start(bf16[8,64,64]{2,1,0:T(8,128)(2,1)} %down_node_ref.1) | copy-start | bytes 196612
  35.4 5.7 %collective-permute-start.9 = (bf16[1,64,128]{2,1,0:T(8,128)(2,1)S(1)}, bf16[1,64,128]{2,1,0:T(8,128)(2,1)S(1)}, u32[]{:S(2)}, u32[]{:S(2)}) collective-permute-start(bf16[1,64,128]{2,1,0:T(8,128)(2,1)S(1)} %get-tuple-element.93), channel_id=1, source_target_pairs={{0,64},{1,65},{2,66},{3,67},{4,68},{5,69},{6,70},{7,71},{8,72},{9,... | collective-permute-start | bytes 49160 | tf_op jit(solution)/shard_map/ppermute | solution.py:602
